TPU v7x, 32 devices: a whole 2x2x4 slice. The times are simulated.
32 devices in a mesh: col: 16 (over z, y, core), row: 2 (over x).
Axes of the slice: x: 2, y: 2, z: 4, core: 2. Of those that a mesh axis runs over, the one named last changes fastest.
Arguments:
- anc_inverse: bfloat16 [4096, 4096], P('col', 'row'), may hold values from -6 to 6
- factor_rows: bfloat16 [16, 256, 2048], P('col', None, 'row'), may hold values from -0.09375 to 0.09375
- structure: int32 [8, 12], replicated, may hold values from 0 to 15, all different within a row
- pivot_inverse: float32 [8, 256, 256], P('row'), may hold values from -6 to 6
Outputs:
- selected: bfloat16 [16, 256, 2048], P('col', None, 'row')
- diagonal_blocks: float32 [8, 256, 256], P('row')
Inputs may be any that keep to these rules, and one draw needn't show every extreme that they name: `structure`: each row names 12 different ancestors; every ancestor is named by some row.
All inputs are finite; a program needn't handle non-finite values.
Results may differ from a plain program's by a relative error of at most 0.0016.
Values may be sent and summed in bfloat16 or wider, within the bound.
No kernel may reach another device: no remote copies, remote signals or barrier semaphores. Data moves between devices by JAX's collectives and lax.ppermute only.
A program may use at most 64 MiB of HBM per device.

v0:
```python
import jax
import jax.numpy as jnp
from jax import lax
from jax.sharding import PartitionSpec as P


def per_device(anc_inverse, factor_rows, structure, pivot_inverse):
    own_blocks = factor_rows.shape[0]
    width = factor_rows.shape[1]
    local_cols = factor_rows.shape[2]
    local_sups = local_cols // width
    inv_rows = anc_inverse.shape[0]
    all_blocks = own_blocks * lax.axis_size("col")
    col_index = lax.axis_index("col")
    row_index = lax.axis_index("row")
    blocks = col_index * own_blocks + jnp.arange(own_blocks, dtype=jnp.int32)
    list_rows = lax.dynamic_slice_in_dim(structure, row_index * local_sups, local_sups, 0)
    in_struct = jnp.any(list_rows[:, :, None] == blocks[None, None, :], axis=1)
    keep_bf = in_struct.T.astype(jnp.bfloat16)[:, None, :, None]
    keep_float = in_struct.T.astype(jnp.float32)[:, None, :, None]
    masked = (factor_rows.reshape(own_blocks, width, local_sups, width) * keep_bf).reshape(
        factor_rows.shape
    )
    gathered = lax.all_gather(anc_inverse, "row", axis=1, tiled=True)
    full_inverse = gathered.reshape(inv_rows, width, all_blocks)
    product = jnp.einsum(
        "iwb,bwn->in",
        full_inverse,
        lax.all_gather(masked, "col", axis=0, tiled=True),
        preferred_element_type=jnp.float32,
    )
    selected = (-(product.reshape(own_blocks, width, local_sups, width) * keep_float)).astype(
        jnp.bfloat16
    )
    selected = selected.reshape(factor_rows.shape)
    factor_flat = masked.reshape(own_blocks * width, local_sups, width)
    selected_flat = selected.reshape(own_blocks * width, local_sups, width)
    local_terms = jnp.einsum(
        "ikp,ikq->kpq", factor_flat, selected_flat, preferred_element_type=jnp.float32
    )
    summed = lax.psum(local_terms, "col")
    return (selected, pivot_inverse - summed)


def solution(mesh):
    in_specs = (P("col", "row"), P("col", None, "row"), P(), P("row", None, None))
    out_specs = (P("col", None, "row"), P("row", None, None))
    return jax.shard_map(
        per_device, mesh=mesh, in_specs=in_specs, out_specs=out_specs, check_vma=False
    )
```

profile of v0, /device:TPU:0, one launch (start us, length us, event | category | flops | bytes accessed | tf_op | source)
XLA Modules:
  0.0 232.6 jit_solution(9564924077262833354)
XLA Ops:
  7.2 0.0 copy-start.2
  7.2 0.0 copy-start
  7.2 0.0 all-gather.5.cloned.1.call-start
  7.2 2.3 copy.16
  9.5 0.0 all-gather.5.cloned.1.call-update
  9.6 0.0 all-gather.3.cloned.1.call-start
  9.6 0.0 copy-done.2
  9.6 0.1 fusion.9
  9.8 0.1 broadcast_bitcast_fusion.1
  9.8 0.0 copy-done
  9.8 0.8 broadcast_multiply_fusion
  10.7 0.0 all-gather.3.cloned.1.call-update
  10.7 0.0 all-reduce.2.cloned.1.call-start
  10.8 0.2 copy.23
  11.0 35.0 %all-gather.5.cloned.1.call-done = bf16[256,4096]{0,1:T(8,128)(2,1)} async-done(((bf16[256,2048]{0,1:T(8,128)(2,1)}), bf16[256,4096]{0,1:T(8,128)(2,1)}) %all-gather.5.cloned.1.call-update) | async-done | bytes 2097168 | tf_op jit(solution)/shard_map/all_gather | solution.py:24
  46.0 77.7 %all-gather.3.cloned.1.call-done = bf16[16,256,1024]{2,1,0:T(8,128)(2,1)} async-done(((bf16[1,256,1024]{2,1,0:T(8,128)(2,1)}), bf16[16,256,1024]{2,1,0:T(8,128)(2,1)}) %all-gather.3.cloned.1.call-update) | async-done | bytes 8388624 | tf_op jit(solution)/shard_map/all_gather | solution.py:29
  123.7 6.6 %fusion = f32[1024,256,1]{1,0,2:T(8,128)S(1)} fusion(bf16[16,256,1024]{2,1,0:T(8,128)(2,1)} %all-gather.3.cloned.1.call-done, bf16[256,256,16]{0,2,1:T(8,128)(2,1)} %bitcast.27), kind=kOutput, calls=%fused_computation | convolution fusion | flops 2147483648 | bytes 11534336 | tf_op jit(solution)/shard_map/iwb,bwn->in/dot_general | solution.py:26
  130.2 0.3 copy.20
  130.6 1.4 fusion.4
  131.9 0.0 copy-start.1
  131.9 0.0 all-reduce.2.cloned.1.call-update
  132.0 0.1 broadcast_bitcast_fusion
  132.0 0.2 fusion.5
  132.3 1.0 copy.21
  133.3 90.4 %all-reduce.2.cloned.1.call-done = f32[4,256,256]{2,1,0:T(8,128)} async-done(((f32[4,256,256]{2,1,0:T(8,128)}), f32[4,256,256]{2,1,0:T(8,128)}) %all-reduce.2.cloned.1.call-update) | async-done | bytes 1048592 | tf_op jit(solution)/shard_map/psum | solution.py:41
  223.7 0.0 copy-done.1
  223.7 2.4 %sub.3 = f32[4,256,256]{2,1,0:T(8,128)} subtract(f32[4,256,256]{2,1,0:T(8,128)S(1)} %copy-done.1, f32[4,256,256]{2,1,0:T(8,128)} %all-reduce.2.cloned.1.call-done) | non-fusion elementwise | flops 262144 | bytes 3145728 | tf_op jit(solution)/shard_map/sub | solution.py:42
  (3 shorter events, 0.0 us)
Async XLA Ops:
  7.2 2.5 %copy-start.2 = (s32[8,12]{1,0:T(8,128)S(1)}, s32[8,12]{1,0:T(8,128)}, u32[]{:S(2)}) copy-start(s32[8,12]{1,0:T(8,128)} %param.6) | copy-start | bytes 1156
  7.2 2.7 %copy-start = (bf16[1,256,1024]{2,1,0:T(8,128)(2,1)S(1)}, bf16[1,256,1024]{2,1,0:T(8,128)(2,1)}, u32[]{:S(2)}) copy-start(bf16[1,256,1024]{2,1,0:T(8,128)(2,1)} %param.5) | copy-start | bytes 1572868
  7.2 38.8 %all-gather.5.cloned.1.call-start = ((), (), s32[]{:S(2)}) async-start(), calls=%async_computation.1 | async-start | bytes 3145728 | tf_op jit(solution)/shard_map/all_gather | solution.py:24
  9.6 114.1 %all-gather.3.cloned.1.call-start = ((), (), s32[]{:S(2)}) async-start(), calls=%async_computation | async-start | bytes 8912896 | tf_op jit(solution)/shard_map/all_gather | solution.py:29
  10.7 213.0 %all-reduce.2.cloned.1.call-start = ((), (), s32[]{:S(2)}) async-start(), calls=%async_computation.2 | async-start | bytes 2097152 | tf_op jit(solution)/shard_map/psum | solution.py:41
  131.9 91.7 %copy-start.1 = (f32[4,256,256]{2,1,0:T(8,128)S(1)}, f32[4,256,256]{2,1,0:T(8,128)}, u32[]{:S(2)}) copy-start(f32[4,256,256]{2,1,0:T(8,128)} %param.7) | copy-start | bytes 3145732
Sparse Core Ops, SparseCore 0:
  10.1 35.7 all-gather.4
  48.7 74.8 all-gather.2
  132.1 91.5 all-reduce.1
where the time goes:
time: 233 us
  waiting for transfers between devices  203 us (87%)
  between operations  13.8 us (6%)
  matrix products  7.94 us (3%)
  local copies, waits for them, and re-layouts  4.02 us (2%)
  other arithmetic  3.56 us (2%)
    psum x1, waiting for transfers between devices, per_device(): summed = lax.psum(local_terms, 'col')  90.4 us
    all_gather x1, waiting for transfers between devices, per_device(): lax.all_gather(masked, 'col', axis=0, tiled=True)  77.7 us
    all_gather x1, waiting for transfers between devices, per_device(): gathered = lax.all_gather(anc_inverse, 'row', axis=1, tiled=True)  35 us
    dot_general x1, matrix products, per_device(): jnp.einsum('iwb,bwn->in', full_inverse, lax.all_gather(masked, 'col', axi...  6.58 us
  transfers between devices with their start and end apart: 3, of which 3 were waited for; matrix products, arithmetic and copies ran while one was open for 1% of the time, Pallas kernels for 0%

commit v1 on v0

--- a/solution.py
+++ b/solution.py
@@ -1,10 +1,19 @@
+import functools
+
 import jax
 import jax.numpy as jnp
 from jax import lax
+from jax.experimental import pallas as pl
+from jax.experimental.pallas import tpu as pltpu
 from jax.sharding import PartitionSpec as P
 
-
-def per_device(anc_inverse, factor_rows, structure, pivot_inverse):
+VMEM = pl.BlockSpec(memory_space=pltpu.VMEM)
+SMEM = pl.BlockSpec(memory_space=pltpu.SMEM)
+PARAMS = pltpu.CompilerParams(vmem_limit_bytes=40 * 1024 * 1024)
+GROUP = 4
+
+
+def generic(anc_inverse, factor_rows, structure, pivot_inverse):
     own_blocks = factor_rows.shape[0]
     width = factor_rows.shape[1]
     local_cols = factor_rows.shape[2]
@@ -42,9 +51,187 @@
     return (selected, pivot_inverse - summed)
 
 
+def is_member(lists, sup, block):
+    found = lists[sup, 0] == block
+    for i in range(1, lists.shape[1]):
+        found = jnp.logical_or(found, lists[sup, i] == block)
+    return found
+
+
+def split_kernel(place, lists, rows_ref, keep_ref, give_ref):
+    col, row = place[0], place[1]
+    width = rows_ref.shape[0]
+    for j in range(GROUP):
+        sup = (col % GROUP) ^ j
+        part = rows_ref[:, pl.ds(pl.multiple_of(sup * width, width), width)]
+        part = jnp.where(is_member(lists, row * GROUP + sup, col), part, jnp.zeros_like(part))
+        (keep_ref if j % 2 == 0 else give_ref)[j // 2] = part
+
+
+def product_kernel(n_groups, first, last, place, lists, *refs):
+    m_refs, refs = refs[:10], refs[10:]
+    a_refs, refs = refs[: 4 * n_groups], refs[4 * n_groups :]
+    if last:
+        before_ref, refs = refs[0], refs[1:]
+    sel_ref, diag_ref = refs
+    col, row = place[0], place[1]
+    width = sel_ref.shape[1]
+    half = width // 2
+    near, far = pl.multiple_of(row * half, half), pl.multiple_of((1 - row) * half, half)
+
+    def level(j, at):
+        z, part = j // 4, (j // 2) % 2
+        ref = m_refs[5 * part + z]
+        block = ref[j % 2, pl.ds(at, half), :]
+        if z == 3:
+            block = block + m_refs[5 * part + 4][j % 2, pl.ds(at, half), :]
+        return block
+
+    sup = row * GROUP + col % GROUP
+    diag = before_ref[...] if last else None
+    totals = [None] * n_groups
+    n_half = a_refs[0].shape[0]
+    for j in range(16):
+        m = jnp.concatenate([level(j, near), level(j, far)], axis=0)
+        block = col ^ j
+        in_low = block < n_half
+        at = block % n_half
+        for g in range(n_groups):
+            low_near, high_near, low_far, high_far = a_refs[4 * g : 4 * g + 4]
+            a_near = jnp.where(in_low, low_near[at], high_near[at])
+            a_far = jnp.where(in_low, low_far[at], high_far[at])
+            a = jnp.concatenate([a_near, a_far], axis=1)
+            term = jnp.dot(a, m, preferred_element_type=jnp.float32)
+            totals[g] = term if totals[g] is None else totals[g] + term
+    for g in range(n_groups):
+        kept = is_member(lists, sup, col ^ (first + g))
+        sel = jnp.where(kept, -totals[g], jnp.zeros_like(totals[g])).astype(jnp.bfloat16)
+        sel_ref[g] = sel
+        left = m_refs[5 * ((first + g) // 2)][(first + g) % 2]
+        term = lax.dot_general(
+            left, sel, (((0,), (0,)), ((), ())), preferred_element_type=jnp.float32
+        )
+        diag = term if diag is None else diag + term
+    diag_ref[...] = diag
+
+
+def merge_kernel(place, own_ref, core_ref, pair_ref, cross_ref, out_ref):
+    col = place[0]
+    width = own_ref.shape[0]
+    for j, ref in enumerate((own_ref, core_ref, pair_ref, cross_ref)):
+        sup = (col % GROUP) ^ j
+        out_ref[:, pl.ds(pl.multiple_of(sup * width, width), width)] = ref[...]
+
+
+def finish_kernel(place, own_ref, other_ref, pivot_ref, out_ref):
+    col = place[0]
+    for j in range(GROUP):
+        sup = (col % GROUP) ^ j
+        ref = own_ref if j % 2 == 0 else other_ref
+        out_ref[sup] = pivot_ref[sup] - ref[j // 2]
+
+
+def per_device(anc_inverse, factor_rows, structure, pivot_inverse):
+    width = factor_rows.shape[1]
+    n_col = lax.axis_size("col")
+    all_blocks = factor_rows.shape[0] * n_col
+    bf16, f32 = jnp.bfloat16, jnp.float32
+    col = lax.axis_index("col")
+    row = lax.axis_index("row")
+    place = jnp.stack([col, row]).astype(jnp.int32)
+    rows = anc_inverse.shape[0]
+    half_w = anc_inverse.shape[1] // all_blocks
+
+    def swap(x, flip):
+        return lax.ppermute(x, "col", [(c, c ^ flip) for c in range(n_col)])
+
+    def middle(x):
+        return lax.ppermute(x, "col", [(c, c ^ 12) for c in range(n_col) if c // 4 in (1, 2)])
+
+    def outward(x):
+        return lax.ppermute(x, "col", [(c, c ^ 4) for c in range(n_col) if c // 4 in (1, 2)])
+
+    def across(x):
+        return lax.ppermute(x, "row", [(0, 1), (1, 0)])
+
+    cut = jax.ShapeDtypeStruct((2, width, width), bf16)
+    keep, give = pl.pallas_call(
+        split_kernel,
+        out_shape=(cut, cut),
+        in_specs=[SMEM, SMEM, VMEM],
+        out_specs=(VMEM, VMEM),
+        compiler_params=PARAMS,
+    )(place, structure, factor_rows.reshape(width, -1))
+    got = swap(give, 1)
+    part_a = jnp.stack([keep[0], got[0]])
+    part_b = swap(jnp.stack([keep[1], got[1]]), 2)
+    level = []
+    for part in (part_a, part_b):
+        two = swap(part, 8)
+        one = swap(part, 4)
+        level += [part, one, two, middle(part), outward(two)]
+
+    inverse = anc_inverse.reshape(rows, half_w, all_blocks).transpose(2, 0, 1)
+    low, high = inverse[: all_blocks // 2], inverse[all_blocks // 2 :]
+    x_low, x_high = across(low), across(high)
+    y_high, y_low = swap(high, 2), swap(low, 2)
+    xy_low, xy_high = swap(x_low, 2), across(y_high)
+    near = [low, high, x_low, x_high]
+    far = [y_low, y_high, xy_low, xy_high]
+    near += [swap(v, 1) for v in near]
+    far += [swap(v, 1) for v in far]
+
+    sel_shape = jax.ShapeDtypeStruct((2, width, width), bf16)
+    diag_shape = jax.ShapeDtypeStruct((width, width), f32)
+
+    def product(first, last, groups, *extra):
+        return pl.pallas_call(
+            functools.partial(product_kernel, 2, first, last),
+            out_shape=(sel_shape, diag_shape),
+            in_specs=[SMEM, SMEM] + [VMEM] * (18 + len(extra)),
+            out_specs=(VMEM, VMEM),
+            compiler_params=PARAMS,
+        )(place, structure, *level, *groups, *extra)
+
+    sel_near, diag = product(0, False, near)
+    sel_far, diag = product(2, True, far, diag)
+
+    diag = diag + swap(diag, 4)
+    diag = diag + swap(diag, 8)
+    pair = jnp.stack([diag, swap(diag, 2)])
+    other = swap(pair, 1)
+    diagonal = pl.pallas_call(
+        finish_kernel,
+        out_shape=jax.ShapeDtypeStruct(pivot_inverse.shape, f32),
+        in_specs=[SMEM, VMEM, VMEM, VMEM],
+        out_specs=VMEM,
+        compiler_params=PARAMS,
+    )(place, pair, other, pivot_inverse)
+
+    selected = pl.pallas_call(
+        merge_kernel,
+        out_shape=jax.ShapeDtypeStruct((width, GROUP * width), bf16),
+        in_specs=[SMEM, VMEM, VMEM, VMEM, VMEM],
+        out_specs=VMEM,
+        compiler_params=PARAMS,
+    )(place, sel_near[0], swap(sel_near[1], 1), swap(sel_far[0], 2), swap(sel_far[1], 3))
+    return selected.reshape(factor_rows.shape), diagonal
+
+
 def solution(mesh):
     in_specs = (P("col", "row"), P("col", None, "row"), P(), P("row", None, None))
     out_specs = (P("col", None, "row"), P("row", None, None))
-    return jax.shard_map(
-        per_device, mesh=mesh, in_specs=in_specs, out_specs=out_specs, check_vma=False
-    )
+
+    def run(anc_inverse, factor_rows, structure, pivot_inverse):
+        n_col, n_row = mesh.shape["col"], mesh.shape["row"]
+        blocks, width, columns = factor_rows.shape
+        fits = n_col == 16 and n_row == 2 and blocks == n_col and columns == n_row * GROUP * width
+        return jax.shard_map(
+            per_device if fits else generic,
+            mesh=mesh,
+            in_specs=in_specs,
+            out_specs=out_specs,
+            check_vma=False,
+        )(anc_inverse, factor_rows, structure, pivot_inverse)
+
+    return run

time: 233 us -> 117 us (0.50)
  waiting for transfers between devices: 203 us -> 74.3 us
  starting transfers between devices: 0.12 us -> 28.7 us
  between operations: 13.8 us -> 0.88 us
  Pallas kernels: 0 us -> 8.08 us
  matrix products: 7.94 us -> 0 us
  other arithmetic: 3.56 us -> 0.23 us
    all_gather x2 -> x0, waiting for transfers between devices: 113 us -> none  [the longest x1 77.7 us: per_device(): lax.all_gather(masked, 'col', axis=0, tiled=True)]
    psum x1 -> x0, waiting for transfers between devices: 90.4 us -> none  [per_device(): summed = lax.psum(local_terms, 'col')]
    ppermute x0 -> x31, waiting for transfers between devices: none -> 74.3 us  [the longest x24 55.7 us: swap(): return lax.ppermute(x, 'col', [(c, c ^ flip) for c in range(n_col)])]
    ppermute x0 -> x31, starting transfers between devices: none -> 28.7 us  [the longest x24 21.3 us: swap(): return lax.ppermute(x, 'col', [(c, c ^ flip) for c in range(n_col)])]
    pallas_call x0 -> x5, Pallas kernels: none -> 8.08 us  [the longest x2 4.33 us: product(): pl.pallas_call(functools.partial(product_kernel, 2, first, last), out_sha...]
    dot_general x2 -> x0, matrix products: 7.94 us -> none  [the longest x1 6.58 us: per_device(): jnp.einsum('iwb,bwn->in', full_inverse, lax.all_gather(masked, 'col', axi...]
    sub x1 -> x0, other arithmetic: 2.39 us -> none  [per_device(): return (selected, pivot_inverse - summed)]
  transfers between devices with their start and end apart: 3 -> 31, of which waited for: 3 -> 13; matrix products, arithmetic and copies ran while one was open for 1% -> 2% of each run, Pallas kernels for 0% -> 3%
where the time goes in v1:
time: 117 us; the launch traced here: 116 us
  waiting for transfers between devices  74.3 us (64%)
  starting transfers between devices  28.7 us (25%)
  Pallas kernels  8.08 us (7%)
  local copies, waits for them, and re-layouts  4.26 us (4%)
    ppermute x24, waiting for transfers between devices, swap(): return lax.ppermute(x, 'col', [(c, c ^ flip) for c in range(n_col)])  55.7 us
    ppermute x24, starting transfers between devices, swap(): return lax.ppermute(x, 'col', [(c, c ^ flip) for c in range(n_col)])  21.3 us
    ppermute x2, waiting for transfers between devices, outward(): lax.ppermute(x, 'col', [(c, c ^ 4) for c in range(n_col) if c // 4 in (1,...  11.6 us
    ppermute x3, waiting for transfers between devices, across(): return lax.ppermute(x, 'row', [(0, 1), (1, 0)])  6.89 us
    pallas_call x2, Pallas kernels, product(): pl.pallas_call(functools.partial(product_kernel, 2, first, last), out_sha...  4.33 us
    ppermute x3, starting transfers between devices, across(): return lax.ppermute(x, 'row', [(0, 1), (1, 0)])  3.48 us
    unnamed x7, local copies, waits for them, and re-layouts  3.13 us
    ppermute x2, starting transfers between devices, outward(): lax.ppermute(x, 'col', [(c, c ^ 4) for c in range(n_col) if c // 4 in (1,...  2.57 us
  transfers between devices with their start and end apart: 31, of which 13 were waited for; matrix products, arithmetic and copies ran while one was open for 2% of the time, Pallas kernels for 3%

profile of v1, /device:TPU:0, one launch (start us, length us, event | category | flops | bytes accessed | tf_op | source)
XLA Modules:
  0.0 116.4 jit_solution(3796974401675970489)
XLA Ops:
  0.6 0.1 pad_add_fusion.place
  0.7 0.6 copy-done.2
  1.3 1.0 copy-done.1
  2.4 0.7 shard_map.59
  3.1 0.5 collective-permute-start
  3.6 1.5 %copy.6 = bf16[256,2048]{0,1:T(8,128)(2,1)S(1)} copy(bf16[256,2048]{1,0:T(8,128)(2,1)} %param.4) | data formatting | bytes 2097152 | tf_op args[0]
  5.1 1.0 copy.7
  6.1 0.1 fusion
  6.2 2.6 %collective-permute-start.10 = (bf16[8,256,128]{2,1,0:T(8,128)(2,1)S(1)}, bf16[8,256,128]{2,1,0:T(8,128)(2,1)S(1)}, u32[]{:S(2)}, u32[]{:S(2)}) collective-permute-start(bf16[8,256,128]{2,1,0:T(8,128)(2,1)S(1)} %get-tuple-element.15.refs_10_), channel_id=1, source_target_pairs={{0,1},{1,0},{2,3},{3,2},{4,5},{5,4},{6,7},{7,6},{8,9},{9,8},{10,11... | collective-permute-start | bytes 1572872 | tf_op jit(solution)/shard_map/ppermute | solution.py:155
  8.8 1.6 %collective-permute-start.1 = (bf16[2,256,256]{2,1,0:T(8,128)(2,1)S(1)}, bf16[2,256,256]{2,1,0:T(8,128)(2,1)S(1)}, u32[]{:S(2)}, u32[]{:S(2)}) collective-permute-start(bf16[2,256,256]{2,1,0:T(8,128)(2,1)S(1)} %pad_maximum_fusion.1.refs_0_), channel_id=1, source_target_pairs={{0,8},{2,10},{4,12},{6,14},{8,0},{10,2},{12,4},{14,6},{16,24},{18,... | collective-permute-start | bytes 786440 | tf_op jit(solution)/shard_map/ppermute | solution.py:146
  10.5 2.6 %collective-permute-start.2 = (bf16[2,256,256]{2,1,0:T(8,128)(2,1)S(1)}, bf16[2,256,256]{2,1,0:T(8,128)(2,1)S(1)}, u32[]{:S(2)}, u32[]{:S(2)}) collective-permute-start(bf16[2,256,256]{2,1,0:T(8,128)(2,1)S(1)} %pad_maximum_fusion.1.refs_0_), channel_id=1, source_target_pairs={{0,16},{2,18},{4,20},{6,22},{8,24},{10,26},{12,28},{14,30},{16,0},... | collective-permute-start | bytes 786440 | tf_op jit(solution)/shard_map/ppermute | solution.py:146
  13.1 0.7 collective-permute-start.3
  13.8 1.6 %collective-permute-start.5 = (bf16[2,256,256]{2,1,0:T(8,128)(2,1)S(1)}, bf16[2,256,256]{2,1,0:T(8,128)(2,1)S(1)}, u32[]{:S(2)}, u32[]{:S(2)}) collective-permute-start(bf16[2,256,256]{2,1,0:T(8,128)(2,1)S(1)} %pad_maximum_fusion.2), channel_id=1, source_target_pairs={{0,4},{2,6},{4,0},{6,2},{8,12},{10,14},{12,8},{14,10},{16,20},{18,... | collective-permute-start | bytes 786440 | tf_op jit(solution)/shard_map/ppermute | solution.py:146
  15.4 7.0 %collective-permute-done.1.refs_1_ = bf16[2,256,256]{2,1,0:T(8,128)(2,1)S(1)} collective-permute-done((bf16[2,256,256]{2,1,0:T(8,128)(2,1)S(1)}, bf16[2,256,256]{2,1,0:T(8,128)(2,1)S(1)}, u32[]{:S(2)}, u32[]{:S(2)}) %collective-permute-start.1) | collective-permute-done | bytes 262176 | tf_op jit(solution)/shard_map/ppermute | solution.py:146
  22.4 0.4 collective-permute-start.11
  22.8 3.4 %collective-permute-done.2.refs_2_ = bf16[2,256,256]{2,1,0:T(8,128)(2,1)S(1)} collective-permute-done((bf16[2,256,256]{2,1,0:T(8,128)(2,1)S(1)}, bf16[2,256,256]{2,1,0:T(8,128)(2,1)S(1)}, u32[]{:S(2)}, u32[]{:S(2)}) %collective-permute-start.2) | collective-permute-done | bytes 262176 | tf_op jit(solution)/shard_map/ppermute | solution.py:146
  26.2 0.5 collective-permute-start.13
  26.7 0.0 collective-permute-done.5.refs_5_
  26.7 1.5 %collective-permute-start.17 = (bf16[8,256,128]{2,1,0:T(8,128)(2,1)S(1)}, bf16[8,256,128]{2,1,0:T(8,128)(2,1)S(1)}, u32[]{:S(2)}, u32[]{:S(2)}) collective-permute-start(bf16[8,256,128]{2,1,0:T(8,128)(2,1)S(1)} %get-tuple-element.15.refs_10_), channel_id=1, source_target_pairs={{0,4},{2,6},{4,0},{6,2},{8,12},{10,14},{12,8},{14,10},{16,20},{18,... | collective-permute-start | bytes 1572872 | tf_op jit(solution)/shard_map/ppermute | solution.py:146
  28.2 0.5 collective-permute-start.18
  28.7 6.9 %collective-permute-done.11.refs_13_ = bf16[8,256,128]{2,1,0:T(8,128)(2,1)S(1)} collective-permute-done((bf16[8,256,128]{2,1,0:T(8,128)(2,1)S(1)}, bf16[8,256,128]{2,1,0:T(8,128)(2,1)S(1)}, u32[]{:S(2)}, u32[]{:S(2)}) %collective-permute-start.11) | collective-permute-done | bytes 524320 | tf_op jit(solution)/shard_map/ppermute | solution.py:155
  35.6 1.3 %collective-permute-start.4 = (bf16[2,256,256]{2,1,0:T(8,128)(2,1)S(1)}, bf16[2,256,256]{2,1,0:T(8,128)(2,1)S(1)}, u32[]{:S(2)}, u32[]{:S(2)}) collective-permute-start(bf16[2,256,256]{2,1,0:T(8,128)(2,1)S(1)} %collective-permute-done.2.refs_2_), channel_id=1, source_target_pairs={{8,0},{10,2},{12,4},{14,6},{16,24},{18,26},{20,28},{22,30},{9,1},{... | collective-permute-start | bytes 786440 | tf_op jit(solution)/shard_map/ppermute | solution.py:152
  36.9 0.0 collective-permute-done.12.refs_14_
  36.9 2.7 %collective-permute-start.6 = (bf16[2,256,256]{2,1,0:T(8,128)(2,1)S(1)}, bf16[2,256,256]{2,1,0:T(8,128)(2,1)S(1)}, u32[]{:S(2)}, u32[]{:S(2)}) collective-permute-start(bf16[2,256,256]{2,1,0:T(8,128)(2,1)S(1)} %collective-permute-done.5.refs_5_), channel_id=1, source_target_pairs={{0,8},{2,10},{4,12},{6,14},{8,0},{10,2},{12,4},{14,6},{16,24},{18,... | collective-permute-start | bytes 786440 | tf_op jit(solution)/shard_map/ppermute | solution.py:146
  39.6 0.0 collective-permute-done.13.refs_15_
  39.6 1.5 %collective-permute-start.7 = (bf16[2,256,256]{2,1,0:T(8,128)(2,1)S(1)}, bf16[2,256,256]{2,1,0:T(8,128)(2,1)S(1)}, u32[]{:S(2)}, u32[]{:S(2)}) collective-permute-start(bf16[2,256,256]{2,1,0:T(8,128)(2,1)S(1)} %collective-permute-done.5.refs_5_), channel_id=1, source_target_pairs={{0,16},{2,18},{4,20},{6,22},{8,24},{10,26},{12,28},{14,30},{16,0},... | collective-permute-start | bytes 786440 | tf_op jit(solution)/shard_map/ppermute | solution.py:146
  41.2 0.3 collective-permute-done.17.refs_10_
  41.5 0.0 collective-permute-start.14
  41.5 10.3 %collective-permute-done.18.refs_11_ = bf16[8,256,128]{2,1,0:T(8,128)(2,1)S(1)} collective-permute-done((bf16[8,256,128]{2,1,0:T(8,128)(2,1)S(1)}, bf16[8,256,128]{2,1,0:T(8,128)(2,1)S(1)}, u32[]{:S(2)}, u32[]{:S(2)}) %collective-permute-start.18) | collective-permute-done | bytes 524320 | tf_op jit(solution)/shard_map/ppermute | solution.py:146
  51.8 1.5 %collective-permute-start.19 = (bf16[8,256,128]{2,1,0:T(8,128)(2,1)S(1)}, bf16[8,256,128]{2,1,0:T(8,128)(2,1)S(1)}, u32[]{:S(2)}, u32[]{:S(2)}) collective-permute-start(bf16[8,256,128]{2,1,0:T(8,128)(2,1)S(1)} %collective-permute-done.10.refs_12_), channel_id=1, source_target_pairs={{0,4},{2,6},{4,0},{6,2},{8,12},{10,14},{12,8},{14,10},{16,20},{18,... | collective-permute-start | bytes 1572872 | tf_op jit(solution)/shard_map/ppermute | solution.py:146
  53.4 0.0 collective-permute-done.4.refs_4_
  53.4 0.5 collective-permute-start.20
  53.9 1.5 %collective-permute-done.6.refs_6_ = bf16[2,256,256]{2,1,0:T(8,128)(2,1)S(1)} collective-permute-done((bf16[2,256,256]{2,1,0:T(8,128)(2,1)S(1)}, bf16[2,256,256]{2,1,0:T(8,128)(2,1)S(1)}, u32[]{:S(2)}, u32[]{:S(2)}) %collective-permute-start.6) | collective-permute-done | bytes 262176 | tf_op jit(solution)/shard_map/ppermute | solution.py:146
  55.4 0.7 collective-permute-start.8
  56.1 0.0 collective-permute-done.7.refs_7_
  56.1 1.3 %collective-permute-start.9 = (bf16[2,256,256]{2,1,0:T(8,128)(2,1)S(1)}, bf16[2,256,256]{2,1,0:T(8,128)(2,1)S(1)}, u32[]{:S(2)}, u32[]{:S(2)}) collective-permute-start(bf16[2,256,256]{2,1,0:T(8,128)(2,1)S(1)} %collective-permute-done.7.refs_7_), channel_id=1, source_target_pairs={{8,0},{10,2},{12,4},{14,6},{16,24},{18,26},{20,28},{22,30},{9,1},{... | collective-permute-start | bytes 786440 | tf_op jit(solution)/shard_map/ppermute | solution.py:152
  57.4 0.1 collective-permute-start.22
  57.5 11.6 %collective-permute-done.9.refs_9_ = bf16[2,256,256]{2,1,0:T(8,128)(2,1)S(1)} collective-permute-done((bf16[2,256,256]{2,1,0:T(8,128)(2,1)S(1)}, bf16[2,256,256]{2,1,0:T(8,128)(2,1)S(1)}, u32[]{:S(2)}, u32[]{:S(2)}) %collective-permute-start.9) | collective-permute-done | bytes 262176 | tf_op jit(solution)/shard_map/ppermute | solution.py:152
  69.1 0.0 collective-permute-start.15
  69.1 0.5 collective-permute-start.21
  69.6 0.1 collective-permute-start.23
  69.7 0.0 collective-permute-done.20.refs_13_
  69.7 0.4 collective-permute-start.24
  70.2 0.9 collective-permute-done.15.refs_17_
  71.0 2.2 %shard_map.60 = (bf16[2,256,256]{2,1,0:T(8,128)(2,1)S(1)}, f32[256,256]{1,0:T(8,128)S(1)}) custom-call(s32[2]{0:T(128)S(1)} %pad_add_fusion.place, s32[8,12]{1,0:T(8,128)S(1)} %copy-done.2, bf16[2,256,256]{2,1,0:T(8,128)(2,1)S(1)} %pad_maximum_fusion.1.refs_0_, bf16[2,256,256]{2,1,0:T(8,128)(2,1)S(1)} %collective-permute-done.1.refs_1_, ...), custom_call_target="tpu_custom_call" | custom-call | tf_op jit(solution)/shard_map/pallas_call | solution.py:188
  73.2 0.0 collective-permute-done.22.refs_15_
  73.3 0.0 collective-permute-done.24.refs_17_
  73.3 2.1 %shard_map.61 = (bf16[2,256,256]{2,1,0:T(8,128)(2,1)S(1)}, f32[256,256]{1,0:T(8,128)S(1)}) custom-call(s32[2]{0:T(128)S(1)} %pad_add_fusion.place, s32[8,12]{1,0:T(8,128)S(1)} %copy-done.2, bf16[2,256,256]{2,1,0:T(8,128)(2,1)S(1)} %pad_maximum_fusion.1.refs_0_, bf16[2,256,256]{2,1,0:T(8,128)(2,1)S(1)} %collective-permute-done.1.refs_1_, ...), custom_call_target="tpu_custom_call" | custom-call | tf_op jit(solution)/shard_map/pallas_call | solution.py:188
  75.4 0.8 collective-permute-start.27
  76.2 7.6 %collective-permute-done.27 = f32[256,256]{1,0:T(8,128)S(1)} collective-permute-done((f32[256,256]{1,0:T(8,128)S(1)}, f32[256,256]{1,0:T(8,128)S(1)}, u32[]{:S(2)}, u32[]{:S(2)}) %collective-permute-start.27) | collective-permute-done | bytes 262176 | tf_op jit(solution)/shard_map/ppermute | solution.py:146
  83.9 2.2 %collective-permute-start.28 = (f32[256,256]{1,0:T(8,128)S(1)}, f32[256,256]{1,0:T(8,128)S(1)}, u32[]{:S(2)}, u32[]{:S(2)}) collective-permute-start(f32[256,256]{1,0:T(8,128)S(1)} %add.6), channel_id=1, source_target_pairs={{0,16},{2,18},{4,20},{6,22},{8,24},{10,26},{12,28},{14,30},{16,0},... | collective-permute-start | bytes 786440 | tf_op jit(solution)/shard_map/ppermute | solution.py:146
  86.0 11.9 %collective-permute-done.28 = f32[256,256]{1,0:T(8,128)S(1)} collective-permute-done((f32[256,256]{1,0:T(8,128)S(1)}, f32[256,256]{1,0:T(8,128)S(1)}, u32[]{:S(2)}, u32[]{:S(2)}) %collective-permute-start.28) | collective-permute-done | bytes 262176 | tf_op jit(solution)/shard_map/ppermute | solution.py:146
  98.0 0.6 collective-permute-start.29
  98.6 6.7 %collective-permute-done.29 = f32[256,256]{1,0:T(8,128)S(1)} collective-permute-done((f32[256,256]{1,0:T(8,128)S(1)}, f32[256,256]{1,0:T(8,128)S(1)}, u32[]{:S(2)}, u32[]{:S(2)}) %collective-permute-start.29) | collective-permute-done | bytes 262176 | tf_op jit(solution)/shard_map/ppermute | solution.py:146
  105.3 0.1 collective-permute-start.30
  105.4 0.0 copy-start
  105.5 0.5 collective-permute-start.16
  106.0 0.9 collective-permute-start.25
  106.9 0.5 collective-permute-start.26
  107.5 0.0 collective-permute-done.16.core_ref
  107.5 4.9 %collective-permute-done.25.pair_ref = bf16[256,256]{1,0:T(8,128)(2,1)S(1)} collective-permute-done((bf16[256,256]{1,0:T(8,128)(2,1)S(1)}, bf16[256,256]{1,0:T(8,128)(2,1)S(1)}, u32[]{:S(2)}, u32[]{:S(2)}) %collective-permute-start.25) | collective-permute-done | bytes 131104 | tf_op jit(solution)/shard_map/ppermute | solution.py:146
  112.4 0.9 collective-permute-done.26.cross_ref
  113.4 1.4 %shard_map.62 = bf16[256,1024]{1,0:T(8,128)(2,1)} custom-call(s32[2]{0:T(128)S(1)} %pad_add_fusion.place, bf16[256,256]{1,0:T(8,128)(2,1)S(1)} %get-tuple-element.19.own_ref, bf16[256,256]{1,0:T(8,128)(2,1)S(1)} %collective-permute-done.16.core_ref, bf16[256,256]{1,0:T(8,128)(2,1)S(1)} %collective-permute-done.25.pair_ref, ...), custom_call_target="tpu_custom_call" | custom-call | tf_op jit(solution)/shard_map/pallas_call | solution.py:211
  114.8 1.6 %shard_map.63 = f32[4,256,256]{2,1,0:T(8,128)} custom-call(s32[2]{0:T(128)S(1)} %pad_add_fusion.place, f32[2,256,256]{2,1,0:T(8,128)S(1)} %pad_maximum_fusion.own_ref, f32[2,256,256]{2,1,0:T(8,128)S(1)} %collective-permute-done.30.other_ref, f32[4,256,256]{2,1,0:T(8,128)S(1)} %copy-done), custom_call_target="tpu_custom_call" | custom-call | tf_op jit(solution)/shard_map/pallas_call | solution.py:203
  (22 shorter events, 0.3 us)
Async XLA Ops:
  0.6 0.7 copy-start.2
  1.3 1.0 copy-start.1
  3.1 5.7 %collective-permute-start = (bf16[2,256,256]{2,1,0:T(8,128)(2,1)S(1)}, bf16[2,256,256]{2,1,0:T(8,128)(2,1)S(1)}, u32[]{:S(2)}, u32[]{:S(2)}) collective-permute-start(bf16[2,256,256]{2,1,0:T(8,128)(2,1)S(1)} %get-tuple-element.9), channel_id=1, source_target_pairs={{0,2},{2,0},{4,6},{6,4},{8,10},{10,8},{12,14},{14,12},{16,18},{18,... | collective-permute-start | bytes 786440 | tf_op jit(solution)/shard_map/ppermute | solution.py:146
  6.2 22.0 %collective-permute-start.10 = (bf16[8,256,128]{2,1,0:T(8,128)(2,1)S(1)}, bf16[8,256,128]{2,1,0:T(8,128)(2,1)S(1)}, u32[]{:S(2)}, u32[]{:S(2)}) collective-permute-start(bf16[8,256,128]{2,1,0:T(8,128)(2,1)S(1)} %get-tuple-element.15.refs_10_), channel_id=1, source_target_pairs={{0,1},{1,0},{2,3},{3,2},{4,5},{5,4},{6,7},{7,6},{8,9},{9,8},{10,11... | collective-permute-start | bytes 1572872 | tf_op jit(solution)/shard_map/ppermute | solution.py:155
  8.8 13.6 %collective-permute-start.1 = (bf16[2,256,256]{2,1,0:T(8,128)(2,1)S(1)}, bf16[2,256,256]{2,1,0:T(8,128)(2,1)S(1)}, u32[]{:S(2)}, u32[]{:S(2)}) collective-permute-start(bf16[2,256,256]{2,1,0:T(8,128)(2,1)S(1)} %pad_maximum_fusion.1.refs_0_), channel_id=1, source_target_pairs={{0,8},{2,10},{4,12},{6,14},{8,0},{10,2},{12,4},{14,6},{16,24},{18,... | collective-permute-start | bytes 786440 | tf_op jit(solution)/shard_map/ppermute | solution.py:146
  10.5 15.7 %collective-permute-start.2 = (bf16[2,256,256]{2,1,0:T(8,128)(2,1)S(1)}, bf16[2,256,256]{2,1,0:T(8,128)(2,1)S(1)}, u32[]{:S(2)}, u32[]{:S(2)}) collective-permute-start(bf16[2,256,256]{2,1,0:T(8,128)(2,1)S(1)} %pad_maximum_fusion.1.refs_0_), channel_id=1, source_target_pairs={{0,16},{2,18},{4,20},{6,22},{8,24},{10,26},{12,28},{14,30},{16,0},... | collective-permute-start | bytes 786440 | tf_op jit(solution)/shard_map/ppermute | solution.py:146
  13.1 13.1 %collective-permute-start.3 = (bf16[2,256,256]{2,1,0:T(8,128)(2,1)S(1)}, bf16[2,256,256]{2,1,0:T(8,128)(2,1)S(1)}, u32[]{:S(2)}, u32[]{:S(2)}) collective-permute-start(bf16[2,256,256]{2,1,0:T(8,128)(2,1)S(1)} %pad_maximum_fusion.1.refs_0_), channel_id=1, source_target_pairs={{8,16},{10,18},{12,20},{14,22},{16,8},{18,10},{20,12},{22,14},{9,1... | collective-permute-start | bytes 786440 | tf_op jit(solution)/shard_map/ppermute | solution.py:149
  13.8 12.9 %collective-permute-start.5 = (bf16[2,256,256]{2,1,0:T(8,128)(2,1)S(1)}, bf16[2,256,256]{2,1,0:T(8,128)(2,1)S(1)}, u32[]{:S(2)}, u32[]{:S(2)}) collective-permute-start(bf16[2,256,256]{2,1,0:T(8,128)(2,1)S(1)} %pad_maximum_fusion.2), channel_id=1, source_target_pairs={{0,4},{2,6},{4,0},{6,2},{8,12},{10,14},{12,8},{14,10},{16,20},{18,... | collective-permute-start | bytes 786440 | tf_op jit(solution)/shard_map/ppermute | solution.py:146
  22.4 13.2 %collective-permute-start.11 = (bf16[8,256,128]{2,1,0:T(8,128)(2,1)S(1)}, bf16[8,256,128]{2,1,0:T(8,128)(2,1)S(1)}, u32[]{:S(2)}, u32[]{:S(2)}) collective-permute-start(bf16[8,256,128]{2,1,0:T(8,128)(2,1)S(1)} %get-tuple-element.14.refs_11_), channel_id=1, source_target_pairs={{0,1},{1,0},{2,3},{3,2},{4,5},{5,4},{6,7},{7,6},{8,9},{9,8},{10,11... | collective-permute-start | bytes 1572872 | tf_op jit(solution)/shard_map/ppermute | solution.py:155
  26.2 10.7 %collective-permute-start.12 = (bf16[8,256,128]{2,1,0:T(8,128)(2,1)S(1)}, bf16[8,256,128]{2,1,0:T(8,128)(2,1)S(1)}, u32[]{:S(2)}, u32[]{:S(2)}) collective-permute-start(bf16[8,256,128]{2,1,0:T(8,128)(2,1)S(1)} %get-tuple-element.15.refs_10_), channel_id=1, source_target_pairs={{0,2},{2,0},{4,6},{6,4},{8,10},{10,8},{12,14},{14,12},{16,18},{18,... | collective-permute-start | bytes 1572872 | tf_op jit(solution)/shard_map/ppermute | solution.py:146
  26.2 13.4 %collective-permute-start.13 = (bf16[8,256,128]{2,1,0:T(8,128)(2,1)S(1)}, bf16[8,256,128]{2,1,0:T(8,128)(2,1)S(1)}, u32[]{:S(2)}, u32[]{:S(2)}) collective-permute-start(bf16[8,256,128]{2,1,0:T(8,128)(2,1)S(1)} %get-tuple-element.14.refs_11_), channel_id=1, source_target_pairs={{0,2},{2,0},{4,6},{6,4},{8,10},{10,8},{12,14},{14,12},{16,18},{18,... | collective-permute-start | bytes 1572872 | tf_op jit(solution)/shard_map/ppermute | solution.py:146
  26.7 14.8 %collective-permute-start.17 = (bf16[8,256,128]{2,1,0:T(8,128)(2,1)S(1)}, bf16[8,256,128]{2,1,0:T(8,128)(2,1)S(1)}, u32[]{:S(2)}, u32[]{:S(2)}) collective-permute-start(bf16[8,256,128]{2,1,0:T(8,128)(2,1)S(1)} %get-tuple-element.15.refs_10_), channel_id=1, source_target_pairs={{0,4},{2,6},{4,0},{6,2},{8,12},{10,14},{12,8},{14,10},{16,20},{18,... | collective-permute-start | bytes 1572872 | tf_op jit(solution)/shard_map/ppermute | solution.py:146
  28.2 23.6 %collective-permute-start.18 = (bf16[8,256,128]{2,1,0:T(8,128)(2,1)S(1)}, bf16[8,256,128]{2,1,0:T(8,128)(2,1)S(1)}, u32[]{:S(2)}, u32[]{:S(2)}) collective-permute-start(bf16[8,256,128]{2,1,0:T(8,128)(2,1)S(1)} %get-tuple-element.14.refs_11_), channel_id=1, source_target_pairs={{0,4},{2,6},{4,0},{6,2},{8,12},{10,14},{12,8},{14,10},{16,20},{18,... | collective-permute-start | bytes 1572872 | tf_op jit(solution)/shard_map/ppermute | solution.py:146
  35.6 17.7 %collective-permute-start.4 = (bf16[2,256,256]{2,1,0:T(8,128)(2,1)S(1)}, bf16[2,256,256]{2,1,0:T(8,128)(2,1)S(1)}, u32[]{:S(2)}, u32[]{:S(2)}) collective-permute-start(bf16[2,256,256]{2,1,0:T(8,128)(2,1)S(1)} %collective-permute-done.2.refs_2_), channel_id=1, source_target_pairs={{8,0},{10,2},{12,4},{14,6},{16,24},{18,26},{20,28},{22,30},{9,1},{... | collective-permute-start | bytes 786440 | tf_op jit(solution)/shard_map/ppermute | solution.py:152
  36.9 18.5 %collective-permute-start.6 = (bf16[2,256,256]{2,1,0:T(8,128)(2,1)S(1)}, bf16[2,256,256]{2,1,0:T(8,128)(2,1)S(1)}, u32[]{:S(2)}, u32[]{:S(2)}) collective-permute-start(bf16[2,256,256]{2,1,0:T(8,128)(2,1)S(1)} %collective-permute-done.5.refs_5_), channel_id=1, source_target_pairs={{0,8},{2,10},{4,12},{6,14},{8,0},{10,2},{12,4},{14,6},{16,24},{18,... | collective-permute-start | bytes 786440 | tf_op jit(solution)/shard_map/ppermute | solution.py:146
  39.6 16.5 %collective-permute-start.7 = (bf16[2,256,256]{2,1,0:T(8,128)(2,1)S(1)}, bf16[2,256,256]{2,1,0:T(8,128)(2,1)S(1)}, u32[]{:S(2)}, u32[]{:S(2)}) collective-permute-start(bf16[2,256,256]{2,1,0:T(8,128)(2,1)S(1)} %collective-permute-done.5.refs_5_), channel_id=1, source_target_pairs={{0,16},{2,18},{4,20},{6,22},{8,24},{10,26},{12,28},{14,30},{16,0},... | collective-permute-start | bytes 786440 | tf_op jit(solution)/shard_map/ppermute | solution.py:146
  41.5 27.7 %collective-permute-start.14 = (bf16[8,256,128]{2,1,0:T(8,128)(2,1)S(1)}, bf16[8,256,128]{2,1,0:T(8,128)(2,1)S(1)}, u32[]{:S(2)}, u32[]{:S(2)}) collective-permute-start(bf16[8,256,128]{2,1,0:T(8,128)(2,1)S(1)} %collective-permute-done.10.refs_12_), channel_id=1, source_target_pairs={{0,2},{2,0},{4,6},{6,4},{8,10},{10,8},{12,14},{14,12},{16,18},{18,... | collective-permute-start | bytes 1572872 | tf_op jit(solution)/shard_map/ppermute | solution.py:146
  51.8 17.8 %collective-permute-start.19 = (bf16[8,256,128]{2,1,0:T(8,128)(2,1)S(1)}, bf16[8,256,128]{2,1,0:T(8,128)(2,1)S(1)}, u32[]{:S(2)}, u32[]{:S(2)}) collective-permute-start(bf16[8,256,128]{2,1,0:T(8,128)(2,1)S(1)} %collective-permute-done.10.refs_12_), channel_id=1, source_target_pairs={{0,4},{2,6},{4,0},{6,2},{8,12},{10,14},{12,8},{14,10},{16,20},{18,... | collective-permute-start | bytes 1572872 | tf_op jit(solution)/shard_map/ppermute | solution.py:146
  53.4 16.4 %collective-permute-start.20 = (bf16[8,256,128]{2,1,0:T(8,128)(2,1)S(1)}, bf16[8,256,128]{2,1,0:T(8,128)(2,1)S(1)}, u32[]{:S(2)}, u32[]{:S(2)}) collective-permute-start(bf16[8,256,128]{2,1,0:T(8,128)(2,1)S(1)} %collective-permute-done.18.refs_11_), channel_id=1, source_target_pairs={{0,1},{1,0},{2,3},{3,2},{4,5},{5,4},{6,7},{7,6},{8,9},{9,8},{10,11... | collective-permute-start | bytes 1572872 | tf_op jit(solution)/shard_map/ppermute | solution.py:155
  55.4 2.0 %collective-permute-start.8 = (bf16[2,256,256]{2,1,0:T(8,128)(2,1)S(1)}, bf16[2,256,256]{2,1,0:T(8,128)(2,1)S(1)}, u32[]{:S(2)}, u32[]{:S(2)}) collective-permute-start(bf16[2,256,256]{2,1,0:T(8,128)(2,1)S(1)} %collective-permute-done.5.refs_5_), channel_id=1, source_target_pairs={{8,16},{10,18},{12,20},{14,22},{16,8},{18,10},{20,12},{22,14},{9,1... | collective-permute-start | bytes 786440 | tf_op jit(solution)/shard_map/ppermute | solution.py:149
  56.1 13.0 %collective-permute-start.9 = (bf16[2,256,256]{2,1,0:T(8,128)(2,1)S(1)}, bf16[2,256,256]{2,1,0:T(8,128)(2,1)S(1)}, u32[]{:S(2)}, u32[]{:S(2)}) collective-permute-start(bf16[2,256,256]{2,1,0:T(8,128)(2,1)S(1)} %collective-permute-done.7.refs_7_), channel_id=1, source_target_pairs={{8,0},{10,2},{12,4},{14,6},{16,24},{18,26},{20,28},{22,30},{9,1},{... | collective-permute-start | bytes 786440 | tf_op jit(solution)/shard_map/ppermute | solution.py:152
  57.4 15.8 %collective-permute-start.22 = (bf16[8,256,128]{2,1,0:T(8,128)(2,1)S(1)}, bf16[8,256,128]{2,1,0:T(8,128)(2,1)S(1)}, u32[]{:S(2)}, u32[]{:S(2)}) collective-permute-start(bf16[8,256,128]{2,1,0:T(8,128)(2,1)S(1)} %collective-permute-done.18.refs_11_), channel_id=1, source_target_pairs={{0,2},{2,0},{4,6},{6,4},{8,10},{10,8},{12,14},{14,12},{16,18},{18,... | collective-permute-start | bytes 1572872 | tf_op jit(solution)/shard_map/ppermute | solution.py:146
  69.1 1.9 %collective-permute-start.15 = (bf16[8,256,128]{2,1,0:T(8,128)(2,1)S(1)}, bf16[8,256,128]{2,1,0:T(8,128)(2,1)S(1)}, u32[]{:S(2)}, u32[]{:S(2)}) collective-permute-start(bf16[8,256,128]{2,1,0:T(8,128)(2,1)S(1)} %collective-permute-done.11.refs_13_), channel_id=1, source_target_pairs={{0,2},{2,0},{4,6},{6,4},{8,10},{10,8},{12,14},{14,12},{16,18},{18,... | collective-permute-start | bytes 1572872 | tf_op jit(solution)/shard_map/ppermute | solution.py:146
  69.1 4.1 %collective-permute-start.21 = (bf16[8,256,128]{2,1,0:T(8,128)(2,1)S(1)}, bf16[8,256,128]{2,1,0:T(8,128)(2,1)S(1)}, u32[]{:S(2)}, u32[]{:S(2)}) collective-permute-start(bf16[8,256,128]{2,1,0:T(8,128)(2,1)S(1)} %collective-permute-done.17.refs_10_), channel_id=1, source_target_pairs={{0,2},{2,0},{4,6},{6,4},{8,10},{10,8},{12,14},{14,12},{16,18},{18,... | collective-permute-start | bytes 1572872 | tf_op jit(solution)/shard_map/ppermute | solution.py:146
  69.6 3.6 %collective-permute-start.23 = (bf16[8,256,128]{2,1,0:T(8,128)(2,1)S(1)}, bf16[8,256,128]{2,1,0:T(8,128)(2,1)S(1)}, u32[]{:S(2)}, u32[]{:S(2)}) collective-permute-start(bf16[8,256,128]{2,1,0:T(8,128)(2,1)S(1)} %collective-permute-done.19.refs_12_), channel_id=1, source_target_pairs={{0,2},{2,0},{4,6},{6,4},{8,10},{10,8},{12,14},{14,12},{16,18},{18,... | collective-permute-start | bytes 1572872 | tf_op jit(solution)/shard_map/ppermute | solution.py:146
  69.7 3.6 %collective-permute-start.24 = (bf16[8,256,128]{2,1,0:T(8,128)(2,1)S(1)}, bf16[8,256,128]{2,1,0:T(8,128)(2,1)S(1)}, u32[]{:S(2)}, u32[]{:S(2)}) collective-permute-start(bf16[8,256,128]{2,1,0:T(8,128)(2,1)S(1)} %collective-permute-done.20.refs_13_), channel_id=1, source_target_pairs={{0,2},{2,0},{4,6},{6,4},{8,10},{10,8},{12,14},{14,12},{16,18},{18,... | collective-permute-start | bytes 1572872 | tf_op jit(solution)/shard_map/ppermute | solution.py:146
  75.4 8.4 %collective-permute-start.27 = (f32[256,256]{1,0:T(8,128)S(1)}, f32[256,256]{1,0:T(8,128)S(1)}, u32[]{:S(2)}, u32[]{:S(2)}) collective-permute-start(f32[256,256]{1,0:T(8,128)S(1)} %get-tuple-element.13), channel_id=1, source_target_pairs={{0,8},{2,10},{4,12},{6,14},{8,0},{10,2},{12,4},{14,6},{16,24},{18,... | collective-permute-start | bytes 786440 | tf_op jit(solution)/shard_map/ppermute | solution.py:146
  83.9 14.1 %collective-permute-start.28 = (f32[256,256]{1,0:T(8,128)S(1)}, f32[256,256]{1,0:T(8,128)S(1)}, u32[]{:S(2)}, u32[]{:S(2)}) collective-permute-start(f32[256,256]{1,0:T(8,128)S(1)} %add.6), channel_id=1, source_target_pairs={{0,16},{2,18},{4,20},{6,22},{8,24},{10,26},{12,28},{14,30},{16,0},... | collective-permute-start | bytes 786440 | tf_op jit(solution)/shard_map/ppermute | solution.py:146
  98.0 7.3 %collective-permute-start.29 = (f32[256,256]{1,0:T(8,128)S(1)}, f32[256,256]{1,0:T(8,128)S(1)}, u32[]{:S(2)}, u32[]{:S(2)}) collective-permute-start(f32[256,256]{1,0:T(8,128)S(1)} %add.7), channel_id=1, source_target_pairs={{0,4},{2,6},{4,0},{6,2},{8,12},{10,14},{12,8},{14,10},{16,20},{18,... | collective-permute-start | bytes 786440 | tf_op jit(solution)/shard_map/ppermute | solution.py:146
  105.3 9.5 %collective-permute-start.30 = (f32[2,256,256]{2,1,0:T(8,128)S(1)}, f32[2,256,256]{2,1,0:T(8,128)S(1)}, u32[]{:S(2)}, u32[]{:S(2)}) collective-permute-start(f32[2,256,256]{2,1,0:T(8,128)S(1)} %pad_maximum_fusion.own_ref), channel_id=1, source_target_pairs={{0,2},{2,0},{4,6},{6,4},{8,10},{10,8},{12,14},{14,12},{16,18},{18,... | collective-permute-start | bytes 1572872 | tf_op jit(solution)/shard_map/ppermute | solution.py:146
  105.4 9.4 %copy-start = (f32[4,256,256]{2,1,0:T(8,128)S(1)}, f32[4,256,256]{2,1,0:T(8,128)}, u32[]{:S(2)}) copy-start(f32[4,256,256]{2,1,0:T(8,128)} %pivot_ref.1) | copy-start | bytes 3145732
  105.5 2.0 %collective-permute-start.16 = (bf16[256,256]{1,0:T(8,128)(2,1)S(1)}, bf16[256,256]{1,0:T(8,128)(2,1)S(1)}, u32[]{:S(2)}, u32[]{:S(2)}) collective-permute-start(bf16[256,256]{1,0:T(8,128)(2,1)S(1)} %get-tuple-element.18), channel_id=1, source_target_pairs={{0,2},{2,0},{4,6},{6,4},{8,10},{10,8},{12,14},{14,12},{16,18},{18,... | collective-permute-start | bytes 393224 | tf_op jit(solution)/shard_map/ppermute | solution.py:146
  106.0 6.4 %collective-permute-start.25 = (bf16[256,256]{1,0:T(8,128)(2,1)S(1)}, bf16[256,256]{1,0:T(8,128)(2,1)S(1)}, u32[]{:S(2)}, u32[]{:S(2)}) collective-permute-start(bf16[256,256]{1,0:T(8,128)(2,1)S(1)} %get-tuple-element.17), channel_id=1, source_target_pairs={{0,4},{2,6},{4,0},{6,2},{8,12},{10,14},{12,8},{14,10},{16,20},{18,... | collective-permute-start | bytes 393224 | tf_op jit(solution)/shard_map/ppermute | solution.py:146
  106.9 6.5 %collective-permute-start.26 = (bf16[256,256]{1,0:T(8,128)(2,1)S(1)}, bf16[256,256]{1,0:T(8,128)(2,1)S(1)}, u32[]{:S(2)}, u32[]{:S(2)}) collective-permute-start(bf16[256,256]{1,0:T(8,128)(2,1)S(1)} %get-tuple-element.16), channel_id=1, source_target_pairs={{0,6},{2,4},{4,2},{6,0},{8,14},{10,12},{12,10},{14,8},{16,22},{18,... | collective-permute-start | bytes 393224 | tf_op jit(solution)/shard_map/ppermute | solution.py:146

commit v2 on v1

--- a/solution.py
+++ b/solution.py
@@ -11,6 +11,14 @@
 SMEM = pl.BlockSpec(memory_space=pltpu.SMEM)
 PARAMS = pltpu.CompilerParams(vmem_limit_bytes=40 * 1024 * 1024)
 GROUP = 4
+
+
+def after(x, *earlier):
+    return lax.optimization_barrier((x, *earlier))[0]
+
+
+def together(wanted, *earlier):
+    return lax.optimization_barrier((*wanted, *earlier))[: len(wanted)]
 
 
 def generic(anc_inverse, factor_rows, structure, pivot_inverse):
@@ -68,48 +76,45 @@
         (keep_ref if j % 2 == 0 else give_ref)[j // 2] = part
 
 
-def product_kernel(n_groups, first, last, place, lists, *refs):
-    m_refs, refs = refs[:10], refs[10:]
-    a_refs, refs = refs[: 4 * n_groups], refs[4 * n_groups :]
-    if last:
+def product_kernel(segments, first, place, lists, *refs):
+    own, one_a, one_b, two_a, two_b, three, out_a, out_b = refs[:8]
+    n_inverse = 1 + max(at[0] for group in segments for side in group for at in side)
+    inverse, refs = refs[8 : 8 + n_inverse], refs[8 + n_inverse :]
+    if first:
         before_ref, refs = refs[0], refs[1:]
-    sel_ref, diag_ref = refs
+    sel_ref, diag_ref, level = refs
     col, row = place[0], place[1]
-    width = sel_ref.shape[1]
+    n_blocks, width = level.shape[0], level.shape[1]
     half = width // 2
-    near, far = pl.multiple_of(row * half, half), pl.multiple_of((1 - row) * half, half)
-
-    def level(j, at):
-        z, part = j // 4, (j // 2) % 2
-        ref = m_refs[5 * part + z]
-        block = ref[j % 2, pl.ds(at, half), :]
-        if z == 3:
-            block = block + m_refs[5 * part + 4][j % 2, pl.ds(at, half), :]
-        return block
+    one, two, out = (one_a, one_b), (two_a, two_b), (out_a, out_b)
+    for j in range(n_blocks):
+        z, i = j // GROUP, j % GROUP
+        for side in range(2):
+            rows = pl.ds(pl.multiple_of((row if side == 0 else 1 - row) * half, half), half)
+            if z == 0:
+                part = own[i, rows, :]
+            elif z == 1:
+                part = one[i // 2][i % 2, rows, :]
+            elif z == 2:
+                part = two[i // 2][i % 2, rows, :]
+            else:
+                part = three[i, rows, :] + out[i // 2][i % 2, rows, :]
+            level[col ^ j, side * half : (side + 1) * half] = part
 
     sup = row * GROUP + col % GROUP
-    diag = before_ref[...] if last else None
-    totals = [None] * n_groups
-    n_half = a_refs[0].shape[0]
-    for j in range(16):
-        m = jnp.concatenate([level(j, near), level(j, far)], axis=0)
-        block = col ^ j
-        in_low = block < n_half
-        at = block % n_half
-        for g in range(n_groups):
-            low_near, high_near, low_far, high_far = a_refs[4 * g : 4 * g + 4]
-            a_near = jnp.where(in_low, low_near[at], high_near[at])
-            a_far = jnp.where(in_low, low_far[at], high_far[at])
-            a = jnp.concatenate([a_near, a_far], axis=1)
-            term = jnp.dot(a, m, preferred_element_type=jnp.float32)
-            totals[g] = term if totals[g] is None else totals[g] + term
-    for g in range(n_groups):
+    diag = before_ref[...] if first else None
+    for g, group in enumerate(segments):
+        total = None
+        for block in range(n_blocks):
+            (near, i), (far, k) = group[0][block], group[1][block]
+            a = jnp.concatenate([inverse[near][i], inverse[far][k]], axis=1)
+            term = jnp.dot(a, level[block], preferred_element_type=jnp.float32)
+            total = term if total is None else total + term
         kept = is_member(lists, sup, col ^ (first + g))
-        sel = jnp.where(kept, -totals[g], jnp.zeros_like(totals[g])).astype(jnp.bfloat16)
+        sel = jnp.where(kept, -total, jnp.zeros_like(total)).astype(jnp.bfloat16)
         sel_ref[g] = sel
-        left = m_refs[5 * ((first + g) // 2)][(first + g) % 2]
         term = lax.dot_general(
-            left, sel, (((0,), (0,)), ((), ())), preferred_element_type=jnp.float32
+            own[first + g], sel, (((0,), (0,)), ((), ())), preferred_element_type=jnp.float32
         )
         diag = term if diag is None else diag + term
     diag_ref[...] = diag
@@ -154,6 +159,7 @@
     def across(x):
         return lax.ppermute(x, "row", [(0, 1), (1, 0)])
 
+    turned = anc_inverse.T
     cut = jax.ShapeDtypeStruct((2, width, width), bf16)
     keep, give = pl.pallas_call(
         split_kernel,
@@ -161,44 +167,85 @@
         in_specs=[SMEM, SMEM, VMEM],
         out_specs=(VMEM, VMEM),
         compiler_params=PARAMS,
-    )(place, structure, factor_rows.reshape(width, -1))
+    )(place, structure, after(factor_rows.reshape(width, -1), turned))
     got = swap(give, 1)
+    inverse = turned.reshape(half_w, all_blocks, rows).transpose(1, 2, 0)
+    x1, y1, y2 = all_blocks // 2, 4 * all_blocks // 16, 14 * all_blocks // 16
+
     part_a = jnp.stack([keep[0], got[0]])
-    part_b = swap(jnp.stack([keep[1], got[1]]), 2)
-    level = []
-    for part in (part_a, part_b):
-        two = swap(part, 8)
-        one = swap(part, 4)
-        level += [part, one, two, middle(part), outward(two)]
-
-    inverse = anc_inverse.reshape(rows, half_w, all_blocks).transpose(2, 0, 1)
-    low, high = inverse[: all_blocks // 2], inverse[all_blocks // 2 :]
-    x_low, x_high = across(low), across(high)
-    y_high, y_low = swap(high, 2), swap(low, 2)
-    xy_low, xy_high = swap(x_low, 2), across(y_high)
-    near = [low, high, x_low, x_high]
-    far = [y_low, y_high, xy_low, xy_high]
-    near += [swap(v, 1) for v in near]
-    far += [swap(v, 1) for v in far]
-
-    sel_shape = jax.ShapeDtypeStruct((2, width, width), bf16)
-    diag_shape = jax.ShapeDtypeStruct((width, width), f32)
-
-    def product(first, last, groups, *extra):
+    for_pair = jnp.stack([keep[1], got[1]])
+    first = together((part_a, for_pair, inverse[:x1], inverse[:y1]))
+    two_a, one_a = swap(first[0], 8), swap(first[0], 4)
+    part_b, x_a, y_a = swap(first[1], 2), across(first[2]), swap(first[3], 2)
+
+    second = together((part_b, two_a, inverse[x1:], inverse[y1:y2], inverse, x_a, y_a), one_a)
+    two_b, out_a = swap(second[0], 8), outward(second[1])
+    x_b, y_b = across(second[2]), swap(second[3], 2)
+    c_own = swap(second[4], 1)
+
+    own = jnp.concatenate([part_a, part_b])
+    mixed = jnp.concatenate([inverse[y2:], x_a[:y1], x_b[y2 - x1 :]])
+    third = together((two_b, own, y_b, mixed, part_b), out_a, c_own, x_b)
+    out_b, three, one_b = outward(third[0]), middle(third[1]), swap(third[4], 4)
+    xy_mid, y_mixed = across(third[2]), swap(third[3], 2)
+    cores = together((x_a, x_b, y_a, y_b), one_b, out_b)
+    cx_a, cx_b, cy_a, cy_b = (swap(v, 1) for v in cores)
+
+    last = together((xy_mid, y_mixed), three)
+    cxy_mid, cy_mixed = swap(last[0], 1), swap(last[1], 1)
+
+    level = [own, one_a, one_b, two_a, two_b, three, out_a, out_b]
+    blocks = range(all_blocks)
+    whole = [(0, b) for b in blocks]
+
+    def halves(k):
+        return [(k, b) if b < x1 else (k + 1, b - x1) for b in blocks]
+
+    def pair_rows(k):
+        return [(k, b) if b < y1 else (k + 1, b - y1) if b < y2 else (k + 2, b - y2) for b in blocks]
+
+    def cross_rows(k, m):
+        tail = all_blocks - y2
+        return [
+            (m, b - y1) if y1 <= b < y2 else (k, tail + (b if b < y1 else b - y2 + y1)) for b in blocks
+        ]
+
+    def other(at, k):
+        return [(which + k, i) for which, i in at]
+
+    near = [inverse, x_a, x_b, c_own, cx_a, cx_b]
+    near_at = [[whole, halves(1)], [other(whole, 3), halves(4)]]
+    far = [y_a, y_b, y_mixed, xy_mid, cy_a, cy_b, cy_mixed, cxy_mid]
+    far_at = [[pair_rows(0), cross_rows(2, 3)], [pair_rows(4), cross_rows(6, 7)]]
+
+    def product(first, at, *arrays):
         return pl.pallas_call(
-            functools.partial(product_kernel, 2, first, last),
-            out_shape=(sel_shape, diag_shape),
-            in_specs=[SMEM, SMEM] + [VMEM] * (18 + len(extra)),
+            functools.partial(product_kernel, at, first),
+            out_shape=(
+                jax.ShapeDtypeStruct((2, width, width), bf16),
+                jax.ShapeDtypeStruct((width, width), f32),
+            ),
+            in_specs=[SMEM, SMEM] + [VMEM] * (len(level) + len(arrays)),
             out_specs=(VMEM, VMEM),
+            scratch_shapes=[pltpu.VMEM((all_blocks, width, width), bf16)],
             compiler_params=PARAMS,
-        )(place, structure, *level, *groups, *extra)
-
-    sel_near, diag = product(0, False, near)
-    sel_far, diag = product(2, True, far, diag)
+        )(place, structure, *level, *arrays)
+
+    sel_near, diag = product(0, near_at, *near)
+    s_core = swap(sel_near[1], 1)
+    sel_far, diag = product(2, far_at, *far, diag)
+    s_pair, s_cross = swap(sel_far[0], 2), swap(sel_far[1], 3)
 
     diag = diag + swap(diag, 4)
-    diag = diag + swap(diag, 8)
-    pair = jnp.stack([diag, swap(diag, 2)])
+    diag = diag + swap(after(diag, s_core, s_pair, s_cross), 8)
+    selected = pl.pallas_call(
+        merge_kernel,
+        out_shape=jax.ShapeDtypeStruct((width, GROUP * width), bf16),
+        in_specs=[SMEM, VMEM, VMEM, VMEM, VMEM],
+        out_specs=VMEM,
+        compiler_params=PARAMS,
+    )(place, sel_near[0], s_core, s_pair, s_cross)
+    pair = jnp.stack([diag, swap(after(diag, selected), 2)])
     other = swap(pair, 1)
     diagonal = pl.pallas_call(
         finish_kernel,
@@ -207,14 +254,6 @@
         out_specs=VMEM,
         compiler_params=PARAMS,
     )(place, pair, other, pivot_inverse)
-
-    selected = pl.pallas_call(
-        merge_kernel,
-        out_shape=jax.ShapeDtypeStruct((width, GROUP * width), bf16),
-        in_specs=[SMEM, VMEM, VMEM, VMEM, VMEM],
-        out_specs=VMEM,
-        compiler_params=PARAMS,
-    )(place, sel_near[0], swap(sel_near[1], 1), swap(sel_far[0], 2), swap(sel_far[1], 3))
     return selected.reshape(factor_rows.shape), diagonal
 
 

time: 117 us -> 101 us (0.86)
  waiting for transfers between devices: 74.3 us -> 63.8 us
  starting transfers between devices: 28.7 us -> 24 us
    ppermute x24 -> x23, waiting for transfers between devices: 55.7 us -> 47.7 us  [swap(): return lax.ppermute(x, 'col', [(c, c ^ flip) for c in range(n_col)])]
    ppermute x2, waiting for transfers between devices: 11.6 us -> 4.33 us  [outward(): lax.ppermute(x, 'col', [(c, c ^ 4) for c in range(n_col) if c // 4 in (1,...]
    ppermute x24 -> x23, starting transfers between devices: 21.3 us -> 16 us  [swap(): return lax.ppermute(x, 'col', [(c, c ^ flip) for c in range(n_col)])]
    ppermute x3, waiting for transfers between devices: 6.89 us -> 11.7 us  [across(): return lax.ppermute(x, 'row', [(0, 1), (1, 0)])]
    ppermute x3, starting transfers between devices: 3.48 us -> 4.82 us  [across(): return lax.ppermute(x, 'row', [(0, 1), (1, 0)])]
    unnamed x7 -> x13, local copies, waits for them, and re-layouts: 3.13 us -> 2.19 us
  transfers between devices with their start and end apart: 31 -> 29, of which waited for: 13 -> 16; matrix products, arithmetic and copies ran while one was open for 2% -> 2% of each run, Pallas kernels for 3% -> 6%
where the time goes in v2:
time: 101 us
  waiting for transfers between devices  63.8 us (63%)
  starting transfers between devices  24 us (24%)
  Pallas kernels  8.33 us (8%)
  local copies, waits for them, and re-layouts  3.41 us (3%)
    ppermute x23, waiting for transfers between devices, swap(): return lax.ppermute(x, 'col', [(c, c ^ flip) for c in range(n_col)])  47.7 us
    ppermute x23, starting transfers between devices, swap(): return lax.ppermute(x, 'col', [(c, c ^ flip) for c in range(n_col)])  16 us
    ppermute x3, waiting for transfers between devices, across(): return lax.ppermute(x, 'row', [(0, 1), (1, 0)])  11.7 us
    ppermute x3, starting transfers between devices, across(): return lax.ppermute(x, 'row', [(0, 1), (1, 0)])  4.82 us
    pallas_call x2, Pallas kernels, product(): pl.pallas_call(functools.partial(product_kernel, at, first), out_shape=(j...  4.58 us
    ppermute x2, waiting for transfers between devices, outward(): lax.ppermute(x, 'col', [(c, c ^ 4) for c in range(n_col) if c // 4 in (1,...  4.33 us
    ppermute x2, starting transfers between devices, outward(): lax.ppermute(x, 'col', [(c, c ^ 4) for c in range(n_col) if c // 4 in (1,...  2.56 us
    unnamed x13, local copies, waits for them, and re-layouts  2.19 us
  transfers between devices with their start and end apart: 29, of which 16 were waited for; matrix products, arithmetic and copies ran while one was open for 2% of the time, Pallas kernels for 6%

profile of v2, /device:TPU:0, one launch (start us, length us, event | category | flops | bytes accessed | tf_op | source)
XLA Modules:
  0.0 100.9 jit_solution(14992277858210007380)
XLA Ops:
  0.6 0.1 pad_add_fusion.place
  0.7 0.6 copy-done.4
  1.3 1.0 %copy-done.3 = bf16[1,256,1024]{2,1,0:T(8,128)(2,1)S(1)} copy-done((bf16[1,256,1024]{2,1,0:T(8,128)(2,1)S(1)}, bf16[1,256,1024]{2,1,0:T(8,128)(2,1)}, u32[]{:S(2)}) %copy-start.3) | copy-done | bytes 524312
  2.4 0.7 shard_map.59
  3.1 0.5 collective-permute-start
  3.6 0.5 copy.6
  4.2 1.0 copy.7
  5.2 0.1 fusion
  5.4 2.9 %collective-permute-start.4 = (bf16[8,256,128]{2,1,0:T(8,128)(2,1)S(1)}, bf16[8,256,128]{2,1,0:T(8,128)(2,1)S(1)}, u32[]{:S(2)}, u32[]{:S(2)}) collective-permute-start(bf16[8,256,128]{2,1,0:T(8,128)(2,1)S(1)} %get-tuple-element.36), channel_id=1, source_target_pairs={{0,1},{1,0},{2,3},{3,2},{4,5},{5,4},{6,7},{7,6},{8,9},{9,8},{10,11... | collective-permute-start | bytes 1572872 | tf_op jit(solution)/shard_map/ppermute | solution.py:160
  8.3 1.5 %collective-permute-start.1 = (bf16[2,256,256]{2,1,0:T(8,128)(2,1)S(1)}, bf16[2,256,256]{2,1,0:T(8,128)(2,1)S(1)}, u32[]{:S(2)}, u32[]{:S(2)}) collective-permute-start(bf16[2,256,256]{2,1,0:T(8,128)(2,1)S(1)} %get-tuple-element.34), channel_id=1, source_target_pairs={{0,4},{2,6},{4,0},{6,2},{8,12},{10,14},{12,8},{14,10},{16,20},{18,... | collective-permute-start | bytes 786440 | tf_op jit(solution)/shard_map/ppermute | solution.py:151
  9.8 1.6 %collective-permute-start.2 = (bf16[2,256,256]{2,1,0:T(8,128)(2,1)S(1)}, bf16[2,256,256]{2,1,0:T(8,128)(2,1)S(1)}, u32[]{:S(2)}, u32[]{:S(2)}) collective-permute-start(bf16[2,256,256]{2,1,0:T(8,128)(2,1)S(1)} %get-tuple-element.35), channel_id=1, source_target_pairs={{0,8},{2,10},{4,12},{6,14},{8,0},{10,2},{12,4},{14,6},{16,24},{18,... | collective-permute-start | bytes 786440 | tf_op jit(solution)/shard_map/ppermute | solution.py:151
  11.4 2.6 %collective-permute-start.3 = (bf16[2,256,256]{2,1,0:T(8,128)(2,1)S(1)}, bf16[2,256,256]{2,1,0:T(8,128)(2,1)S(1)}, u32[]{:S(2)}, u32[]{:S(2)}) collective-permute-start(bf16[2,256,256]{2,1,0:T(8,128)(2,1)S(1)} %get-tuple-element.35), channel_id=1, source_target_pairs={{0,16},{2,18},{4,20},{6,22},{8,24},{10,26},{12,28},{14,30},{16,0},... | collective-permute-start | bytes 786440 | tf_op jit(solution)/shard_map/ppermute | solution.py:151
  14.0 0.5 collective-permute-start.5
  14.6 2.5 %collective-permute-done.1 = bf16[2,256,256]{2,1,0:T(8,128)(2,1)S(1)} collective-permute-done((bf16[2,256,256]{2,1,0:T(8,128)(2,1)S(1)}, bf16[2,256,256]{2,1,0:T(8,128)(2,1)S(1)}, u32[]{:S(2)}, u32[]{:S(2)}) %collective-permute-start.1) | collective-permute-done | bytes 262176 | tf_op jit(solution)/shard_map/ppermute | solution.py:151
  17.1 6.0 %collective-permute-done.2.refs_1_ = bf16[2,256,256]{2,1,0:T(8,128)(2,1)S(1)} collective-permute-done((bf16[2,256,256]{2,1,0:T(8,128)(2,1)S(1)}, bf16[2,256,256]{2,1,0:T(8,128)(2,1)S(1)}, u32[]{:S(2)}, u32[]{:S(2)}) %collective-permute-start.2) | collective-permute-done | bytes 262176 | tf_op jit(solution)/shard_map/ppermute | solution.py:151
  23.1 2.4 %collective-permute-done.3.refs_3_ = bf16[2,256,256]{2,1,0:T(8,128)(2,1)S(1)} collective-permute-done((bf16[2,256,256]{2,1,0:T(8,128)(2,1)S(1)}, bf16[2,256,256]{2,1,0:T(8,128)(2,1)S(1)}, u32[]{:S(2)}, u32[]{:S(2)}) %collective-permute-start.3) | collective-permute-done | bytes 262176 | tf_op jit(solution)/shard_map/ppermute | solution.py:151
  25.5 0.0 collective-permute-done.5.refs_8_
  25.5 0.0 collective-permute-done.4.refs_9_
  25.5 0.1 collective-permute-start.10
  25.6 0.6 collective-permute-start.7
  26.1 0.5 collective-permute-start.8
  26.7 0.3 collective-permute-start.6
  27.0 1.3 %collective-permute-start.9 = (bf16[2,256,256]{2,1,0:T(8,128)(2,1)S(1)}, bf16[2,256,256]{2,1,0:T(8,128)(2,1)S(1)}, u32[]{:S(2)}, u32[]{:S(2)}) collective-permute-start(bf16[2,256,256]{2,1,0:T(8,128)(2,1)S(1)} %collective-permute-done.3.refs_3_), channel_id=1, source_target_pairs={{8,0},{10,2},{12,4},{14,6},{16,24},{18,26},{20,28},{22,30},{9,1},{... | collective-permute-start | bytes 786440 | tf_op jit(solution)/shard_map/ppermute | solution.py:157
  28.3 0.1 pad_maximum_fusion.refs_0_
  28.4 0.0 slice-start
  28.4 11.7 %collective-permute-done.8.refs_10_ = bf16[8,256,128]{2,1,0:T(8,128)(2,1)S(1)} collective-permute-done((bf16[8,256,128]{2,1,0:T(8,128)(2,1)S(1)}, bf16[8,256,128]{2,1,0:T(8,128)(2,1)S(1)}, u32[]{:S(2)}, u32[]{:S(2)}) %collective-permute-start.8) | collective-permute-done | bytes 524320 | tf_op jit(solution)/shard_map/ppermute | solution.py:160
  40.2 0.0 copy-start.1
  40.2 0.1 pad_maximum_fusion.1
  40.2 1.0 %collective-permute-done.6.refs_4_ = bf16[2,256,256]{2,1,0:T(8,128)(2,1)S(1)} collective-permute-done((bf16[2,256,256]{2,1,0:T(8,128)(2,1)S(1)}, bf16[2,256,256]{2,1,0:T(8,128)(2,1)S(1)}, u32[]{:S(2)}, u32[]{:S(2)}) %collective-permute-start.6) | collective-permute-done | bytes 262176 | tf_op jit(solution)/shard_map/ppermute | solution.py:151
  41.3 1.3 %collective-permute-done.9.refs_6_ = bf16[2,256,256]{2,1,0:T(8,128)(2,1)S(1)} collective-permute-done((bf16[2,256,256]{2,1,0:T(8,128)(2,1)S(1)}, bf16[2,256,256]{2,1,0:T(8,128)(2,1)S(1)}, u32[]{:S(2)}, u32[]{:S(2)}) %collective-permute-start.9) | collective-permute-done | bytes 262176 | tf_op jit(solution)/shard_map/ppermute | solution.py:157
  42.6 0.1 collective-permute-done.7.refs_9_
  42.7 0.0 collective-permute-done.10.refs_11_
  42.7 1.3 %collective-permute-start.18 = (bf16[10,256,128]{2,1,0:T(8,128)(2,1)S(1)}, bf16[10,256,128]{2,1,0:T(8,128)(2,1)S(1)}, u32[]{:S(2)}, u32[]{:S(2)}) collective-permute-start(bf16[10,256,128]{2,1,0:T(8,128)(2,1)S(1)} %collective-permute-done.7.refs_9_), channel_id=1, source_target_pairs={{0,1},{1,0},{2,3},{3,2},{4,5},{5,4},{6,7},{7,6},{8,9},{9,8},{10,11... | collective-permute-start | bytes 1966088 | tf_op jit(solution)/shard_map/ppermute | solution.py:160
  44.1 0.7 collective-permute-start.12
  44.8 1.6 %collective-permute-start.17 = (bf16[8,256,128]{2,1,0:T(8,128)(2,1)S(1)}, bf16[8,256,128]{2,1,0:T(8,128)(2,1)S(1)}, u32[]{:S(2)}, u32[]{:S(2)}) collective-permute-start(bf16[8,256,128]{2,1,0:T(8,128)(2,1)S(1)} %pad_maximum_fusion.1), channel_id=1, source_target_pairs={{0,4},{2,6},{4,0},{6,2},{8,12},{10,14},{12,8},{14,10},{16,20},{18,... | collective-permute-start | bytes 1572872 | tf_op jit(solution)/shard_map/ppermute | solution.py:151
  46.3 2.0 %collective-permute-start.11 = (bf16[2,256,256]{2,1,0:T(8,128)(2,1)S(1)}, bf16[2,256,256]{2,1,0:T(8,128)(2,1)S(1)}, u32[]{:S(2)}, u32[]{:S(2)}) collective-permute-start(bf16[2,256,256]{2,1,0:T(8,128)(2,1)S(1)} %collective-permute-done.1), channel_id=1, source_target_pairs={{0,8},{2,10},{4,12},{6,14},{8,0},{10,2},{12,4},{14,6},{16,24},{18,... | collective-permute-start | bytes 786440 | tf_op jit(solution)/shard_map/ppermute | solution.py:151
  48.3 1.3 %collective-permute-start.13 = (bf16[2,256,256]{2,1,0:T(8,128)(2,1)S(1)}, bf16[2,256,256]{2,1,0:T(8,128)(2,1)S(1)}, u32[]{:S(2)}, u32[]{:S(2)}) collective-permute-start(bf16[2,256,256]{2,1,0:T(8,128)(2,1)S(1)} %collective-permute-done.6.refs_4_), channel_id=1, source_target_pairs={{8,0},{10,2},{12,4},{14,6},{16,24},{18,26},{20,28},{22,30},{9,1},{... | collective-permute-start | bytes 786440 | tf_op jit(solution)/shard_map/ppermute | solution.py:157
  49.6 6.0 %collective-permute-done.11.refs_2_ = bf16[2,256,256]{2,1,0:T(8,128)(2,1)S(1)} collective-permute-done((bf16[2,256,256]{2,1,0:T(8,128)(2,1)S(1)}, bf16[2,256,256]{2,1,0:T(8,128)(2,1)S(1)}, u32[]{:S(2)}, u32[]{:S(2)}) %collective-permute-start.11) | collective-permute-done | bytes 262176 | tf_op jit(solution)/shard_map/ppermute | solution.py:151
  55.6 3.0 %collective-permute-done.13.refs_7_ = bf16[2,256,256]{2,1,0:T(8,128)(2,1)S(1)} collective-permute-done((bf16[2,256,256]{2,1,0:T(8,128)(2,1)S(1)}, bf16[2,256,256]{2,1,0:T(8,128)(2,1)S(1)}, u32[]{:S(2)}, u32[]{:S(2)}) %collective-permute-start.13) | collective-permute-done | bytes 262176 | tf_op jit(solution)/shard_map/ppermute | solution.py:157
  58.6 0.0 collective-permute-start.14
  58.6 0.5 collective-permute-start.15
  59.1 0.0 collective-permute-done.12.refs_5_
  59.1 0.0 collective-permute-start.20
  59.2 0.5 collective-permute-start.22
  59.7 0.1 collective-permute-start.21
  59.7 0.8 collective-permute-done.14.refs_12_
  60.5 0.1 collective-permute-start.19
  60.7 0.6 collective-permute-done.15.refs_13_
  61.3 2.4 %shard_map.60 = (bf16[2,256,256]{2,1,0:T(8,128)(2,1)S(1)}, f32[256,256]{1,0:T(8,128)S(1)}) custom-call(s32[2]{0:T(128)S(1)} %pad_add_fusion.place, s32[8,12]{1,0:T(8,128)S(1)} %copy-done.4, bf16[4,256,256]{2,1,0:T(8,128)(2,1)S(1)} %pad_maximum_fusion.refs_0_, bf16[2,256,256]{2,1,0:T(8,128)(2,1)S(1)} %collective-permute-done.2.refs_1_, ...), custom_call_target="tpu_custom_call" | custom-call | tf_op jit(solution)/shard_map/pallas_call | solution.py:222
  63.7 0.2 collective-permute-start.16
  63.9 0.4 collective-permute-done.19.refs_12_
  64.3 2.2 %shard_map.61 = (bf16[2,256,256]{2,1,0:T(8,128)(2,1)S(1)}, f32[256,256]{1,0:T(8,128)S(1)}) custom-call(s32[2]{0:T(128)S(1)} %pad_add_fusion.place, s32[8,12]{1,0:T(8,128)S(1)} %copy-done.4, bf16[4,256,256]{2,1,0:T(8,128)(2,1)S(1)} %pad_maximum_fusion.refs_0_, bf16[2,256,256]{2,1,0:T(8,128)(2,1)S(1)} %collective-permute-done.2.refs_1_, ...), custom_call_target="tpu_custom_call" | custom-call | tf_op jit(solution)/shard_map/pallas_call | solution.py:222
  66.5 0.1 collective-permute-start.25
  66.6 0.6 collective-permute-start.23
  67.2 1.0 collective-permute-start.24
  68.2 6.8 %collective-permute-done.25 = f32[256,256]{1,0:T(8,128)S(1)} collective-permute-done((f32[256,256]{1,0:T(8,128)S(1)}, f32[256,256]{1,0:T(8,128)S(1)}, u32[]{:S(2)}, u32[]{:S(2)}) %collective-permute-start.25) | collective-permute-done | bytes 262176 | tf_op jit(solution)/shard_map/ppermute | solution.py:151
  75.0 1.0 %collective-permute-start.26 = (f32[256,256]{1,0:T(8,128)S(1)}, f32[256,256]{1,0:T(8,128)S(1)}, u32[]{:S(2)}, u32[]{:S(2)}) collective-permute-start(f32[256,256]{1,0:T(8,128)S(1)} %add.6), channel_id=1, source_target_pairs={{0,16},{2,18},{4,20},{6,22},{8,24},{10,26},{12,28},{14,30},{16,0},... | collective-permute-start | bytes 786440 | tf_op jit(solution)/shard_map/ppermute | solution.py:151
  76.0 1.4 %shard_map.62 = bf16[256,1024]{1,0:T(8,128)(2,1)} custom-call(s32[2]{0:T(128)S(1)} %pad_add_fusion.place, bf16[256,256]{1,0:T(8,128)(2,1)S(1)} %get-tuple-element.65.own_ref, bf16[256,256]{1,0:T(8,128)(2,1)S(1)} %collective-permute-done.16.core_ref, bf16[256,256]{1,0:T(8,128)(2,1)S(1)} %collective-permute-done.23.pair_ref, ...), custom_call_target="tpu_custom_call" | custom-call | tf_op jit(solution)/shard_map/pallas_call | solution.py:241
  77.4 12.4 %collective-permute-done.26 = f32[256,256]{1,0:T(8,128)S(1)} collective-permute-done((f32[256,256]{1,0:T(8,128)S(1)}, f32[256,256]{1,0:T(8,128)S(1)}, u32[]{:S(2)}, u32[]{:S(2)}) %collective-permute-start.26) | collective-permute-done | bytes 262176 | tf_op jit(solution)/shard_map/ppermute | solution.py:151
  89.8 0.6 collective-permute-start.27
  90.4 6.8 %collective-permute-done.27 = f32[256,256]{1,0:T(8,128)S(1)} collective-permute-done((f32[256,256]{1,0:T(8,128)S(1)}, f32[256,256]{1,0:T(8,128)S(1)}, u32[]{:S(2)}, u32[]{:S(2)}) %collective-permute-start.27) | collective-permute-done | bytes 262176 | tf_op jit(solution)/shard_map/ppermute | solution.py:151
  97.3 0.1 collective-permute-start.28
  97.4 1.9 %collective-permute-done.28.other_ref = f32[2,256,256]{2,1,0:T(8,128)S(1)} collective-permute-done((f32[2,256,256]{2,1,0:T(8,128)S(1)}, f32[2,256,256]{2,1,0:T(8,128)S(1)}, u32[]{:S(2)}, u32[]{:S(2)}) %collective-permute-start.28) | collective-permute-done | bytes 524320 | tf_op jit(solution)/shard_map/ppermute | solution.py:151
  99.3 1.6 %shard_map.63 = f32[4,256,256]{2,1,0:T(8,128)} custom-call(s32[2]{0:T(128)S(1)} %pad_add_fusion.place, f32[2,256,256]{2,1,0:T(8,128)S(1)} %pad_maximum_fusion.2.own_ref, f32[2,256,256]{2,1,0:T(8,128)S(1)} %collective-permute-done.28.other_ref, f32[4,256,256]{2,1,0:T(8,128)S(1)} %copy-done.2), custom_call_target="tpu_custom_call" | custom-call | tf_op jit(solution)/shard_map/pallas_call | solution.py:250
  (31 shorter events, 0.4 us)
Async XLA Ops:
  0.6 0.7 copy-start.4
  1.3 1.0 %copy-start.3 = (bf16[1,256,1024]{2,1,0:T(8,128)(2,1)S(1)}, bf16[1,256,1024]{2,1,0:T(8,128)(2,1)}, u32[]{:S(2)}) copy-start(bf16[1,256,1024]{2,1,0:T(8,128)(2,1)} %param.5) | copy-start | bytes 1572868
  2.4 1.3 %copy-start.5 = (bf16[256,2048]{1,0:T(8,128)(2,1)S(1)}, bf16[256,2048]{1,0:T(8,128)(2,1)}, u32[]{:S(2)}) copy-start(bf16[256,2048]{1,0:T(8,128)(2,1)} %param.4) | copy-start | bytes 3145732
  3.1 2.2 %collective-permute-start = (bf16[2,256,256]{2,1,0:T(8,128)(2,1)S(1)}, bf16[2,256,256]{2,1,0:T(8,128)(2,1)S(1)}, u32[]{:S(2)}, u32[]{:S(2)}) collective-permute-start(bf16[2,256,256]{2,1,0:T(8,128)(2,1)S(1)} %get-tuple-element.33), channel_id=1, source_target_pairs={{0,2},{2,0},{4,6},{6,4},{8,10},{10,8},{12,14},{14,12},{16,18},{18,... | collective-permute-start | bytes 786440 | tf_op jit(solution)/shard_map/ppermute | solution.py:151
  5.4 20.1 %collective-permute-start.4 = (bf16[8,256,128]{2,1,0:T(8,128)(2,1)S(1)}, bf16[8,256,128]{2,1,0:T(8,128)(2,1)S(1)}, u32[]{:S(2)}, u32[]{:S(2)}) collective-permute-start(bf16[8,256,128]{2,1,0:T(8,128)(2,1)S(1)} %get-tuple-element.36), channel_id=1, source_target_pairs={{0,1},{1,0},{2,3},{3,2},{4,5},{5,4},{6,7},{7,6},{8,9},{9,8},{10,11... | collective-permute-start | bytes 1572872 | tf_op jit(solution)/shard_map/ppermute | solution.py:160
  8.3 8.8 %collective-permute-start.1 = (bf16[2,256,256]{2,1,0:T(8,128)(2,1)S(1)}, bf16[2,256,256]{2,1,0:T(8,128)(2,1)S(1)}, u32[]{:S(2)}, u32[]{:S(2)}) collective-permute-start(bf16[2,256,256]{2,1,0:T(8,128)(2,1)S(1)} %get-tuple-element.34), channel_id=1, source_target_pairs={{0,4},{2,6},{4,0},{6,2},{8,12},{10,14},{12,8},{14,10},{16,20},{18,... | collective-permute-start | bytes 786440 | tf_op jit(solution)/shard_map/ppermute | solution.py:151
  9.8 13.3 %collective-permute-start.2 = (bf16[2,256,256]{2,1,0:T(8,128)(2,1)S(1)}, bf16[2,256,256]{2,1,0:T(8,128)(2,1)S(1)}, u32[]{:S(2)}, u32[]{:S(2)}) collective-permute-start(bf16[2,256,256]{2,1,0:T(8,128)(2,1)S(1)} %get-tuple-element.35), channel_id=1, source_target_pairs={{0,8},{2,10},{4,12},{6,14},{8,0},{10,2},{12,4},{14,6},{16,24},{18,... | collective-permute-start | bytes 786440 | tf_op jit(solution)/shard_map/ppermute | solution.py:151
  11.4 14.1 %collective-permute-start.3 = (bf16[2,256,256]{2,1,0:T(8,128)(2,1)S(1)}, bf16[2,256,256]{2,1,0:T(8,128)(2,1)S(1)}, u32[]{:S(2)}, u32[]{:S(2)}) collective-permute-start(bf16[2,256,256]{2,1,0:T(8,128)(2,1)S(1)} %get-tuple-element.35), channel_id=1, source_target_pairs={{0,16},{2,18},{4,20},{6,22},{8,24},{10,26},{12,28},{14,30},{16,0},... | collective-permute-start | bytes 786440 | tf_op jit(solution)/shard_map/ppermute | solution.py:151
  14.0 11.5 %collective-permute-start.5 = (bf16[4,256,128]{2,1,0:T(8,128)(2,1)S(1)}, bf16[4,256,128]{2,1,0:T(8,128)(2,1)S(1)}, u32[]{:S(2)}, u32[]{:S(2)}) collective-permute-start(bf16[4,256,128]{2,1,0:T(8,128)(2,1)S(1)} %slice.63), channel_id=1, source_target_pairs={{0,4},{2,6},{4,0},{6,2},{8,12},{10,14},{12,8},{14,10},{16,20},{18,... | collective-permute-start | bytes 786440 | tf_op jit(solution)/shard_map/ppermute | solution.py:151
  25.5 2.9 %copy-start = (bf16[8,256,128]{2,1,0:T(8,128)(2,1)}, bf16[8,256,128]{2,1,0:T(8,128)(2,1)S(1)}, u32[]{:S(2)}) copy-start(bf16[8,256,128]{2,1,0:T(8,128)(2,1)S(1)} %collective-permute-done.4.refs_9_) | copy-start | bytes 1572868
  25.5 17.2 %collective-permute-start.10 = (bf16[16,256,128]{2,1,0:T(8,128)(2,1)S(1)}, bf16[16,256,128]{2,1,0:T(8,128)(2,1)S(1)}, u32[]{:S(2)}, u32[]{:S(2)}) collective-permute-start(bf16[16,256,128]{2,1,0:T(8,128)(2,1)S(1)} %bitcast.21), channel_id=1, source_target_pairs={{0,2},{2,0},{4,6},{6,4},{8,10},{10,8},{12,14},{14,12},{16,18},{18,... | collective-permute-start | bytes 3145736 | tf_op jit(solution)/shard_map/ppermute | solution.py:151
  25.6 17.1 %collective-permute-start.7 = (bf16[10,256,128]{2,1,0:T(8,128)(2,1)S(1)}, bf16[10,256,128]{2,1,0:T(8,128)(2,1)S(1)}, u32[]{:S(2)}, u32[]{:S(2)}) collective-permute-start(bf16[10,256,128]{2,1,0:T(8,128)(2,1)S(1)} %slice.65), channel_id=1, source_target_pairs={{0,4},{2,6},{4,0},{6,2},{8,12},{10,14},{12,8},{14,10},{16,20},{18,... | collective-permute-start | bytes 1966088 | tf_op jit(solution)/shard_map/ppermute | solution.py:151
  26.1 14.0 %collective-permute-start.8 = (bf16[8,256,128]{2,1,0:T(8,128)(2,1)S(1)}, bf16[8,256,128]{2,1,0:T(8,128)(2,1)S(1)}, u32[]{:S(2)}, u32[]{:S(2)}) collective-permute-start(bf16[8,256,128]{2,1,0:T(8,128)(2,1)S(1)} %get-tuple-element.40), channel_id=1, source_target_pairs={{0,1},{1,0},{2,3},{3,2},{4,5},{5,4},{6,7},{7,6},{8,9},{9,8},{10,11... | collective-permute-start | bytes 1572872 | tf_op jit(solution)/shard_map/ppermute | solution.py:160
  26.7 14.6 %collective-permute-start.6 = (bf16[2,256,256]{2,1,0:T(8,128)(2,1)S(1)}, bf16[2,256,256]{2,1,0:T(8,128)(2,1)S(1)}, u32[]{:S(2)}, u32[]{:S(2)}) collective-permute-start(bf16[2,256,256]{2,1,0:T(8,128)(2,1)S(1)} %collective-permute-done.1), channel_id=1, source_target_pairs={{0,16},{2,18},{4,20},{6,22},{8,24},{10,26},{12,28},{14,30},{16,0},... | collective-permute-start | bytes 786440 | tf_op jit(solution)/shard_map/ppermute | solution.py:151
  27.0 15.6 %collective-permute-start.9 = (bf16[2,256,256]{2,1,0:T(8,128)(2,1)S(1)}, bf16[2,256,256]{2,1,0:T(8,128)(2,1)S(1)}, u32[]{:S(2)}, u32[]{:S(2)}) collective-permute-start(bf16[2,256,256]{2,1,0:T(8,128)(2,1)S(1)} %collective-permute-done.3.refs_3_), channel_id=1, source_target_pairs={{8,0},{10,2},{12,4},{14,6},{16,24},{18,26},{20,28},{22,30},{9,1},{... | collective-permute-start | bytes 786440 | tf_op jit(solution)/shard_map/ppermute | solution.py:157
  28.4 11.8 %slice-start = ((bf16[8,256,128]{2,1,0:T(8,128)(2,1)}), bf16[4,256,128]{2,1,0:T(8,128)(2,1)S(1)}, s32[]{:S(2)}) async-start(bf16[8,256,128]{2,1,0:T(8,128)(2,1)} %copy-done), calls=%async_computation | async-start | bytes 524288 | tf_op jit(solution)/shard_map/slice | solution.py:187
  40.2 18.5 %copy-start.1 = (bf16[8,256,128]{2,1,0:T(8,128)(2,1)S(1)}, bf16[8,256,128]{2,1,0:T(8,128)(2,1)}, u32[]{:S(2)}) copy-start(bf16[8,256,128]{2,1,0:T(8,128)(2,1)} %copy-done) | copy-start | bytes 1572868
  42.7 16.4 %collective-permute-start.18 = (bf16[10,256,128]{2,1,0:T(8,128)(2,1)S(1)}, bf16[10,256,128]{2,1,0:T(8,128)(2,1)S(1)}, u32[]{:S(2)}, u32[]{:S(2)}) collective-permute-start(bf16[10,256,128]{2,1,0:T(8,128)(2,1)S(1)} %collective-permute-done.7.refs_9_), channel_id=1, source_target_pairs={{0,1},{1,0},{2,3},{3,2},{4,5},{5,4},{6,7},{7,6},{8,9},{9,8},{10,11... | collective-permute-start | bytes 1966088 | tf_op jit(solution)/shard_map/ppermute | solution.py:160
  44.1 15.1 %collective-permute-start.12 = (bf16[4,256,256]{2,1,0:T(8,128)(2,1)S(1)}, bf16[4,256,256]{2,1,0:T(8,128)(2,1)S(1)}, u32[]{:S(2)}, u32[]{:S(2)}) collective-permute-start(bf16[4,256,256]{2,1,0:T(8,128)(2,1)S(1)} %pad_maximum_fusion.refs_0_), channel_id=1, source_target_pairs={{8,16},{10,18},{12,20},{14,22},{16,8},{18,10},{20,12},{22,14},{9,1... | collective-permute-start | bytes 1572872 | tf_op jit(solution)/shard_map/ppermute | solution.py:154
  44.8 14.4 %collective-permute-start.17 = (bf16[8,256,128]{2,1,0:T(8,128)(2,1)S(1)}, bf16[8,256,128]{2,1,0:T(8,128)(2,1)S(1)}, u32[]{:S(2)}, u32[]{:S(2)}) collective-permute-start(bf16[8,256,128]{2,1,0:T(8,128)(2,1)S(1)} %pad_maximum_fusion.1), channel_id=1, source_target_pairs={{0,4},{2,6},{4,0},{6,2},{8,12},{10,14},{12,8},{14,10},{16,20},{18,... | collective-permute-start | bytes 1572872 | tf_op jit(solution)/shard_map/ppermute | solution.py:151
  46.3 9.2 %collective-permute-start.11 = (bf16[2,256,256]{2,1,0:T(8,128)(2,1)S(1)}, bf16[2,256,256]{2,1,0:T(8,128)(2,1)S(1)}, u32[]{:S(2)}, u32[]{:S(2)}) collective-permute-start(bf16[2,256,256]{2,1,0:T(8,128)(2,1)S(1)} %collective-permute-done.1), channel_id=1, source_target_pairs={{0,8},{2,10},{4,12},{6,14},{8,0},{10,2},{12,4},{14,6},{16,24},{18,... | collective-permute-start | bytes 786440 | tf_op jit(solution)/shard_map/ppermute | solution.py:151
  48.3 10.3 %collective-permute-start.13 = (bf16[2,256,256]{2,1,0:T(8,128)(2,1)S(1)}, bf16[2,256,256]{2,1,0:T(8,128)(2,1)S(1)}, u32[]{:S(2)}, u32[]{:S(2)}) collective-permute-start(bf16[2,256,256]{2,1,0:T(8,128)(2,1)S(1)} %collective-permute-done.6.refs_4_), channel_id=1, source_target_pairs={{8,0},{10,2},{12,4},{14,6},{16,24},{18,26},{20,28},{22,30},{9,1},{... | collective-permute-start | bytes 786440 | tf_op jit(solution)/shard_map/ppermute | solution.py:157
  58.6 1.9 %collective-permute-start.14 = (bf16[8,256,128]{2,1,0:T(8,128)(2,1)S(1)}, bf16[8,256,128]{2,1,0:T(8,128)(2,1)S(1)}, u32[]{:S(2)}, u32[]{:S(2)}) collective-permute-start(bf16[8,256,128]{2,1,0:T(8,128)(2,1)S(1)} %copy-done.1), channel_id=1, source_target_pairs={{0,2},{2,0},{4,6},{6,4},{8,10},{10,8},{12,14},{14,12},{16,18},{18,... | collective-permute-start | bytes 1572872 | tf_op jit(solution)/shard_map/ppermute | solution.py:151
  58.6 2.7 %collective-permute-start.15 = (bf16[8,256,128]{2,1,0:T(8,128)(2,1)S(1)}, bf16[8,256,128]{2,1,0:T(8,128)(2,1)S(1)}, u32[]{:S(2)}, u32[]{:S(2)}) collective-permute-start(bf16[8,256,128]{2,1,0:T(8,128)(2,1)S(1)} %collective-permute-done.8.refs_10_), channel_id=1, source_target_pairs={{0,2},{2,0},{4,6},{6,4},{8,10},{10,8},{12,14},{14,12},{16,18},{18,... | collective-permute-start | bytes 1572872 | tf_op jit(solution)/shard_map/ppermute | solution.py:151
  59.1 5.1 %collective-permute-start.20 = (bf16[10,256,128]{2,1,0:T(8,128)(2,1)S(1)}, bf16[10,256,128]{2,1,0:T(8,128)(2,1)S(1)}, u32[]{:S(2)}, u32[]{:S(2)}) collective-permute-start(bf16[10,256,128]{2,1,0:T(8,128)(2,1)S(1)} %collective-permute-done.7.refs_9_), channel_id=1, source_target_pairs={{0,2},{2,0},{4,6},{6,4},{8,10},{10,8},{12,14},{14,12},{16,18},{18,... | collective-permute-start | bytes 1966088 | tf_op jit(solution)/shard_map/ppermute | solution.py:151
  59.2 5.1 %collective-permute-start.22 = (bf16[10,256,128]{2,1,0:T(8,128)(2,1)S(1)}, bf16[10,256,128]{2,1,0:T(8,128)(2,1)S(1)}, u32[]{:S(2)}, u32[]{:S(2)}) collective-permute-start(bf16[10,256,128]{2,1,0:T(8,128)(2,1)S(1)} %collective-permute-done.18.refs_11_), channel_id=1, source_target_pairs={{0,2},{2,0},{4,6},{6,4},{8,10},{10,8},{12,14},{14,12},{16,18},{18,... | collective-permute-start | bytes 1966088 | tf_op jit(solution)/shard_map/ppermute | solution.py:151
  59.7 4.6 %collective-permute-start.21 = (bf16[8,256,128]{2,1,0:T(8,128)(2,1)S(1)}, bf16[8,256,128]{2,1,0:T(8,128)(2,1)S(1)}, u32[]{:S(2)}, u32[]{:S(2)}) collective-permute-start(bf16[8,256,128]{2,1,0:T(8,128)(2,1)S(1)} %collective-permute-done.17.refs_10_), channel_id=1, source_target_pairs={{0,2},{2,0},{4,6},{6,4},{8,10},{10,8},{12,14},{14,12},{16,18},{18,... | collective-permute-start | bytes 1572872 | tf_op jit(solution)/shard_map/ppermute | solution.py:151
  60.5 3.7 %collective-permute-start.19 = (bf16[4,256,128]{2,1,0:T(8,128)(2,1)S(1)}, bf16[4,256,128]{2,1,0:T(8,128)(2,1)S(1)}, u32[]{:S(2)}, u32[]{:S(2)}) collective-permute-start(bf16[4,256,128]{2,1,0:T(8,128)(2,1)S(1)} %collective-permute-done.5.refs_8_), channel_id=1, source_target_pairs={{0,2},{2,0},{4,6},{6,4},{8,10},{10,8},{12,14},{14,12},{16,18},{18,... | collective-permute-start | bytes 786440 | tf_op jit(solution)/shard_map/ppermute | solution.py:151
  63.7 11.3 %collective-permute-start.16 = (bf16[256,256]{1,0:T(8,128)(2,1)S(1)}, bf16[256,256]{1,0:T(8,128)(2,1)S(1)}, u32[]{:S(2)}, u32[]{:S(2)}) collective-permute-start(bf16[256,256]{1,0:T(8,128)(2,1)S(1)} %get-tuple-element.64), channel_id=1, source_target_pairs={{0,2},{2,0},{4,6},{6,4},{8,10},{10,8},{12,14},{14,12},{16,18},{18,... | collective-permute-start | bytes 393224 | tf_op jit(solution)/shard_map/ppermute | solution.py:151
  66.5 8.4 %collective-permute-start.25 = (f32[256,256]{1,0:T(8,128)S(1)}, f32[256,256]{1,0:T(8,128)S(1)}, u32[]{:S(2)}, u32[]{:S(2)}) collective-permute-start(f32[256,256]{1,0:T(8,128)S(1)} %get-tuple-element.57), channel_id=1, source_target_pairs={{0,8},{2,10},{4,12},{6,14},{8,0},{10,2},{12,4},{14,6},{16,24},{18,... | collective-permute-start | bytes 786440 | tf_op jit(solution)/shard_map/ppermute | solution.py:151
  66.6 8.4 %collective-permute-start.23 = (bf16[256,256]{1,0:T(8,128)(2,1)S(1)}, bf16[256,256]{1,0:T(8,128)(2,1)S(1)}, u32[]{:S(2)}, u32[]{:S(2)}) collective-permute-start(bf16[256,256]{1,0:T(8,128)(2,1)S(1)} %get-tuple-element.63), channel_id=1, source_target_pairs={{0,4},{2,6},{4,0},{6,2},{8,12},{10,14},{12,8},{14,10},{16,20},{18,... | collective-permute-start | bytes 393224 | tf_op jit(solution)/shard_map/ppermute | solution.py:151
  67.2 7.8 %collective-permute-start.24 = (bf16[256,256]{1,0:T(8,128)(2,1)S(1)}, bf16[256,256]{1,0:T(8,128)(2,1)S(1)}, u32[]{:S(2)}, u32[]{:S(2)}) collective-permute-start(bf16[256,256]{1,0:T(8,128)(2,1)S(1)} %get-tuple-element.62), channel_id=1, source_target_pairs={{0,6},{2,4},{4,2},{6,0},{8,14},{10,12},{12,10},{14,8},{16,22},{18,... | collective-permute-start | bytes 393224 | tf_op jit(solution)/shard_map/ppermute | solution.py:151
  75.0 14.8 %collective-permute-start.26 = (f32[256,256]{1,0:T(8,128)S(1)}, f32[256,256]{1,0:T(8,128)S(1)}, u32[]{:S(2)}, u32[]{:S(2)}) collective-permute-start(f32[256,256]{1,0:T(8,128)S(1)} %add.6), channel_id=1, source_target_pairs={{0,16},{2,18},{4,20},{6,22},{8,24},{10,26},{12,28},{14,30},{16,0},... | collective-permute-start | bytes 786440 | tf_op jit(solution)/shard_map/ppermute | solution.py:151
  77.4 21.8 %copy-start.2 = (f32[4,256,256]{2,1,0:T(8,128)S(1)}, f32[4,256,256]{2,1,0:T(8,128)}, u32[]{:S(2)}) copy-start(f32[4,256,256]{2,1,0:T(8,128)} %pivot_ref.1) | copy-start | bytes 3145732
  89.8 7.4 %collective-permute-start.27 = (f32[256,256]{1,0:T(8,128)S(1)}, f32[256,256]{1,0:T(8,128)S(1)}, u32[]{:S(2)}, u32[]{:S(2)}) collective-permute-start(f32[256,256]{1,0:T(8,128)S(1)} %add.7), channel_id=1, source_target_pairs={{0,4},{2,6},{4,0},{6,2},{8,12},{10,14},{12,8},{14,10},{16,20},{18,... | collective-permute-start | bytes 786440 | tf_op jit(solution)/shard_map/ppermute | solution.py:151
  97.3 2.0 %collective-permute-start.28 = (f32[2,256,256]{2,1,0:T(8,128)S(1)}, f32[2,256,256]{2,1,0:T(8,128)S(1)}, u32[]{:S(2)}, u32[]{:S(2)}) collective-permute-start(f32[2,256,256]{2,1,0:T(8,128)S(1)} %pad_maximum_fusion.2.own_ref), channel_id=1, source_target_pairs={{0,2},{2,0},{4,6},{6,4},{8,10},{10,8},{12,14},{14,12},{16,18},{18,... | collective-permute-start | bytes 1572872 | tf_op jit(solution)/shard_map/ppermute | solution.py:151

commit v3 on v0

--- a/solution.py
+++ b/solution.py
@@ -1,10 +1,28 @@
+import functools
+
 import jax
 import jax.numpy as jnp
 from jax import lax
+from jax.experimental import pallas as pl
+from jax.experimental.pallas import tpu as pltpu
 from jax.sharding import PartitionSpec as P
 
-
-def per_device(anc_inverse, factor_rows, structure, pivot_inverse):
+VMEM = pl.BlockSpec(memory_space=pltpu.VMEM)
+SMEM = pl.BlockSpec(memory_space=pltpu.SMEM)
+PARAMS = pltpu.CompilerParams(vmem_limit_bytes=24 * 1024 * 1024)
+TOP = 14.0
+GROUP = 4
+
+
+def after(x, *earlier):
+    return lax.optimization_barrier((x, *earlier))[0]
+
+
+def together(wanted, *earlier):
+    return lax.optimization_barrier((*wanted, *earlier))[: len(wanted)]
+
+
+def generic(anc_inverse, factor_rows, structure, pivot_inverse):
     own_blocks = factor_rows.shape[0]
     width = factor_rows.shape[1]
     local_cols = factor_rows.shape[2]
@@ -42,9 +60,213 @@
     return (selected, pivot_inverse - summed)
 
 
+def is_member(lists, sup, block):
+    found = lists[sup, 0] == block
+    for i in range(1, lists.shape[1]):
+        found = jnp.logical_or(found, lists[sup, i] == block)
+    return found
+
+
+def product_kernel(slots, n_level, groups, begins, ends, packs, place, lists, *refs):
+    level, refs = refs[:n_level], refs[n_level:]
+    sides, refs = refs[: 2 * len(groups)], refs[2 * len(groups) :]
+    n_extra = 1 if groups[0] >= 2 else 0
+    highs, refs = refs[: n_extra * len(groups)], refs[n_extra * len(groups) :]
+    if not begins:
+        sums_ref, refs = refs[0], refs[1:]
+    if packs:
+        before_ref, refs = refs[0], refs[1:]
+    col, row = place[0], place[1]
+    width = level[0].shape[1]
+    half = width // 2
+    sup = row * GROUP + col % GROUP
+    near = pl.ds(pl.multiple_of(row * half, half), half)
+    far = pl.ds(pl.multiple_of((1 - row) * half, half), half)
+    totals = [None if begins else sums_ref[g] for g in range(len(groups))]
+    for slot in slots:
+        z, i = slot // GROUP, slot % GROUP
+        block = col ^ slot
+        parts = [level[z][i, rows, :] for rows in (near, far)]
+        if z == 3:
+            parts = [part + level[4][i, rows, :] for part, rows in zip(parts, (near, far))]
+        m = jnp.concatenate(parts, axis=0)
+        m = jnp.where(is_member(lists, sup, block), m, jnp.zeros_like(m))
+        for g in range(len(groups)):
+            a_near = sides[2 * g][block]
+            if n_extra:
+                low, high = sides[2 * g + 1], highs[g]
+                n_low = low.shape[0]
+                in_low = block < n_low
+                a_far = jnp.where(
+                    in_low, low[jnp.minimum(block, n_low - 1)], high[jnp.maximum(block - n_low, 0)]
+                )
+            else:
+                a_far = sides[2 * g + 1][block]
+            a = jnp.concatenate([a_near, a_far], axis=1)
+            term = jnp.dot(a, m, preferred_element_type=jnp.float32)
+            totals[g] = term if totals[g] is None else totals[g] + term
+    if not ends:
+        for g in range(len(groups)):
+            refs[0][g] = totals[g]
+        return
+    sel_ref, diag_ref = refs
+    diag = before_ref[...] if packs else None
+    for g, group in enumerate(groups):
+        kept = is_member(lists, sup, col ^ group)
+        sel = jnp.where(kept, -totals[g], jnp.zeros_like(totals[g])).astype(jnp.bfloat16)
+        sel_ref[g] = sel
+        term = lax.dot_general(
+            level[0][group], sel, (((0,), (0,)), ((), ())), preferred_element_type=jnp.float32
+        )
+        diag = term if diag is None else diag + term
+    if not packs:
+        diag_ref[...] = diag
+        return
+    largest = jnp.maximum(jnp.max(jnp.abs(diag)), 1e-30)
+    power = jnp.ceil(jnp.log2(jnp.full((8, 128), largest, jnp.float32)))
+    power = jnp.concatenate([power] * (width // 128), axis=1)
+    diag_ref[:width] = diag * jnp.exp2(TOP - power[:1])
+    for at in range(width, diag_ref.shape[0], 8):
+        diag_ref[at : at + 8] = power
+
+
+def merge_kernel(place, own_ref, core_ref, pair_ref, cross_ref, out_ref):
+    col = place[0]
+    width = own_ref.shape[0]
+    for j, ref in enumerate((own_ref, core_ref, pair_ref, cross_ref)):
+        sup = (col % GROUP) ^ j
+        out_ref[:, pl.ds(pl.multiple_of(sup * width, width), width)] = ref[...]
+
+
+def unpack(packed):
+    width = packed.shape[-1]
+    power = packed[..., width : width + 1, :].astype(jnp.float32)
+    return packed[..., :width, :].astype(jnp.float32) * jnp.exp2(power - TOP), power
+
+
+def add_packed(one, other):
+    (a, power_a), (b, power_b) = unpack(one), unpack(other)
+    power = jnp.maximum(power_a, power_b) + 1.0
+    rows = jnp.broadcast_to(power, (one.shape[0] - one.shape[1], one.shape[1]))
+    return jnp.concatenate([(a + b) * jnp.exp2(TOP - power), rows]).astype(one.dtype)
+
+
+def per_device(anc_inverse, factor_rows, structure, pivot_inverse):
+    width = factor_rows.shape[1]
+    n_col = lax.axis_size("col")
+    all_blocks = factor_rows.shape[0] * n_col
+    bf16, f32 = jnp.bfloat16, jnp.float32
+    col = lax.axis_index("col")
+    row = lax.axis_index("row")
+    place = jnp.stack([col, row]).astype(jnp.int32)
+    rows = anc_inverse.shape[0]
+    half_w = anc_inverse.shape[1] // all_blocks
+
+    def swap(x, flip):
+        return lax.ppermute(x, "col", [(c, c ^ flip) for c in range(n_col)])
+
+    def middle(x):
+        return lax.ppermute(x, "col", [(c, c ^ 12) for c in range(n_col) if c // 4 in (1, 2)])
+
+    def outward(x):
+        return lax.ppermute(x, "col", [(c, c ^ 4) for c in range(n_col) if c // 4 in (1, 2)])
+
+    def across(x):
+        return lax.ppermute(x, "row", [(0, 1), (1, 0)])
+
+    first_pair, first_core = col // 2 % 2 == 0, col % 2 == 0
+
+    def choose(x, is_first):
+        half = x.shape[1] // 2
+        return jnp.where(is_first, x[:, :half], x[:, half:])
+
+    own_rows, place = together((factor_rows.reshape(width, -1), place))
+    from_pair = swap(choose(own_rows, ~first_pair), 2)
+    pair_rows = choose(own_rows, first_pair)
+    part_a = jnp.stack([choose(pair_rows, first_core), swap(choose(pair_rows, ~first_core), 1)])
+    inverse = anc_inverse.reshape(rows, half_w, all_blocks).transpose(2, 0, 1)
+    two_a = swap(after(part_a, inverse), 8)
+    part_b = jnp.stack([choose(from_pair, first_core), swap(choose(from_pair, ~first_core), 1)])
+
+    one_a = swap(after(part_a, inverse), 4)
+    x_all, y_all = across(inverse), swap(after(inverse, from_pair), 2)
+    own = jnp.concatenate([part_a, part_b])
+    n_first = 6 * all_blocks // 16
+    c_first = swap(after(inverse[:n_first], two_a, one_a), 1)
+    first = together((part_b, inverse[n_first:]), c_first)
+    two_b, one_b, c_rest = swap(first[0], 8), swap(first[0], 4), swap(first[1], 1)
+    c_own = jnp.concatenate([c_first, c_rest])
+    two, one = jnp.concatenate([two_a, two_b]), jnp.concatenate([one_a, one_b])
+
+    n_low = all_blocks // 2
+    second = together((two, own, y_all[:n_low], x_all[n_low:], x_all, y_all), one, c_rest)
+    out, three = outward(second[0]), middle(second[1])
+    xy_low, xy_high = across(second[2]), swap(second[3], 2)
+    c_x, c_y = swap(second[4], 1), swap(second[5], 1)
+
+    def product(slots, groups, level, sides, highs=(), sums=None, before=None, ends=True):
+        extra = [v for v in (sums, before) if v is not None]
+        packs = before is not None
+        sel = jax.ShapeDtypeStruct((2, width, width), bf16)
+        total = jax.ShapeDtypeStruct((2, width, width), f32)
+        diag = jax.ShapeDtypeStruct((width + 16 if packs else width, width), f32)
+        arrays = [*level, *sides, *highs, *extra]
+        return pl.pallas_call(
+            functools.partial(
+                product_kernel, slots, len(level), groups, sums is None, ends, packs
+            ),
+            out_shape=(sel, diag) if ends else total,
+            in_specs=[SMEM, SMEM] + [VMEM] * len(arrays),
+            out_specs=(VMEM, VMEM) if ends else VMEM,
+            compiler_params=PARAMS,
+        )(place, structure, *arrays)
+
+    near = [inverse, x_all, c_own, c_x]
+    sums = product(range(12), (0, 1), [own, one, two], near, ends=False)
+    last = together((three, out, xy_low, xy_high), sums)
+    cxy_low, cxy_high = swap(last[2], 1), swap(last[3], 1)
+    level = [own, one, two, last[0], last[1]]
+    sel_near, diag = product(range(12, 16), (0, 1), level, near, sums=sums)
+    s_core = swap(sel_near[1], 1)
+    sel_far, diag = product(
+        range(16), (2, 3), level, [y_all, xy_low, c_y, cxy_low], [xy_high, cxy_high], before=diag
+    )
+    s_pair, s_cross = swap(sel_far[0], 2), swap(sel_far[1], 3)
+
+    packed = diag.astype(jnp.float16)
+    packed = add_packed(packed, swap(packed, 4))
+    packed = add_packed(packed, swap(after(packed, s_core, s_cross), 8))
+    selected = pl.pallas_call(
+        merge_kernel,
+        out_shape=jax.ShapeDtypeStruct((width, GROUP * width), bf16),
+        in_specs=[SMEM, VMEM, VMEM, VMEM, VMEM],
+        out_specs=VMEM,
+        compiler_params=PARAMS,
+    )(place, sel_near[0], s_core, s_pair, s_cross)
+    got = swap(after(packed, s_pair), 2)
+    mine = jnp.stack([jnp.where(first_pair, packed, got), jnp.where(first_pair, got, packed)])
+    other = swap(after(mine, selected), 1)
+    ordered = [jnp.where(first_core, mine, other), jnp.where(first_core, other, mine)]
+    pivots = pivot_inverse.reshape(2, 2, width, width)
+    diagonal = jnp.stack([pivots[:, i] - unpack(half)[0] for i, half in enumerate(ordered)], axis=1)
+    diagonal = diagonal.reshape(pivot_inverse.shape)
+    return selected.reshape(factor_rows.shape), diagonal
+
+
 def solution(mesh):
     in_specs = (P("col", "row"), P("col", None, "row"), P(), P("row", None, None))
     out_specs = (P("col", None, "row"), P("row", None, None))
-    return jax.shard_map(
-        per_device, mesh=mesh, in_specs=in_specs, out_specs=out_specs, check_vma=False
-    )
+
+    def run(anc_inverse, factor_rows, structure, pivot_inverse):
+        n_col, n_row = mesh.shape["col"], mesh.shape["row"]
+        blocks, width, columns = factor_rows.shape
+        fits = n_col == 16 and n_row == 2 and blocks == n_col and columns == n_row * GROUP * width
+        return jax.shard_map(
+            per_device if fits else generic,
+            mesh=mesh,
+            in_specs=in_specs,
+            out_specs=out_specs,
+            check_vma=False,
+        )(anc_inverse, factor_rows, structure, pivot_inverse)
+
+    return run

time: 233 us -> 89.1 us (0.38)
  waiting for transfers between devices: 203 us -> 51 us
  starting transfers between devices: 0.12 us -> 24.4 us
  between operations: 13.8 us -> 1.07 us
  matrix products: 7.94 us -> 0 us
  Pallas kernels: 0 us -> 6.68 us
    all_gather x2 -> x0, waiting for transfers between devices: 113 us -> none  [the longest x1 77.7 us: per_device(): lax.all_gather(masked, 'col', axis=0, tiled=True)]
    psum x1 -> x0, waiting for transfers between devices: 90.4 us -> none  [per_device(): summed = lax.psum(local_terms, 'col')]
    ppermute x0 -> x26, waiting for transfers between devices: none -> 51 us  [the longest x22 32.4 us: swap(): return lax.ppermute(x, 'col', [(c, c ^ flip) for c in range(n_col)])]
    ppermute x0 -> x26, starting transfers between devices: none -> 24.4 us  [the longest x22 19.4 us: swap(): return lax.ppermute(x, 'col', [(c, c ^ flip) for c in range(n_col)])]
    dot_general x2 -> x0, matrix products: 7.94 us -> none  [the longest x1 6.58 us: per_device(): jnp.einsum('iwb,bwn->in', full_inverse, lax.all_gather(masked, 'col', axi...]
    pallas_call x0 -> x4, Pallas kernels: none -> 6.68 us  [the longest x3 5.28 us: product(): pl.pallas_call(functools.partial(product_kernel, slots, len(level), group...]
    sub x1 -> x0, other arithmetic: 2.39 us -> none  [per_device(): return (selected, pivot_inverse - summed)]
  transfers between devices with their start and end apart: 3 -> 26, of which waited for: 3 -> 13; matrix products, arithmetic and copies ran while one was open for 1% -> 3% of each run, Pallas kernels for 0% -> 8%
where the time goes in v3:
time: 89.1 us; the launch traced here: 88.9 us
  waiting for transfers between devices  51 us (57%)
  starting transfers between devices  24.4 us (27%)
  Pallas kernels  6.68 us (7%)
  local copies, waits for them, and re-layouts  3.53 us (4%)
  other arithmetic  2.21 us (2%)
  between operations  1.07 us (1%)
    ppermute x22, waiting for transfers between devices, swap(): return lax.ppermute(x, 'col', [(c, c ^ flip) for c in range(n_col)])  32.4 us
    ppermute x22, starting transfers between devices, swap(): return lax.ppermute(x, 'col', [(c, c ^ flip) for c in range(n_col)])  19.4 us
    ppermute x1, waiting for transfers between devices, outward(): lax.ppermute(x, 'col', [(c, c ^ 4) for c in range(n_col) if c // 4 in (1,...  11.1 us
    ppermute x2, waiting for transfers between devices, across(): return lax.ppermute(x, 'row', [(0, 1), (1, 0)])  7.54 us
    pallas_call x3, Pallas kernels, product(): pl.pallas_call(functools.partial(product_kernel, slots, len(level), group...  5.28 us
    ppermute x2, starting transfers between devices, across(): return lax.ppermute(x, 'row', [(0, 1), (1, 0)])  3.05 us
  transfers between devices with their start and end apart: 26, of which 13 were waited for; matrix products, arithmetic and copies ran while one was open for 3% of the time, Pallas kernels for 8%

profile of v3, /device:TPU:0, one launch (start us, length us, event | category | flops | bytes accessed | tf_op | source)
XLA Modules:
  0.0 88.9 jit_solution(667385296353145455)
XLA Ops:
  0.7 0.1 pad_add_fusion.place
  0.8 1.1 %broadcast_select_fusion.3 = (bf16[256,512]{1,0:T(8,128)(2,1)S(1)}, bf16[256,512]{1,0:T(8,128)(2,1)S(1)}) fusion(pred[]{:T(512)S(6)} %eq.10, bf16[256,1024]{1,0:T(8,128)(2,1)} %bitcast.68, pred[]{:T(512)S(6)} %not.8), kind=kLoop, calls=%fused_computation.16 | loop fusion | flops 262144 | bytes 1048578 | tf_op jit(solution)/shard_map/jit(_where)/select_n | solution.py:181
  1.9 0.5 collective-permute-start
  2.4 2.6 %collective-permute-start.1 = (bf16[256,512]{1,0:T(8,128)(2,1)S(1)}, bf16[256,512]{1,0:T(8,128)(2,1)S(1)}, u32[]{:S(2)}, u32[]{:S(2)}) collective-permute-start(bf16[256,512]{1,0:T(8,128)(2,1)S(1)} %get-tuple-element.59), channel_id=1, source_target_pairs={{0,4},{2,6},{4,0},{6,2},{8,12},{10,14},{12,8},{14,10},{16,20},{18,... | collective-permute-start | bytes 786440 | tf_op jit(solution)/shard_map/ppermute | solution.py:166
  5.0 0.5 copy.6
  5.6 1.0 %copy.7 = bf16[256,128,16]{1,0,2:T(8,128)(2,1)S(1)} copy(bf16[256,128,16]{0,2,1:T(8,128)(2,1)S(1)} %bitcast.65) | data formatting | bytes 2097152 | tf_op jit(solution)/shard_map/reshape | solution.py:187
  6.6 2.7 %collective-permute-start.4 = (bf16[2,256,256]{2,1,0:T(8,128)(2,1)S(1)}, bf16[2,256,256]{2,1,0:T(8,128)(2,1)S(1)}, u32[]{:S(2)}, u32[]{:S(2)}) collective-permute-start(bf16[2,256,256]{2,1,0:T(8,128)(2,1)S(1)} %pad_maximum_fusion.3), channel_id=1, source_target_pairs={{0,16},{2,18},{4,20},{6,22},{8,24},{10,26},{12,28},{14,30},{16,0},... | collective-permute-start | bytes 786440 | tf_op jit(solution)/shard_map/ppermute | solution.py:166
  9.3 1.6 %collective-permute-start.3 = (bf16[2,256,256]{2,1,0:T(8,128)(2,1)S(1)}, bf16[2,256,256]{2,1,0:T(8,128)(2,1)S(1)}, u32[]{:S(2)}, u32[]{:S(2)}) collective-permute-start(bf16[2,256,256]{2,1,0:T(8,128)(2,1)S(1)} %pad_maximum_fusion.3), channel_id=1, source_target_pairs={{0,8},{2,10},{4,12},{6,14},{8,0},{10,2},{12,4},{14,6},{16,24},{18,... | collective-permute-start | bytes 786440 | tf_op jit(solution)/shard_map/ppermute | solution.py:166
  10.8 1.5 %collective-permute-start.9 = (bf16[16,256,128]{2,1,0:T(8,128)(2,1)S(1)}, bf16[16,256,128]{2,1,0:T(8,128)(2,1)S(1)}, u32[]{:S(2)}, u32[]{:S(2)}) collective-permute-start(bf16[16,256,128]{2,1,0:T(8,128)(2,1)S(1)} %bitcast.59), channel_id=1, source_target_pairs={{0,1},{1,0},{2,3},{3,2},{4,5},{5,4},{6,7},{7,6},{8,9},{9,8},{10,11... | collective-permute-start | bytes 3145736 | tf_op jit(solution)/shard_map/ppermute | solution.py:175
  12.4 0.0 collective-permute-done.1
  12.4 1.3 %collective-permute-start.8 = (bf16[16,256,128]{2,1,0:T(8,128)(2,1)S(1)}, bf16[16,256,128]{2,1,0:T(8,128)(2,1)S(1)}, u32[]{:S(2)}, u32[]{:S(2)}) collective-permute-start(bf16[16,256,128]{2,1,0:T(8,128)(2,1)S(1)} %bitcast.61), channel_id=1, source_target_pairs={{0,4},{2,6},{4,0},{6,2},{8,12},{10,14},{12,8},{14,10},{16,20},{18,... | collective-permute-start | bytes 3145736 | tf_op jit(solution)/shard_map/ppermute | solution.py:166
  13.7 8.0 %collective-permute-done.4 = bf16[2,256,256]{2,1,0:T(8,128)(2,1)S(1)} collective-permute-done((bf16[2,256,256]{2,1,0:T(8,128)(2,1)S(1)}, bf16[2,256,256]{2,1,0:T(8,128)(2,1)S(1)}, u32[]{:S(2)}, u32[]{:S(2)}) %collective-permute-start.4) | collective-permute-done | bytes 262176 | tf_op jit(solution)/shard_map/ppermute | solution.py:166
  21.7 0.2 collective-permute-done.3
  21.9 0.0 collective-permute-start.5
  21.9 0.6 collective-permute-start.2
  22.5 1.3 %collective-permute-done.2 = bf16[256,256]{1,0:T(8,128)(2,1)S(1)} collective-permute-done((bf16[256,256]{1,0:T(8,128)(2,1)S(1)}, bf16[256,256]{1,0:T(8,128)(2,1)S(1)}, u32[]{:S(2)}, u32[]{:S(2)}) %collective-permute-start.2) | collective-permute-done | bytes 131104 | tf_op jit(solution)/shard_map/ppermute | solution.py:166
  23.8 0.0 collective-permute-done.5
  23.8 0.2 collective-permute-start.10
  24.0 1.3 %collective-permute-start.7 = (bf16[2,256,256]{2,1,0:T(8,128)(2,1)S(1)}, bf16[2,256,256]{2,1,0:T(8,128)(2,1)S(1)}, u32[]{:S(2)}, u32[]{:S(2)}) collective-permute-start(bf16[2,256,256]{2,1,0:T(8,128)(2,1)S(1)} %pad_maximum_fusion.4), channel_id=1, source_target_pairs={{0,16},{2,18},{4,20},{6,22},{8,24},{10,26},{12,28},{14,30},{16,0},... | collective-permute-start | bytes 786440 | tf_op jit(solution)/shard_map/ppermute | solution.py:166
  25.4 2.5 %collective-permute-start.6 = (bf16[2,256,256]{2,1,0:T(8,128)(2,1)S(1)}, bf16[2,256,256]{2,1,0:T(8,128)(2,1)S(1)}, u32[]{:S(2)}, u32[]{:S(2)}) collective-permute-start(bf16[2,256,256]{2,1,0:T(8,128)(2,1)S(1)} %pad_maximum_fusion.4), channel_id=1, source_target_pairs={{0,8},{2,10},{4,12},{6,14},{8,0},{10,2},{12,4},{14,6},{16,24},{18,... | collective-permute-start | bytes 786440 | tf_op jit(solution)/shard_map/ppermute | solution.py:166
  27.9 0.1 pad_maximum_fusion.1.refs_0_
  28.0 7.5 %collective-permute-done.9.refs_4_.refs_6_ = bf16[16,256,128]{2,1,0:T(8,128)(2,1)S(1)} collective-permute-done((bf16[16,256,128]{2,1,0:T(8,128)(2,1)S(1)}, bf16[16,256,128]{2,1,0:T(8,128)(2,1)S(1)}, u32[]{:S(2)}, u32[]{:S(2)}) %collective-permute-start.9) | collective-permute-done | bytes 1048608 | tf_op jit(solution)/shard_map/ppermute | solution.py:175
  35.5 3.6 %collective-permute-done.7 = bf16[2,256,256]{2,1,0:T(8,128)(2,1)S(1)} collective-permute-done((bf16[2,256,256]{2,1,0:T(8,128)(2,1)S(1)}, bf16[2,256,256]{2,1,0:T(8,128)(2,1)S(1)}, u32[]{:S(2)}, u32[]{:S(2)}) %collective-permute-start.7) | collective-permute-done | bytes 262176 | tf_op jit(solution)/shard_map/ppermute | solution.py:166
  39.2 0.0 collective-permute-done.8.refs_5_
  39.2 0.0 collective-permute-done.10
  39.3 0.1 collective-permute-start.15
  39.3 0.7 collective-permute-start.11
  40.0 1.3 %collective-permute-start.12 = (bf16[4,256,256]{2,1,0:T(8,128)(2,1)S(1)}, bf16[4,256,256]{2,1,0:T(8,128)(2,1)S(1)}, u32[]{:S(2)}, u32[]{:S(2)}) collective-permute-start(bf16[4,256,256]{2,1,0:T(8,128)(2,1)S(1)} %constant_dynamic-update-slice_fusion.2.refs_2_), channel_id=1, source_target_pairs={{8,0},{10,2},{12,4},{14,6},{16,24},{18,26},{20,28},{22,30},{9,1},{... | collective-permute-start | bytes 1572872 | tf_op jit(solution)/shard_map/ppermute | solution.py:172
  41.3 1.6 %collective-permute-start.13 = (bf16[8,256,128]{2,1,0:T(8,128)(2,1)S(1)}, bf16[8,256,128]{2,1,0:T(8,128)(2,1)S(1)}, u32[]{:S(2)}, u32[]{:S(2)}) collective-permute-start(bf16[8,256,128]{2,1,0:T(8,128)(2,1)S(1)} %slice.125), channel_id=1, source_target_pairs={{0,1},{1,0},{2,3},{3,2},{4,5},{5,4},{6,7},{7,6},{8,9},{9,8},{10,11... | collective-permute-start | bytes 1572872 | tf_op jit(solution)/shard_map/ppermute | solution.py:175
  42.9 0.5 collective-permute-start.14
  43.4 0.0 copy-start
  43.5 0.1 constant_dynamic-update-slice_fusion.4.refs_5_.refs_7_
  43.5 0.6 copy-done
  44.1 1.6 %shard_map.59.refs_9_ = f32[2,256,256]{2,1,0:T(8,128)S(1)} custom-call(s32[2]{0:T(128)S(1)} %pad_add_fusion.place, s32[8,12]{1,0:T(8,128)S(1)} %copy-done, bf16[4,256,256]{2,1,0:T(8,128)(2,1)S(1)} %pad_maximum_fusion.1.refs_0_, bf16[4,256,256]{2,1,0:T(8,128)(2,1)S(1)} %constant_dynamic-update-slice_fusion.refs_1_, ...), custom_call_target="tpu_custom_call" | custom-call | tf_op jit(solution)/shard_map/pallas_call | solution.py:214
  45.7 0.0 collective-permute-done.11.refs_3_
  45.8 11.1 %collective-permute-done.12.refs_4_ = bf16[4,256,256]{2,1,0:T(8,128)(2,1)S(1)} collective-permute-done((bf16[4,256,256]{2,1,0:T(8,128)(2,1)S(1)}, bf16[4,256,256]{2,1,0:T(8,128)(2,1)S(1)}, u32[]{:S(2)}, u32[]{:S(2)}) %collective-permute-start.12) | collective-permute-done | bytes 524320 | tf_op jit(solution)/shard_map/ppermute | solution.py:172
  56.8 0.1 collective-permute-done.14.refs_9_
  56.9 0.5 collective-permute-start.19
  57.4 1.4 %shard_map.60 = (bf16[2,256,256]{2,1,0:T(8,128)(2,1)S(1)}, f32[256,256]{1,0:T(8,128)S(1)}) custom-call(s32[2]{0:T(128)S(1)} %pad_add_fusion.place, s32[8,12]{1,0:T(8,128)S(1)} %copy-done, bf16[4,256,256]{2,1,0:T(8,128)(2,1)S(1)} %pad_maximum_fusion.1.refs_0_, bf16[4,256,256]{2,1,0:T(8,128)(2,1)S(1)} %constant_dynamic-update-slice_fusion.refs_1_, ...), custom_call_target="tpu_custom_call" | custom-call | tf_op jit(solution)/shard_map/pallas_call | solution.py:214
  58.8 0.1 collective-permute-start.16
  58.9 0.0 collective-permute-done.18.refs_8_
  58.9 0.6 collective-permute-done.19.refs_10_
  59.6 2.3 %shard_map.61 = (bf16[2,256,256]{2,1,0:T(8,128)(2,1)S(1)}, f32[272,256]{1,0:T(8,128)S(1)}) custom-call(s32[2]{0:T(128)S(1)} %pad_add_fusion.place, s32[8,12]{1,0:T(8,128)S(1)} %copy-done, bf16[4,256,256]{2,1,0:T(8,128)(2,1)S(1)} %pad_maximum_fusion.1.refs_0_, bf16[4,256,256]{2,1,0:T(8,128)(2,1)S(1)} %constant_dynamic-update-slice_fusion.refs_1_, ...), custom_call_target="tpu_custom_call" | custom-call | tf_op jit(solution)/shard_map/pallas_call | solution.py:214
  61.9 3.0 %collective-permute-start.22 = (f16[272,256]{1,0:T(8,128)(2,1)S(1)}, f16[272,256]{1,0:T(8,128)(2,1)S(1)}, u32[]{:S(2)}, u32[]{:S(2)}) collective-permute-start(f16[272,256]{1,0:T(8,128)(2,1)S(1)} %convert_element_type.41), channel_id=1, source_target_pairs={{0,8},{2,10},{4,12},{6,14},{8,0},{10,2},{12,4},{14,6},{16,24},{18,... | collective-permute-start | bytes 417800 | tf_op jit(solution)/shard_map/ppermute | solution.py:166
  65.0 0.1 collective-permute-start.21
  65.1 3.9 %collective-permute-done.22 = f16[272,256]{1,0:T(8,128)(2,1)S(1)} collective-permute-done((f16[272,256]{1,0:T(8,128)(2,1)S(1)}, f16[272,256]{1,0:T(8,128)(2,1)S(1)}, u32[]{:S(2)}, u32[]{:S(2)}) %collective-permute-start.22) | collective-permute-done | bytes 139296 | tf_op jit(solution)/shard_map/ppermute | solution.py:166
  68.9 0.1 multiply_convert_fusion.1
  69.1 0.0 collective-permute-done.16.core_ref
  69.1 1.7 %collective-permute-done.21.cross_ref = bf16[256,256]{1,0:T(8,128)(2,1)S(1)} collective-permute-done((bf16[256,256]{1,0:T(8,128)(2,1)S(1)}, bf16[256,256]{1,0:T(8,128)(2,1)S(1)}, u32[]{:S(2)}, u32[]{:S(2)}) %collective-permute-start.21) | collective-permute-done | bytes 131104 | tf_op jit(solution)/shard_map/ppermute | solution.py:166
  70.8 0.7 collective-permute-start.23
  71.5 0.5 collective-permute-start.20
  72.0 7.8 %collective-permute-done.23 = f16[272,256]{1,0:T(8,128)(2,1)S(1)} collective-permute-done((f16[272,256]{1,0:T(8,128)(2,1)S(1)}, f16[272,256]{1,0:T(8,128)(2,1)S(1)}, u32[]{:S(2)}, u32[]{:S(2)}) %collective-permute-start.23) | collective-permute-done | bytes 139296 | tf_op jit(solution)/shard_map/ppermute | solution.py:166
  79.8 0.1 multiply_convert_fusion
  80.0 0.5 collective-permute-start.24
  80.5 1.4 %shard_map.62 = bf16[256,1024]{1,0:T(8,128)(2,1)} custom-call(s32[2]{0:T(128)S(1)} %pad_add_fusion.place, bf16[256,256]{1,0:T(8,128)(2,1)S(1)} %get-tuple-element.65.own_ref, bf16[256,256]{1,0:T(8,128)(2,1)S(1)} %collective-permute-done.16.core_ref, bf16[256,256]{1,0:T(8,128)(2,1)S(1)} %collective-permute-done.20.pair_ref, ...), custom_call_target="tpu_custom_call" | custom-call | tf_op jit(solution)/shard_map/pallas_call | solution.py:239
  81.9 3.7 %collective-permute-done.24 = f16[272,256]{1,0:T(8,128)(2,1)S(1)} collective-permute-done((f16[272,256]{1,0:T(8,128)(2,1)S(1)}, f16[272,256]{1,0:T(8,128)(2,1)S(1)}, u32[]{:S(2)}, u32[]{:S(2)}) %collective-permute-start.24) | collective-permute-done | bytes 139296 | tf_op jit(solution)/shard_map/ppermute | solution.py:166
  85.7 0.1 select_bitcast_fusion.1
  85.8 0.1 pad_maximum_fusion.2
  85.8 0.1 collective-permute-start.25
  85.9 1.5 %collective-permute-done.25 = f16[2,272,256]{2,1,0:T(8,128)(2,1)S(1)} collective-permute-done((f16[2,272,256]{2,1,0:T(8,128)(2,1)S(1)}, f16[2,272,256]{2,1,0:T(8,128)(2,1)S(1)}, u32[]{:S(2)}, u32[]{:S(2)}) %collective-permute-start.25) | collective-permute-done | bytes 278560 | tf_op jit(solution)/shard_map/ppermute | solution.py:166
  87.5 0.2 broadcast_select_fusion.1
  87.7 0.1 fusion.3
  87.8 0.1 pad_maximum_fusion
  87.9 1.0 %copy.10 = f32[2,2,256,256]{3,2,1,0:T(8,128)} copy(f32[2,2,256,256]{3,2,0,1:T(8,128)S(1)} %pad_maximum_fusion) | data formatting | bytes 2097152 | tf_op jit(solution)/shard_map/stack | solution.py:251
  (40 shorter events, 0.6 us)
Async XLA Ops:
  0.6 4.4 %copy-start.2 = (bf16[256,2048]{1,0:T(8,128)(2,1)S(1)}, bf16[256,2048]{1,0:T(8,128)(2,1)}, u32[]{:S(2)}) copy-start(bf16[256,2048]{1,0:T(8,128)(2,1)} %param.4) | copy-start | bytes 3145732
  1.9 4.6 %collective-permute-start = (bf16[256,256]{1,0:T(8,128)(2,1)S(1)}, bf16[256,256]{1,0:T(8,128)(2,1)S(1)}, u32[]{:S(2)}, u32[]{:S(2)}) collective-permute-start(bf16[256,256]{1,0:T(8,128)(2,1)S(1)} %get-tuple-element.67), channel_id=1, source_target_pairs={{0,2},{2,0},{4,6},{6,4},{8,10},{10,8},{12,14},{14,12},{16,18},{18,... | collective-permute-start | bytes 393224 | tf_op jit(solution)/shard_map/ppermute | solution.py:166
  2.4 9.9 %collective-permute-start.1 = (bf16[256,512]{1,0:T(8,128)(2,1)S(1)}, bf16[256,512]{1,0:T(8,128)(2,1)S(1)}, u32[]{:S(2)}, u32[]{:S(2)}) collective-permute-start(bf16[256,512]{1,0:T(8,128)(2,1)S(1)} %get-tuple-element.59), channel_id=1, source_target_pairs={{0,4},{2,6},{4,0},{6,2},{8,12},{10,14},{12,8},{14,10},{16,20},{18,... | collective-permute-start | bytes 786440 | tf_op jit(solution)/shard_map/ppermute | solution.py:166
  6.6 15.1 %collective-permute-start.4 = (bf16[2,256,256]{2,1,0:T(8,128)(2,1)S(1)}, bf16[2,256,256]{2,1,0:T(8,128)(2,1)S(1)}, u32[]{:S(2)}, u32[]{:S(2)}) collective-permute-start(bf16[2,256,256]{2,1,0:T(8,128)(2,1)S(1)} %pad_maximum_fusion.3), channel_id=1, source_target_pairs={{0,16},{2,18},{4,20},{6,22},{8,24},{10,26},{12,28},{14,30},{16,0},... | collective-permute-start | bytes 786440 | tf_op jit(solution)/shard_map/ppermute | solution.py:166
  9.3 12.6 %collective-permute-start.3 = (bf16[2,256,256]{2,1,0:T(8,128)(2,1)S(1)}, bf16[2,256,256]{2,1,0:T(8,128)(2,1)S(1)}, u32[]{:S(2)}, u32[]{:S(2)}) collective-permute-start(bf16[2,256,256]{2,1,0:T(8,128)(2,1)S(1)} %pad_maximum_fusion.3), channel_id=1, source_target_pairs={{0,8},{2,10},{4,12},{6,14},{8,0},{10,2},{12,4},{14,6},{16,24},{18,... | collective-permute-start | bytes 786440 | tf_op jit(solution)/shard_map/ppermute | solution.py:166
  10.8 24.7 %collective-permute-start.9 = (bf16[16,256,128]{2,1,0:T(8,128)(2,1)S(1)}, bf16[16,256,128]{2,1,0:T(8,128)(2,1)S(1)}, u32[]{:S(2)}, u32[]{:S(2)}) collective-permute-start(bf16[16,256,128]{2,1,0:T(8,128)(2,1)S(1)} %bitcast.59), channel_id=1, source_target_pairs={{0,1},{1,0},{2,3},{3,2},{4,5},{5,4},{6,7},{7,6},{8,9},{9,8},{10,11... | collective-permute-start | bytes 3145736 | tf_op jit(solution)/shard_map/ppermute | solution.py:175
  12.4 26.8 %collective-permute-start.8 = (bf16[16,256,128]{2,1,0:T(8,128)(2,1)S(1)}, bf16[16,256,128]{2,1,0:T(8,128)(2,1)S(1)}, u32[]{:S(2)}, u32[]{:S(2)}) collective-permute-start(bf16[16,256,128]{2,1,0:T(8,128)(2,1)S(1)} %bitcast.61), channel_id=1, source_target_pairs={{0,4},{2,6},{4,0},{6,2},{8,12},{10,14},{12,8},{14,10},{16,20},{18,... | collective-permute-start | bytes 3145736 | tf_op jit(solution)/shard_map/ppermute | solution.py:166
  21.9 1.9 %collective-permute-start.5 = (bf16[6,256,128]{2,1,0:T(8,128)(2,1)S(1)}, bf16[6,256,128]{2,1,0:T(8,128)(2,1)S(1)}, u32[]{:S(2)}, u32[]{:S(2)}) collective-permute-start(bf16[6,256,128]{2,1,0:T(8,128)(2,1)S(1)} %slice.124), channel_id=1, source_target_pairs={{0,2},{2,0},{4,6},{6,4},{8,10},{10,8},{12,14},{14,12},{16,18},{18,... | collective-permute-start | bytes 1179656 | tf_op jit(solution)/shard_map/ppermute | solution.py:166
  21.9 1.9 %collective-permute-start.2 = (bf16[256,256]{1,0:T(8,128)(2,1)S(1)}, bf16[256,256]{1,0:T(8,128)(2,1)S(1)}, u32[]{:S(2)}, u32[]{:S(2)}) collective-permute-start(bf16[256,256]{1,0:T(8,128)(2,1)S(1)} %get-tuple-element.69), channel_id=1, source_target_pairs={{0,2},{2,0},{4,6},{6,4},{8,10},{10,8},{12,14},{14,12},{16,18},{18,... | collective-permute-start | bytes 393224 | tf_op jit(solution)/shard_map/ppermute | solution.py:166
  23.8 15.4 %collective-permute-start.10 = (bf16[10,256,128]{2,1,0:T(8,128)(2,1)S(1)}, bf16[10,256,128]{2,1,0:T(8,128)(2,1)S(1)}, u32[]{:S(2)}, u32[]{:S(2)}) collective-permute-start(bf16[10,256,128]{2,1,0:T(8,128)(2,1)S(1)} %slice.123), channel_id=1, source_target_pairs={{0,2},{2,0},{4,6},{6,4},{8,10},{10,8},{12,14},{14,12},{16,18},{18,... | collective-permute-start | bytes 1966088 | tf_op jit(solution)/shard_map/ppermute | solution.py:166
  24.0 15.1 %collective-permute-start.7 = (bf16[2,256,256]{2,1,0:T(8,128)(2,1)S(1)}, bf16[2,256,256]{2,1,0:T(8,128)(2,1)S(1)}, u32[]{:S(2)}, u32[]{:S(2)}) collective-permute-start(bf16[2,256,256]{2,1,0:T(8,128)(2,1)S(1)} %pad_maximum_fusion.4), channel_id=1, source_target_pairs={{0,16},{2,18},{4,20},{6,22},{8,24},{10,26},{12,28},{14,30},{16,0},... | collective-permute-start | bytes 786440 | tf_op jit(solution)/shard_map/ppermute | solution.py:166
  25.4 13.8 %collective-permute-start.6 = (bf16[2,256,256]{2,1,0:T(8,128)(2,1)S(1)}, bf16[2,256,256]{2,1,0:T(8,128)(2,1)S(1)}, u32[]{:S(2)}, u32[]{:S(2)}) collective-permute-start(bf16[2,256,256]{2,1,0:T(8,128)(2,1)S(1)} %pad_maximum_fusion.4), channel_id=1, source_target_pairs={{0,8},{2,10},{4,12},{6,14},{8,0},{10,2},{12,4},{14,6},{16,24},{18,... | collective-permute-start | bytes 786440 | tf_op jit(solution)/shard_map/ppermute | solution.py:166
  39.3 4.2 %collective-permute-start.15 = (bf16[16,256,128]{2,1,0:T(8,128)(2,1)S(1)}, bf16[16,256,128]{2,1,0:T(8,128)(2,1)S(1)}, u32[]{:S(2)}, u32[]{:S(2)}) collective-permute-start(bf16[16,256,128]{2,1,0:T(8,128)(2,1)S(1)} %collective-permute-done.9.refs_4_.refs_6_), channel_id=1, source_target_pairs={{0,2},{2,0},{4,6},{6,4},{8,10},{10,8},{12,14},{14,12},{16,18},{18,... | collective-permute-start | bytes 3145736 | tf_op jit(solution)/shard_map/ppermute | solution.py:166
  39.3 6.4 %collective-permute-start.11 = (bf16[4,256,256]{2,1,0:T(8,128)(2,1)S(1)}, bf16[4,256,256]{2,1,0:T(8,128)(2,1)S(1)}, u32[]{:S(2)}, u32[]{:S(2)}) collective-permute-start(bf16[4,256,256]{2,1,0:T(8,128)(2,1)S(1)} %pad_maximum_fusion.1.refs_0_), channel_id=1, source_target_pairs={{8,16},{10,18},{12,20},{14,22},{16,8},{18,10},{20,12},{22,14},{9,1... | collective-permute-start | bytes 1572872 | tf_op jit(solution)/shard_map/ppermute | solution.py:169
  40.0 16.8 %collective-permute-start.12 = (bf16[4,256,256]{2,1,0:T(8,128)(2,1)S(1)}, bf16[4,256,256]{2,1,0:T(8,128)(2,1)S(1)}, u32[]{:S(2)}, u32[]{:S(2)}) collective-permute-start(bf16[4,256,256]{2,1,0:T(8,128)(2,1)S(1)} %constant_dynamic-update-slice_fusion.2.refs_2_), channel_id=1, source_target_pairs={{8,0},{10,2},{12,4},{14,6},{16,24},{18,26},{20,28},{22,30},{9,1},{... | collective-permute-start | bytes 1572872 | tf_op jit(solution)/shard_map/ppermute | solution.py:172
  41.3 15.5 %collective-permute-start.13 = (bf16[8,256,128]{2,1,0:T(8,128)(2,1)S(1)}, bf16[8,256,128]{2,1,0:T(8,128)(2,1)S(1)}, u32[]{:S(2)}, u32[]{:S(2)}) collective-permute-start(bf16[8,256,128]{2,1,0:T(8,128)(2,1)S(1)} %slice.125), channel_id=1, source_target_pairs={{0,1},{1,0},{2,3},{3,2},{4,5},{5,4},{6,7},{7,6},{8,9},{9,8},{10,11... | collective-permute-start | bytes 1572872 | tf_op jit(solution)/shard_map/ppermute | solution.py:175
  42.9 14.0 %collective-permute-start.14 = (bf16[8,256,128]{2,1,0:T(8,128)(2,1)S(1)}, bf16[8,256,128]{2,1,0:T(8,128)(2,1)S(1)}, u32[]{:S(2)}, u32[]{:S(2)}) collective-permute-start(bf16[8,256,128]{2,1,0:T(8,128)(2,1)S(1)} %slice.126), channel_id=1, source_target_pairs={{0,4},{2,6},{4,0},{6,2},{8,12},{10,14},{12,8},{14,10},{16,20},{18,... | collective-permute-start | bytes 1572872 | tf_op jit(solution)/shard_map/ppermute | solution.py:166
  43.4 15.5 %collective-permute-start.17 = (bf16[16,256,128]{2,1,0:T(8,128)(2,1)S(1)}, bf16[16,256,128]{2,1,0:T(8,128)(2,1)S(1)}, u32[]{:S(2)}, u32[]{:S(2)}) collective-permute-start(bf16[16,256,128]{2,1,0:T(8,128)(2,1)S(1)} %collective-permute-done.8.refs_5_), channel_id=1, source_target_pairs={{0,2},{2,0},{4,6},{6,4},{8,10},{10,8},{12,14},{14,12},{16,18},{18,... | collective-permute-start | bytes 3145736 | tf_op jit(solution)/shard_map/ppermute | solution.py:166
  43.4 0.7 copy-start
  56.9 2.0 %collective-permute-start.18 = (bf16[8,256,128]{2,1,0:T(8,128)(2,1)S(1)}, bf16[8,256,128]{2,1,0:T(8,128)(2,1)S(1)}, u32[]{:S(2)}, u32[]{:S(2)}) collective-permute-start(bf16[8,256,128]{2,1,0:T(8,128)(2,1)S(1)} %collective-permute-done.13.refs_6_), channel_id=1, source_target_pairs={{0,2},{2,0},{4,6},{6,4},{8,10},{10,8},{12,14},{14,12},{16,18},{18,... | collective-permute-start | bytes 1572872 | tf_op jit(solution)/shard_map/ppermute | solution.py:166
  56.9 2.7 %collective-permute-start.19 = (bf16[8,256,128]{2,1,0:T(8,128)(2,1)S(1)}, bf16[8,256,128]{2,1,0:T(8,128)(2,1)S(1)}, u32[]{:S(2)}, u32[]{:S(2)}) collective-permute-start(bf16[8,256,128]{2,1,0:T(8,128)(2,1)S(1)} %collective-permute-done.14.refs_9_), channel_id=1, source_target_pairs={{0,2},{2,0},{4,6},{6,4},{8,10},{10,8},{12,14},{14,12},{16,18},{18,... | collective-permute-start | bytes 1572872 | tf_op jit(solution)/shard_map/ppermute | solution.py:166
  58.8 10.2 %collective-permute-start.16 = (bf16[256,256]{1,0:T(8,128)(2,1)S(1)}, bf16[256,256]{1,0:T(8,128)(2,1)S(1)}, u32[]{:S(2)}, u32[]{:S(2)}) collective-permute-start(bf16[256,256]{1,0:T(8,128)(2,1)S(1)} %get-tuple-element.64), channel_id=1, source_target_pairs={{0,2},{2,0},{4,6},{6,4},{8,10},{10,8},{12,14},{14,12},{16,18},{18,... | collective-permute-start | bytes 393224 | tf_op jit(solution)/shard_map/ppermute | solution.py:166
  61.9 7.0 %collective-permute-start.22 = (f16[272,256]{1,0:T(8,128)(2,1)S(1)}, f16[272,256]{1,0:T(8,128)(2,1)S(1)}, u32[]{:S(2)}, u32[]{:S(2)}) collective-permute-start(f16[272,256]{1,0:T(8,128)(2,1)S(1)} %convert_element_type.41), channel_id=1, source_target_pairs={{0,8},{2,10},{4,12},{6,14},{8,0},{10,2},{12,4},{14,6},{16,24},{18,... | collective-permute-start | bytes 417800 | tf_op jit(solution)/shard_map/ppermute | solution.py:166
  65.0 5.8 %collective-permute-start.21 = (bf16[256,256]{1,0:T(8,128)(2,1)S(1)}, bf16[256,256]{1,0:T(8,128)(2,1)S(1)}, u32[]{:S(2)}, u32[]{:S(2)}) collective-permute-start(bf16[256,256]{1,0:T(8,128)(2,1)S(1)} %get-tuple-element.62), channel_id=1, source_target_pairs={{0,6},{2,4},{4,2},{6,0},{8,14},{10,12},{12,10},{14,8},{16,22},{18,... | collective-permute-start | bytes 393224 | tf_op jit(solution)/shard_map/ppermute | solution.py:166
  70.8 9.0 %collective-permute-start.23 = (f16[272,256]{1,0:T(8,128)(2,1)S(1)}, f16[272,256]{1,0:T(8,128)(2,1)S(1)}, u32[]{:S(2)}, u32[]{:S(2)}) collective-permute-start(f16[272,256]{1,0:T(8,128)(2,1)S(1)} %pad_maximum_fusion.5), channel_id=1, source_target_pairs={{0,16},{2,18},{4,20},{6,22},{8,24},{10,26},{12,28},{14,30},{16,0},... | collective-permute-start | bytes 417800 | tf_op jit(solution)/shard_map/ppermute | solution.py:166
  71.5 8.4 %collective-permute-start.20 = (bf16[256,256]{1,0:T(8,128)(2,1)S(1)}, bf16[256,256]{1,0:T(8,128)(2,1)S(1)}, u32[]{:S(2)}, u32[]{:S(2)}) collective-permute-start(bf16[256,256]{1,0:T(8,128)(2,1)S(1)} %get-tuple-element.63), channel_id=1, source_target_pairs={{0,4},{2,6},{4,0},{6,2},{8,12},{10,14},{12,8},{14,10},{16,20},{18,... | collective-permute-start | bytes 393224 | tf_op jit(solution)/shard_map/ppermute | solution.py:166
  80.0 5.7 %collective-permute-start.24 = (f16[272,256]{1,0:T(8,128)(2,1)S(1)}, f16[272,256]{1,0:T(8,128)(2,1)S(1)}, u32[]{:S(2)}, u32[]{:S(2)}) collective-permute-start(f16[272,256]{1,0:T(8,128)(2,1)S(1)} %pad_maximum_fusion.6), channel_id=1, source_target_pairs={{0,4},{2,6},{4,0},{6,2},{8,12},{10,14},{12,8},{14,10},{16,20},{18,... | collective-permute-start | bytes 417800 | tf_op jit(solution)/shard_map/ppermute | solution.py:166
  81.9 5.7 %copy-start.1 = (f32[4,256,256]{2,1,0:T(8,128)S(1)}, f32[4,256,256]{2,1,0:T(8,128)}, u32[]{:S(2)}) copy-start(f32[4,256,256]{2,1,0:T(8,128)} %param.7) | copy-start | bytes 3145732
  85.8 1.6 %collective-permute-start.25 = (f16[2,272,256]{2,1,0:T(8,128)(2,1)S(1)}, f16[2,272,256]{2,1,0:T(8,128)(2,1)S(1)}, u32[]{:S(2)}, u32[]{:S(2)}) collective-permute-start(f16[2,272,256]{2,1,0:T(8,128)(2,1)S(1)} %pad_maximum_fusion.2), channel_id=1, source_target_pairs={{0,2},{2,0},{4,6},{6,4},{8,10},{10,8},{12,14},{14,12},{16,18},{18,... | collective-permute-start | bytes 835592 | tf_op jit(solution)/shard_map/ppermute | solution.py:166

commit v4 on v3

--- a/solution.py
+++ b/solution.py
@@ -67,52 +67,78 @@
     return found
 
 
-def product_kernel(slots, n_level, groups, begins, ends, packs, place, lists, *refs):
+def product_kernel(groups, n_level, ends, packs, *refs):
+    if ends:
+        place, refs = refs[0], refs[1:]
+    else:
+        place, lists, refs = refs[0], refs[1], refs[2:]
     level, refs = refs[:n_level], refs[n_level:]
-    sides, refs = refs[: 2 * len(groups)], refs[2 * len(groups) :]
-    n_extra = 1 if groups[0] >= 2 else 0
-    highs, refs = refs[: n_extra * len(groups)], refs[n_extra * len(groups) :]
-    if not begins:
-        sums_ref, refs = refs[0], refs[1:]
-    if packs:
-        before_ref, refs = refs[0], refs[1:]
+    sides = []
+    for _, _, n_arrays, _ in groups:
+        sides.append(refs[:n_arrays])
+        refs = refs[n_arrays:]
     col, row = place[0], place[1]
     width = level[0].shape[1]
     half = width // 2
-    sup = row * GROUP + col % GROUP
     near = pl.ds(pl.multiple_of(row * half, half), half)
     far = pl.ds(pl.multiple_of((1 - row) * half, half), half)
-    totals = [None if begins else sums_ref[g] for g in range(len(groups))]
-    for slot in slots:
-        z, i = slot // GROUP, slot % GROUP
-        block = col ^ slot
-        parts = [level[z][i, rows, :] for rows in (near, far)]
-        if z == 3:
-            parts = [part + level[4][i, rows, :] for part, rows in zip(parts, (near, far))]
-        m = jnp.concatenate(parts, axis=0)
-        m = jnp.where(is_member(lists, sup, block), m, jnp.zeros_like(m))
-        for g in range(len(groups)):
-            a_near = sides[2 * g][block]
-            if n_extra:
-                low, high = sides[2 * g + 1], highs[g]
-                n_low = low.shape[0]
-                in_low = block < n_low
-                a_far = jnp.where(
-                    in_low, low[jnp.minimum(block, n_low - 1)], high[jnp.maximum(block - n_low, 0)]
-                )
-            else:
-                a_far = sides[2 * g + 1][block]
-            a = jnp.concatenate([a_near, a_far], axis=1)
-            term = jnp.dot(a, m, preferred_element_type=jnp.float32)
+    totals = [None] * len(groups)
+    if any(begun for *_, begun in groups):
+        sums_ref, refs = refs[0], refs[1:]
+        for g, (*_, begun) in enumerate(groups):
+            totals[g] = sums_ref[g] if begun else None
+    if packs:
+        before_ref, refs = refs[0], refs[1:]
+
+    sup = row * GROUP + col % GROUP
+
+    def is_kept(block):
+        return place[2 + block] != 0 if ends else is_member(lists, sup, block)
+
+    def inverse_rows(g, block):
+        near_ref, low, *high = sides[g]
+        if not high:
+            return near_ref[block], low[block]
+        n_low = low.shape[0]
+        from_high = high[0][jnp.maximum(block - n_low, 0)]
+        return near_ref[block], jnp.where(
+            block < n_low, low[jnp.minimum(block, n_low - 1)], from_high
+        )
+
+    for z in sorted({z for _, steps, *_ in groups for z in steps}):
+        blocks = [col ^ (z * GROUP + i) for i in range(GROUP)]
+        m = []
+        for i, block in enumerate(blocks):
+            parts = [level[z][i, rows, :] for rows in (near, far)]
+            if z == 3:
+                parts = [part + level[4][i, rows, :] for part, rows in zip(parts, (near, far))]
+            kept = is_kept(block)
+            m += [jnp.where(kept, part, jnp.zeros_like(part)) for part in parts]
+        here = [g for g, (_, steps, *_) in enumerate(groups) if z in steps]
+        rows = [
+            jnp.concatenate([v for block in blocks for v in inverse_rows(g, block)], axis=1)
+            for g in here
+        ]
+        terms = jnp.dot(
+            jnp.concatenate(rows, axis=0),
+            jnp.concatenate(m, axis=0),
+            preferred_element_type=jnp.float32,
+        )
+        for i, g in enumerate(here):
+            term = terms[i * width : (i + 1) * width]
             totals[g] = term if totals[g] is None else totals[g] + term
     if not ends:
-        for g in range(len(groups)):
-            refs[0][g] = totals[g]
+        sums_out, place_out = refs
+        for g, total in enumerate(totals):
+            sums_out[g] = total
+        place_out[0], place_out[1] = col, row
+        for block in range(place_out.shape[0] - 2):
+            place_out[2 + block] = is_kept(block).astype(jnp.int32)
         return
     sel_ref, diag_ref = refs
     diag = before_ref[...] if packs else None
-    for g, group in enumerate(groups):
-        kept = is_member(lists, sup, col ^ group)
+    for g, (group, *_) in enumerate(groups):
+        kept = is_kept(col ^ group)
         sel = jnp.where(kept, -totals[g], jnp.zeros_like(totals[g])).astype(jnp.bfloat16)
         sel_ref[g] = sel
         term = lax.dot_general(
@@ -185,10 +211,9 @@
     pair_rows = choose(own_rows, first_pair)
     part_a = jnp.stack([choose(pair_rows, first_core), swap(choose(pair_rows, ~first_core), 1)])
     inverse = anc_inverse.reshape(rows, half_w, all_blocks).transpose(2, 0, 1)
-    two_a = swap(after(part_a, inverse), 8)
-    part_b = jnp.stack([choose(from_pair, first_core), swap(choose(from_pair, ~first_core), 1)])
-
-    one_a = swap(after(part_a, inverse), 4)
+    two_a, one_a = swap(after(part_a, inverse), 8), swap(after(part_a, inverse), 4)
+    give_b = choose(from_pair, ~first_core)
+    part_b = jnp.stack([choose(from_pair, first_core), swap(give_b, 1)])
     x_all, y_all = across(inverse), swap(after(inverse, from_pair), 2)
     own = jnp.concatenate([part_a, part_b])
     n_first = 6 * all_blocks // 16
@@ -197,53 +222,52 @@
     two_b, one_b, c_rest = swap(first[0], 8), swap(first[0], 4), swap(first[1], 1)
     c_own = jnp.concatenate([c_first, c_rest])
     two, one = jnp.concatenate([two_a, two_b]), jnp.concatenate([one_a, one_b])
-
-    n_low = all_blocks // 2
+    n_low = 9 * all_blocks // 16
     second = together((two, own, y_all[:n_low], x_all[n_low:], x_all, y_all), one, c_rest)
     out, three = outward(second[0]), middle(second[1])
     xy_low, xy_high = across(second[2]), swap(second[3], 2)
     c_x, c_y = swap(second[4], 1), swap(second[5], 1)
 
-    def product(slots, groups, level, sides, highs=(), sums=None, before=None, ends=True):
-        extra = [v for v in (sums, before) if v is not None]
+    def product(scalars, level, groups, sums=None, before=None, ends=True):
         packs = before is not None
-        sel = jax.ShapeDtypeStruct((2, width, width), bf16)
-        total = jax.ShapeDtypeStruct((2, width, width), f32)
+        what = tuple((g, tuple(steps), len(v), sums is not None and g < 2) for g, steps, v in groups)
+        arrays = [*level, *(v for _, _, arrays in groups for v in arrays)]
+        arrays += [v for v in (sums, before) if v is not None]
+        sel = jax.ShapeDtypeStruct((len(groups), width, width), bf16)
+        total = jax.ShapeDtypeStruct((len(groups), width, width), f32)
         diag = jax.ShapeDtypeStruct((width + 16 if packs else width, width), f32)
-        arrays = [*level, *sides, *highs, *extra]
         return pl.pallas_call(
-            functools.partial(
-                product_kernel, slots, len(level), groups, sums is None, ends, packs
-            ),
-            out_shape=(sel, diag) if ends else total,
-            in_specs=[SMEM, SMEM] + [VMEM] * len(arrays),
-            out_specs=(VMEM, VMEM) if ends else VMEM,
+            functools.partial(product_kernel, what, len(level), ends, packs),
+            out_shape=(sel, diag) if ends else (total, jax.ShapeDtypeStruct((2 + all_blocks,), jnp.int32)),
+            in_specs=[SMEM] * len(scalars) + [VMEM] * len(arrays),
+            out_specs=(VMEM, VMEM) if ends else (VMEM, SMEM),
             compiler_params=PARAMS,
-        )(place, structure, *arrays)
-
-    near = [inverse, x_all, c_own, c_x]
-    sums = product(range(12), (0, 1), [own, one, two], near, ends=False)
-    last = together((three, out, xy_low, xy_high), sums)
-    cxy_low, cxy_high = swap(last[2], 1), swap(last[3], 1)
+        )(*scalars, *arrays)
+
+    early, late, steps = (0, 1, 2), (3,), (0, 1, 2, 3)
+    rows_0, rows_1 = (inverse, x_all), (c_own, c_x)
+    first_groups = [(0, early, rows_0), (1, early, rows_1)]
+    sums, kept = product((place, structure), [own, one, two], first_groups, ends=False)
+    last = together((three, out, xy_high, xy_low), sums)
+    cxy_low, cxy_high = swap(last[3], 1), swap(last[2], 1)
     level = [own, one, two, last[0], last[1]]
-    sel_near, diag = product(range(12, 16), (0, 1), level, near, sums=sums)
-    s_core = swap(sel_near[1], 1)
-    sel_far, diag = product(
-        range(16), (2, 3), level, [y_all, xy_low, c_y, cxy_low], [xy_high, cxy_high], before=diag
-    )
-    s_pair, s_cross = swap(sel_far[0], 2), swap(sel_far[1], 3)
+    groups = [(0, late, rows_0), (1, late, rows_1), (2, steps, (y_all, last[3], last[2]))]
+    sel, diag = product((kept,), level, groups, sums=sums)
+    s_core, s_pair = swap(sel[1], 1), swap(sel[2], 2)
+    sel_cross, diag = product((kept,), level, [(3, steps, (c_y, cxy_low, cxy_high))], before=diag)
+    s_cross = swap(sel_cross[0], 3)
 
     packed = diag.astype(jnp.float16)
     packed = add_packed(packed, swap(packed, 4))
-    packed = add_packed(packed, swap(after(packed, s_core, s_cross), 8))
+    packed = add_packed(packed, swap(after(packed, s_core, s_pair), 8))
     selected = pl.pallas_call(
         merge_kernel,
         out_shape=jax.ShapeDtypeStruct((width, GROUP * width), bf16),
         in_specs=[SMEM, VMEM, VMEM, VMEM, VMEM],
         out_specs=VMEM,
         compiler_params=PARAMS,
-    )(place, sel_near[0], s_core, s_pair, s_cross)
-    got = swap(after(packed, s_pair), 2)
+    )(place, sel[0], s_core, s_pair, s_cross)
+    got = swap(after(packed, s_cross), 2)
     mine = jnp.stack([jnp.where(first_pair, packed, got), jnp.where(first_pair, got, packed)])
     other = swap(after(mine, selected), 1)
     ordered = [jnp.where(first_core, mine, other), jnp.where(first_core, other, mine)]

time: 89.1 us -> 86 us (0.965)
  waiting for transfers between devices: 51 us -> 48.2 us
  starting transfers between devices: 24.4 us -> 23.4 us
    ppermute x1, waiting for transfers between devices: 11.1 us -> 2.5 us  [outward(): lax.ppermute(x, 'col', [(c, c ^ 4) for c in range(n_col) if c // 4 in (1,...]
    ppermute x22, waiting for transfers between devices: 32.4 us -> 38.2 us  [swap(): return lax.ppermute(x, 'col', [(c, c ^ flip) for c in range(n_col)])]
    ppermute x22, starting transfers between devices: 19.4 us -> 18.4 us  [swap(): return lax.ppermute(x, 'col', [(c, c ^ flip) for c in range(n_col)])]
  transfers between devices with their start and end apart: 26 -> 26, of which waited for: 13 -> 12; matrix products, arithmetic and copies ran while one was open for 3% -> 3% of each run, Pallas kernels for 8% -> 7%
where the time goes in v4:
time: 86 us; the launch traced here: 85.8 us
  waiting for transfers between devices  48.2 us (56%)
  starting transfers between devices  23.4 us (27%)
  Pallas kernels  7.42 us (9%)
  local copies, waits for them, and re-layouts  3.52 us (4%)
  other arithmetic  2.21 us (3%)
  between operations  1.04 us (1%)
    ppermute x22, waiting for transfers between devices, swap(): return lax.ppermute(x, 'col', [(c, c ^ flip) for c in range(n_col)])  38.2 us
    ppermute x22, starting transfers between devices, swap(): return lax.ppermute(x, 'col', [(c, c ^ flip) for c in range(n_col)])  18.4 us
    ppermute x2, waiting for transfers between devices, across(): return lax.ppermute(x, 'row', [(0, 1), (1, 0)])  7.54 us
    pallas_call x3, Pallas kernels, product(): pl.pallas_call(functools.partial(product_kernel, what, len(level), ends,...  6.02 us
    ppermute x2, starting transfers between devices, across(): return lax.ppermute(x, 'row', [(0, 1), (1, 0)])  3.05 us
    ppermute x1, waiting for transfers between devices, outward(): lax.ppermute(x, 'col', [(c, c ^ 4) for c in range(n_col) if c // 4 in (1,...  2.5 us
  transfers between devices with their start and end apart: 26, of which 12 were waited for; matrix products, arithmetic and copies ran while one was open for 3% of the time, Pallas kernels for 7%

profile of v4, /device:TPU:0, one launch (start us, length us, event | category | flops | bytes accessed | tf_op | source)
XLA Modules:
  0.0 85.8 jit_solution(14336571905206896330)
XLA Ops:
  0.7 0.1 pad_add_fusion.refs_0_.place
  0.8 1.1 %broadcast_select_fusion.3 = (bf16[256,512]{1,0:T(8,128)(2,1)S(1)}, bf16[256,512]{1,0:T(8,128)(2,1)S(1)}) fusion(pred[]{:T(512)S(6)} %eq.10, bf16[256,1024]{1,0:T(8,128)(2,1)} %bitcast.68, pred[]{:T(512)S(6)} %not.8), kind=kLoop, calls=%fused_computation.16 | loop fusion | flops 262144 | bytes 1048578 | tf_op jit(solution)/shard_map/jit(_where)/select_n | solution.py:207
  1.9 0.5 collective-permute-start
  2.4 2.6 %collective-permute-start.1 = (bf16[256,512]{1,0:T(8,128)(2,1)S(1)}, bf16[256,512]{1,0:T(8,128)(2,1)S(1)}, u32[]{:S(2)}, u32[]{:S(2)}) collective-permute-start(bf16[256,512]{1,0:T(8,128)(2,1)S(1)} %get-tuple-element.63), channel_id=1, source_target_pairs={{0,4},{2,6},{4,0},{6,2},{8,12},{10,14},{12,8},{14,10},{16,20},{18,... | collective-permute-start | bytes 786440 | tf_op jit(solution)/shard_map/ppermute | solution.py:192
  5.0 0.5 copy.6
  5.6 1.0 %copy.7 = bf16[256,128,16]{1,0,2:T(8,128)(2,1)S(1)} copy(bf16[256,128,16]{0,2,1:T(8,128)(2,1)S(1)} %bitcast.65) | data formatting | bytes 2097152 | tf_op jit(solution)/shard_map/reshape | solution.py:213
  6.6 2.7 %collective-permute-start.4 = (bf16[2,256,256]{2,1,0:T(8,128)(2,1)S(1)}, bf16[2,256,256]{2,1,0:T(8,128)(2,1)S(1)}, u32[]{:S(2)}, u32[]{:S(2)}) collective-permute-start(bf16[2,256,256]{2,1,0:T(8,128)(2,1)S(1)} %pad_maximum_fusion.3), channel_id=1, source_target_pairs={{0,16},{2,18},{4,20},{6,22},{8,24},{10,26},{12,28},{14,30},{16,0},... | collective-permute-start | bytes 786440 | tf_op jit(solution)/shard_map/ppermute | solution.py:192
  9.3 1.6 %collective-permute-start.3 = (bf16[2,256,256]{2,1,0:T(8,128)(2,1)S(1)}, bf16[2,256,256]{2,1,0:T(8,128)(2,1)S(1)}, u32[]{:S(2)}, u32[]{:S(2)}) collective-permute-start(bf16[2,256,256]{2,1,0:T(8,128)(2,1)S(1)} %pad_maximum_fusion.3), channel_id=1, source_target_pairs={{0,8},{2,10},{4,12},{6,14},{8,0},{10,2},{12,4},{14,6},{16,24},{18,... | collective-permute-start | bytes 786440 | tf_op jit(solution)/shard_map/ppermute | solution.py:192
  10.8 1.5 %collective-permute-start.8 = (bf16[16,256,128]{2,1,0:T(8,128)(2,1)S(1)}, bf16[16,256,128]{2,1,0:T(8,128)(2,1)S(1)}, u32[]{:S(2)}, u32[]{:S(2)}) collective-permute-start(bf16[16,256,128]{2,1,0:T(8,128)(2,1)S(1)} %bitcast.58), channel_id=1, source_target_pairs={{0,1},{1,0},{2,3},{3,2},{4,5},{5,4},{6,7},{7,6},{8,9},{9,8},{10,11... | collective-permute-start | bytes 3145736 | tf_op jit(solution)/shard_map/ppermute | solution.py:201
  12.4 1.3 %collective-permute-start.10 = (bf16[16,256,128]{2,1,0:T(8,128)(2,1)S(1)}, bf16[16,256,128]{2,1,0:T(8,128)(2,1)S(1)}, u32[]{:S(2)}, u32[]{:S(2)}) collective-permute-start(bf16[16,256,128]{2,1,0:T(8,128)(2,1)S(1)} %bitcast.60), channel_id=1, source_target_pairs={{0,4},{2,6},{4,0},{6,2},{8,12},{10,14},{12,8},{14,10},{16,20},{18,... | collective-permute-start | bytes 3145736 | tf_op jit(solution)/shard_map/ppermute | solution.py:192
  13.7 8.0 %collective-permute-done.4 = bf16[2,256,256]{2,1,0:T(8,128)(2,1)S(1)} collective-permute-done((bf16[2,256,256]{2,1,0:T(8,128)(2,1)S(1)}, bf16[2,256,256]{2,1,0:T(8,128)(2,1)S(1)}, u32[]{:S(2)}, u32[]{:S(2)}) %collective-permute-start.4) | collective-permute-done | bytes 262176 | tf_op jit(solution)/shard_map/ppermute | solution.py:192
  21.7 0.2 collective-permute-done.3
  21.9 0.6 collective-permute-start.2
  22.5 1.3 %collective-permute-done.2 = bf16[256,256]{1,0:T(8,128)(2,1)S(1)} collective-permute-done((bf16[256,256]{1,0:T(8,128)(2,1)S(1)}, bf16[256,256]{1,0:T(8,128)(2,1)S(1)}, u32[]{:S(2)}, u32[]{:S(2)}) %collective-permute-start.2) | collective-permute-done | bytes 131104 | tf_op jit(solution)/shard_map/ppermute | solution.py:192
  23.8 0.2 collective-permute-start.9
  24.0 1.3 %collective-permute-start.7 = (bf16[2,256,256]{2,1,0:T(8,128)(2,1)S(1)}, bf16[2,256,256]{2,1,0:T(8,128)(2,1)S(1)}, u32[]{:S(2)}, u32[]{:S(2)}) collective-permute-start(bf16[2,256,256]{2,1,0:T(8,128)(2,1)S(1)} %pad_maximum_fusion.4), channel_id=1, source_target_pairs={{0,16},{2,18},{4,20},{6,22},{8,24},{10,26},{12,28},{14,30},{16,0},... | collective-permute-start | bytes 786440 | tf_op jit(solution)/shard_map/ppermute | solution.py:192
  25.4 2.5 %collective-permute-start.6 = (bf16[2,256,256]{2,1,0:T(8,128)(2,1)S(1)}, bf16[2,256,256]{2,1,0:T(8,128)(2,1)S(1)}, u32[]{:S(2)}, u32[]{:S(2)}) collective-permute-start(bf16[2,256,256]{2,1,0:T(8,128)(2,1)S(1)} %pad_maximum_fusion.4), channel_id=1, source_target_pairs={{0,8},{2,10},{4,12},{6,14},{8,0},{10,2},{12,4},{14,6},{16,24},{18,... | collective-permute-start | bytes 786440 | tf_op jit(solution)/shard_map/ppermute | solution.py:192
  27.9 0.1 pad_maximum_fusion.1.refs_2_.refs_1_
  28.0 7.5 %collective-permute-done.8.refs_6_.refs_7_ = bf16[16,256,128]{2,1,0:T(8,128)(2,1)S(1)} collective-permute-done((bf16[16,256,128]{2,1,0:T(8,128)(2,1)S(1)}, bf16[16,256,128]{2,1,0:T(8,128)(2,1)S(1)}, u32[]{:S(2)}, u32[]{:S(2)}) %collective-permute-start.8) | collective-permute-done | bytes 1048608 | tf_op jit(solution)/shard_map/ppermute | solution.py:201
  35.5 3.6 %collective-permute-done.7 = bf16[2,256,256]{2,1,0:T(8,128)(2,1)S(1)} collective-permute-done((bf16[2,256,256]{2,1,0:T(8,128)(2,1)S(1)}, bf16[2,256,256]{2,1,0:T(8,128)(2,1)S(1)}, u32[]{:S(2)}, u32[]{:S(2)}) %collective-permute-start.7) | collective-permute-done | bytes 262176 | tf_op jit(solution)/shard_map/ppermute | solution.py:192
  39.2 0.0 collective-permute-done.6
  39.2 0.0 collective-permute-done.10.refs_10_
  39.2 0.0 collective-permute-done.9
  39.3 0.1 collective-permute-start.11
  39.3 1.6 %collective-permute-start.15 = (bf16[9,256,128]{2,1,0:T(8,128)(2,1)S(1)}, bf16[9,256,128]{2,1,0:T(8,128)(2,1)S(1)}, u32[]{:S(2)}, u32[]{:S(2)}) collective-permute-start(bf16[9,256,128]{2,1,0:T(8,128)(2,1)S(1)} %slice.121), channel_id=1, source_target_pairs={{0,1},{1,0},{2,3},{3,2},{4,5},{5,4},{6,7},{7,6},{8,9},{9,8},{10,11... | collective-permute-start | bytes 1769480 | tf_op jit(solution)/shard_map/ppermute | solution.py:201
  40.9 0.7 collective-permute-start.12
  41.6 1.3 %collective-permute-start.13 = (bf16[4,256,256]{2,1,0:T(8,128)(2,1)S(1)}, bf16[4,256,256]{2,1,0:T(8,128)(2,1)S(1)}, u32[]{:S(2)}, u32[]{:S(2)}) collective-permute-start(bf16[4,256,256]{2,1,0:T(8,128)(2,1)S(1)} %constant_dynamic-update-slice_fusion.2.refs_4_.refs_3_), channel_id=1, source_target_pairs={{8,0},{10,2},{12,4},{14,6},{16,24},{18,26},{20,28},{22,30},{9,1},{... | collective-permute-start | bytes 1572872 | tf_op jit(solution)/shard_map/ppermute | solution.py:198
  42.9 0.6 collective-permute-start.14
  43.5 0.0 copy-start
  43.5 0.1 constant_dynamic-update-slice_fusion.4.refs_7_.refs_8_
  43.6 0.6 copy-done
  44.2 2.3 %shard_map.59 = (f32[2,256,256]{2,1,0:T(8,128)S(1)}, s32[18]{0:T(128)S(1)}) custom-call(s32[2]{0:T(128)S(1)} %pad_add_fusion.refs_0_.place, s32[8,12]{1,0:T(8,128)S(1)} %copy-done, bf16[4,256,256]{2,1,0:T(8,128)(2,1)S(1)} %pad_maximum_fusion.1.refs_2_.refs_1_, bf16[4,256,256]{2,1,0:T(8,128)(2,1)S(1)} %constant_dynamic-update-slice_fusion.refs_3_.refs_2_, ...), custom_call_target="tpu_custom_call" | custom-call | tf_op jit(solution)/shard_map/pallas_call | solution.py:239
  46.5 9.1 %collective-permute-done.14.refs_12_ = bf16[7,256,128]{2,1,0:T(8,128)(2,1)S(1)} collective-permute-done((bf16[7,256,128]{2,1,0:T(8,128)(2,1)S(1)}, bf16[7,256,128]{2,1,0:T(8,128)(2,1)S(1)}, u32[]{:S(2)}, u32[]{:S(2)}) %collective-permute-start.14) | collective-permute-done | bytes 458784 | tf_op jit(solution)/shard_map/ppermute | solution.py:192
  55.5 0.0 collective-permute-done.12.refs_4_
  55.5 2.5 %collective-permute-done.13.refs_5_ = bf16[4,256,256]{2,1,0:T(8,128)(2,1)S(1)} collective-permute-done((bf16[4,256,256]{2,1,0:T(8,128)(2,1)S(1)}, bf16[4,256,256]{2,1,0:T(8,128)(2,1)S(1)}, u32[]{:S(2)}, u32[]{:S(2)}) %collective-permute-start.13) | collective-permute-done | bytes 524320 | tf_op jit(solution)/shard_map/ppermute | solution.py:198
  58.0 0.0 collective-permute-done.15.refs_11_
  58.0 0.0 collective-permute-start.19
  58.1 0.5 collective-permute-start.20
  58.6 2.1 %shard_map.60 = (bf16[3,256,256]{2,1,0:T(8,128)(2,1)S(1)}, f32[256,256]{1,0:T(8,128)S(1)}) custom-call(s32[18]{0:T(128)S(1)} %get-tuple-element.36.refs_0_, bf16[4,256,256]{2,1,0:T(8,128)(2,1)S(1)} %pad_maximum_fusion.1.refs_2_.refs_1_, bf16[4,256,256]{2,1,0:T(8,128)(2,1)S(1)} %constant_dynamic-update-slice_fusion.refs_3_.refs_2_, ...), custom_call_target="tpu_custom_call" | custom-call | tf_op jit(solution)/shard_map/pallas_call | solution.py:239
  60.6 0.0 collective-permute-done.18.refs_6_
  60.6 0.1 collective-permute-done.20.refs_8_
  60.7 0.0 collective-permute-done.19.refs_7_
  60.7 1.7 %shard_map.61 = (bf16[1,256,256]{2,1,0:T(8,128)(2,1)S(1)}, f32[272,256]{1,0:T(8,128)S(1)}) custom-call(s32[18]{0:T(128)S(1)} %get-tuple-element.36.refs_0_, bf16[4,256,256]{2,1,0:T(8,128)(2,1)S(1)} %pad_maximum_fusion.1.refs_2_.refs_1_, bf16[4,256,256]{2,1,0:T(8,128)(2,1)S(1)} %constant_dynamic-update-slice_fusion.refs_3_.refs_2_, ...), custom_call_target="tpu_custom_call" | custom-call | tf_op jit(solution)/shard_map/pallas_call | solution.py:239
  62.4 0.6 collective-permute-start.22
  63.1 0.6 collective-permute-start.17
  63.6 0.0 collective-permute-start.16
  63.6 4.6 %collective-permute-done.22 = f16[272,256]{1,0:T(8,128)(2,1)S(1)} collective-permute-done((f16[272,256]{1,0:T(8,128)(2,1)S(1)}, f16[272,256]{1,0:T(8,128)(2,1)S(1)}, u32[]{:S(2)}, u32[]{:S(2)}) %collective-permute-start.22) | collective-permute-done | bytes 139296 | tf_op jit(solution)/shard_map/ppermute | solution.py:192
  68.2 0.1 multiply_convert_fusion.1
  68.4 0.0 collective-permute-done.17.pair_ref
  68.4 0.0 collective-permute-done.16.core_ref
  68.4 2.1 %collective-permute-start.23 = (f16[272,256]{1,0:T(8,128)(2,1)S(1)}, f16[272,256]{1,0:T(8,128)(2,1)S(1)}, u32[]{:S(2)}, u32[]{:S(2)}) collective-permute-start(f16[272,256]{1,0:T(8,128)(2,1)S(1)} %pad_maximum_fusion.5), channel_id=1, source_target_pairs={{0,16},{2,18},{4,20},{6,22},{8,24},{10,26},{12,28},{14,30},{16,0},... | collective-permute-start | bytes 417800 | tf_op jit(solution)/shard_map/ppermute | solution.py:192
  70.5 6.7 %collective-permute-done.23 = f16[272,256]{1,0:T(8,128)(2,1)S(1)} collective-permute-done((f16[272,256]{1,0:T(8,128)(2,1)S(1)}, f16[272,256]{1,0:T(8,128)(2,1)S(1)}, u32[]{:S(2)}, u32[]{:S(2)}) %collective-permute-start.23) | collective-permute-done | bytes 139296 | tf_op jit(solution)/shard_map/ppermute | solution.py:192
  77.2 0.1 multiply_convert_fusion
  77.4 0.6 collective-permute-start.24
  78.0 1.4 %shard_map.62 = bf16[256,1024]{1,0:T(8,128)(2,1)} custom-call(s32[2]{0:T(128)S(1)} %pad_add_fusion.refs_0_.place, bf16[256,256]{1,0:T(8,128)(2,1)S(1)} %get-tuple-element.66.own_ref, bf16[256,256]{1,0:T(8,128)(2,1)S(1)} %collective-permute-done.16.core_ref, bf16[256,256]{1,0:T(8,128)(2,1)S(1)} %collective-permute-done.17.pair_ref, ...), custom_call_target="tpu_custom_call" | custom-call | tf_op jit(solution)/shard_map/pallas_call | solution.py:263
  79.4 3.1 %collective-permute-done.24 = f16[272,256]{1,0:T(8,128)(2,1)S(1)} collective-permute-done((f16[272,256]{1,0:T(8,128)(2,1)S(1)}, f16[272,256]{1,0:T(8,128)(2,1)S(1)}, u32[]{:S(2)}, u32[]{:S(2)}) %collective-permute-start.24) | collective-permute-done | bytes 139296 | tf_op jit(solution)/shard_map/ppermute | solution.py:192
  82.5 0.1 select_bitcast_fusion.1
  82.6 0.1 pad_maximum_fusion.2
  82.7 0.1 collective-permute-start.25
  82.8 1.5 %collective-permute-done.25 = f16[2,272,256]{2,1,0:T(8,128)(2,1)S(1)} collective-permute-done((f16[2,272,256]{2,1,0:T(8,128)(2,1)S(1)}, f16[2,272,256]{2,1,0:T(8,128)(2,1)S(1)}, u32[]{:S(2)}, u32[]{:S(2)}) %collective-permute-start.25) | collective-permute-done | bytes 278560 | tf_op jit(solution)/shard_map/ppermute | solution.py:192
  84.3 0.2 broadcast_select_fusion.1
  84.5 0.1 fusion.3
  84.7 0.1 pad_maximum_fusion
  84.7 1.0 %copy.10 = f32[2,2,256,256]{3,2,1,0:T(8,128)} copy(f32[2,2,256,256]{3,2,0,1:T(8,128)S(1)} %pad_maximum_fusion) | data formatting | bytes 2097152 | tf_op jit(solution)/shard_map/stack | solution.py:275
  (39 shorter events, 0.6 us)
Async XLA Ops:
  0.6 4.4 %copy-start.2 = (bf16[256,2048]{1,0:T(8,128)(2,1)S(1)}, bf16[256,2048]{1,0:T(8,128)(2,1)}, u32[]{:S(2)}) copy-start(bf16[256,2048]{1,0:T(8,128)(2,1)} %param.4) | copy-start | bytes 3145732
  1.9 4.6 %collective-permute-start = (bf16[256,256]{1,0:T(8,128)(2,1)S(1)}, bf16[256,256]{1,0:T(8,128)(2,1)S(1)}, u32[]{:S(2)}, u32[]{:S(2)}) collective-permute-start(bf16[256,256]{1,0:T(8,128)(2,1)S(1)} %get-tuple-element.70), channel_id=1, source_target_pairs={{0,2},{2,0},{4,6},{6,4},{8,10},{10,8},{12,14},{14,12},{16,18},{18,... | collective-permute-start | bytes 393224 | tf_op jit(solution)/shard_map/ppermute | solution.py:192
  2.4 9.9 %collective-permute-start.1 = (bf16[256,512]{1,0:T(8,128)(2,1)S(1)}, bf16[256,512]{1,0:T(8,128)(2,1)S(1)}, u32[]{:S(2)}, u32[]{:S(2)}) collective-permute-start(bf16[256,512]{1,0:T(8,128)(2,1)S(1)} %get-tuple-element.63), channel_id=1, source_target_pairs={{0,4},{2,6},{4,0},{6,2},{8,12},{10,14},{12,8},{14,10},{16,20},{18,... | collective-permute-start | bytes 786440 | tf_op jit(solution)/shard_map/ppermute | solution.py:192
  6.6 15.1 %collective-permute-start.4 = (bf16[2,256,256]{2,1,0:T(8,128)(2,1)S(1)}, bf16[2,256,256]{2,1,0:T(8,128)(2,1)S(1)}, u32[]{:S(2)}, u32[]{:S(2)}) collective-permute-start(bf16[2,256,256]{2,1,0:T(8,128)(2,1)S(1)} %pad_maximum_fusion.3), channel_id=1, source_target_pairs={{0,16},{2,18},{4,20},{6,22},{8,24},{10,26},{12,28},{14,30},{16,0},... | collective-permute-start | bytes 786440 | tf_op jit(solution)/shard_map/ppermute | solution.py:192
  9.3 12.6 %collective-permute-start.3 = (bf16[2,256,256]{2,1,0:T(8,128)(2,1)S(1)}, bf16[2,256,256]{2,1,0:T(8,128)(2,1)S(1)}, u32[]{:S(2)}, u32[]{:S(2)}) collective-permute-start(bf16[2,256,256]{2,1,0:T(8,128)(2,1)S(1)} %pad_maximum_fusion.3), channel_id=1, source_target_pairs={{0,8},{2,10},{4,12},{6,14},{8,0},{10,2},{12,4},{14,6},{16,24},{18,... | collective-permute-start | bytes 786440 | tf_op jit(solution)/shard_map/ppermute | solution.py:192
  10.8 24.7 %collective-permute-start.8 = (bf16[16,256,128]{2,1,0:T(8,128)(2,1)S(1)}, bf16[16,256,128]{2,1,0:T(8,128)(2,1)S(1)}, u32[]{:S(2)}, u32[]{:S(2)}) collective-permute-start(bf16[16,256,128]{2,1,0:T(8,128)(2,1)S(1)} %bitcast.58), channel_id=1, source_target_pairs={{0,1},{1,0},{2,3},{3,2},{4,5},{5,4},{6,7},{7,6},{8,9},{9,8},{10,11... | collective-permute-start | bytes 3145736 | tf_op jit(solution)/shard_map/ppermute | solution.py:201
  12.4 26.8 %collective-permute-start.10 = (bf16[16,256,128]{2,1,0:T(8,128)(2,1)S(1)}, bf16[16,256,128]{2,1,0:T(8,128)(2,1)S(1)}, u32[]{:S(2)}, u32[]{:S(2)}) collective-permute-start(bf16[16,256,128]{2,1,0:T(8,128)(2,1)S(1)} %bitcast.60), channel_id=1, source_target_pairs={{0,4},{2,6},{4,0},{6,2},{8,12},{10,14},{12,8},{14,10},{16,20},{18,... | collective-permute-start | bytes 3145736 | tf_op jit(solution)/shard_map/ppermute | solution.py:192
  21.9 1.9 %collective-permute-start.5 = (bf16[6,256,128]{2,1,0:T(8,128)(2,1)S(1)}, bf16[6,256,128]{2,1,0:T(8,128)(2,1)S(1)}, u32[]{:S(2)}, u32[]{:S(2)}) collective-permute-start(bf16[6,256,128]{2,1,0:T(8,128)(2,1)S(1)} %slice.120), channel_id=1, source_target_pairs={{0,2},{2,0},{4,6},{6,4},{8,10},{10,8},{12,14},{14,12},{16,18},{18,... | collective-permute-start | bytes 1179656 | tf_op jit(solution)/shard_map/ppermute | solution.py:192
  21.9 1.9 %collective-permute-start.2 = (bf16[256,256]{1,0:T(8,128)(2,1)S(1)}, bf16[256,256]{1,0:T(8,128)(2,1)S(1)}, u32[]{:S(2)}, u32[]{:S(2)}) collective-permute-start(bf16[256,256]{1,0:T(8,128)(2,1)S(1)} %get-tuple-element.72), channel_id=1, source_target_pairs={{0,2},{2,0},{4,6},{6,4},{8,10},{10,8},{12,14},{14,12},{16,18},{18,... | collective-permute-start | bytes 393224 | tf_op jit(solution)/shard_map/ppermute | solution.py:192
  23.8 15.4 %collective-permute-start.9 = (bf16[10,256,128]{2,1,0:T(8,128)(2,1)S(1)}, bf16[10,256,128]{2,1,0:T(8,128)(2,1)S(1)}, u32[]{:S(2)}, u32[]{:S(2)}) collective-permute-start(bf16[10,256,128]{2,1,0:T(8,128)(2,1)S(1)} %slice.119), channel_id=1, source_target_pairs={{0,2},{2,0},{4,6},{6,4},{8,10},{10,8},{12,14},{14,12},{16,18},{18,... | collective-permute-start | bytes 1966088 | tf_op jit(solution)/shard_map/ppermute | solution.py:192
  24.0 15.1 %collective-permute-start.7 = (bf16[2,256,256]{2,1,0:T(8,128)(2,1)S(1)}, bf16[2,256,256]{2,1,0:T(8,128)(2,1)S(1)}, u32[]{:S(2)}, u32[]{:S(2)}) collective-permute-start(bf16[2,256,256]{2,1,0:T(8,128)(2,1)S(1)} %pad_maximum_fusion.4), channel_id=1, source_target_pairs={{0,16},{2,18},{4,20},{6,22},{8,24},{10,26},{12,28},{14,30},{16,0},... | collective-permute-start | bytes 786440 | tf_op jit(solution)/shard_map/ppermute | solution.py:192
  25.4 13.8 %collective-permute-start.6 = (bf16[2,256,256]{2,1,0:T(8,128)(2,1)S(1)}, bf16[2,256,256]{2,1,0:T(8,128)(2,1)S(1)}, u32[]{:S(2)}, u32[]{:S(2)}) collective-permute-start(bf16[2,256,256]{2,1,0:T(8,128)(2,1)S(1)} %pad_maximum_fusion.4), channel_id=1, source_target_pairs={{0,8},{2,10},{4,12},{6,14},{8,0},{10,2},{12,4},{14,6},{16,24},{18,... | collective-permute-start | bytes 786440 | tf_op jit(solution)/shard_map/ppermute | solution.py:192
  39.3 4.2 %collective-permute-start.11 = (bf16[16,256,128]{2,1,0:T(8,128)(2,1)S(1)}, bf16[16,256,128]{2,1,0:T(8,128)(2,1)S(1)}, u32[]{:S(2)}, u32[]{:S(2)}) collective-permute-start(bf16[16,256,128]{2,1,0:T(8,128)(2,1)S(1)} %collective-permute-done.8.refs_6_.refs_7_), channel_id=1, source_target_pairs={{0,2},{2,0},{4,6},{6,4},{8,10},{10,8},{12,14},{14,12},{16,18},{18,... | collective-permute-start | bytes 3145736 | tf_op jit(solution)/shard_map/ppermute | solution.py:192
  39.3 18.7 %collective-permute-start.15 = (bf16[9,256,128]{2,1,0:T(8,128)(2,1)S(1)}, bf16[9,256,128]{2,1,0:T(8,128)(2,1)S(1)}, u32[]{:S(2)}, u32[]{:S(2)}) collective-permute-start(bf16[9,256,128]{2,1,0:T(8,128)(2,1)S(1)} %slice.121), channel_id=1, source_target_pairs={{0,1},{1,0},{2,3},{3,2},{4,5},{5,4},{6,7},{7,6},{8,9},{9,8},{10,11... | collective-permute-start | bytes 1769480 | tf_op jit(solution)/shard_map/ppermute | solution.py:201
  40.9 14.6 %collective-permute-start.12 = (bf16[4,256,256]{2,1,0:T(8,128)(2,1)S(1)}, bf16[4,256,256]{2,1,0:T(8,128)(2,1)S(1)}, u32[]{:S(2)}, u32[]{:S(2)}) collective-permute-start(bf16[4,256,256]{2,1,0:T(8,128)(2,1)S(1)} %pad_maximum_fusion.1.refs_2_.refs_1_), channel_id=1, source_target_pairs={{8,16},{10,18},{12,20},{14,22},{16,8},{18,10},{20,12},{22,14},{9,1... | collective-permute-start | bytes 1572872 | tf_op jit(solution)/shard_map/ppermute | solution.py:195
  41.6 16.5 %collective-permute-start.13 = (bf16[4,256,256]{2,1,0:T(8,128)(2,1)S(1)}, bf16[4,256,256]{2,1,0:T(8,128)(2,1)S(1)}, u32[]{:S(2)}, u32[]{:S(2)}) collective-permute-start(bf16[4,256,256]{2,1,0:T(8,128)(2,1)S(1)} %constant_dynamic-update-slice_fusion.2.refs_4_.refs_3_), channel_id=1, source_target_pairs={{8,0},{10,2},{12,4},{14,6},{16,24},{18,26},{20,28},{22,30},{9,1},{... | collective-permute-start | bytes 1572872 | tf_op jit(solution)/shard_map/ppermute | solution.py:198
  42.9 12.7 %collective-permute-start.14 = (bf16[7,256,128]{2,1,0:T(8,128)(2,1)S(1)}, bf16[7,256,128]{2,1,0:T(8,128)(2,1)S(1)}, u32[]{:S(2)}, u32[]{:S(2)}) collective-permute-start(bf16[7,256,128]{2,1,0:T(8,128)(2,1)S(1)} %slice.122), channel_id=1, source_target_pairs={{0,4},{2,6},{4,0},{6,2},{8,12},{10,14},{12,8},{14,10},{16,20},{18,... | collective-permute-start | bytes 1376264 | tf_op jit(solution)/shard_map/ppermute | solution.py:192
  43.5 17.2 %collective-permute-start.18 = (bf16[16,256,128]{2,1,0:T(8,128)(2,1)S(1)}, bf16[16,256,128]{2,1,0:T(8,128)(2,1)S(1)}, u32[]{:S(2)}, u32[]{:S(2)}) collective-permute-start(bf16[16,256,128]{2,1,0:T(8,128)(2,1)S(1)} %collective-permute-done.10.refs_10_), channel_id=1, source_target_pairs={{0,2},{2,0},{4,6},{6,4},{8,10},{10,8},{12,14},{14,12},{16,18},{18,... | collective-permute-start | bytes 3145736 | tf_op jit(solution)/shard_map/ppermute | solution.py:192
  43.5 0.7 copy-start
  58.0 2.7 %collective-permute-start.19 = (bf16[9,256,128]{2,1,0:T(8,128)(2,1)S(1)}, bf16[9,256,128]{2,1,0:T(8,128)(2,1)S(1)}, u32[]{:S(2)}, u32[]{:S(2)}) collective-permute-start(bf16[9,256,128]{2,1,0:T(8,128)(2,1)S(1)} %collective-permute-done.15.refs_11_), channel_id=1, source_target_pairs={{0,2},{2,0},{4,6},{6,4},{8,10},{10,8},{12,14},{14,12},{16,18},{18,... | collective-permute-start | bytes 1769480 | tf_op jit(solution)/shard_map/ppermute | solution.py:192
  58.1 2.7 %collective-permute-start.20 = (bf16[7,256,128]{2,1,0:T(8,128)(2,1)S(1)}, bf16[7,256,128]{2,1,0:T(8,128)(2,1)S(1)}, u32[]{:S(2)}, u32[]{:S(2)}) collective-permute-start(bf16[7,256,128]{2,1,0:T(8,128)(2,1)S(1)} %collective-permute-done.14.refs_12_), channel_id=1, source_target_pairs={{0,2},{2,0},{4,6},{6,4},{8,10},{10,8},{12,14},{14,12},{16,18},{18,... | collective-permute-start | bytes 1376264 | tf_op jit(solution)/shard_map/ppermute | solution.py:192
  62.4 5.8 %collective-permute-start.22 = (f16[272,256]{1,0:T(8,128)(2,1)S(1)}, f16[272,256]{1,0:T(8,128)(2,1)S(1)}, u32[]{:S(2)}, u32[]{:S(2)}) collective-permute-start(f16[272,256]{1,0:T(8,128)(2,1)S(1)} %convert_element_type.41), channel_id=1, source_target_pairs={{0,8},{2,10},{4,12},{6,14},{8,0},{10,2},{12,4},{14,6},{16,24},{18,... | collective-permute-start | bytes 417800 | tf_op jit(solution)/shard_map/ppermute | solution.py:192
  63.1 5.3 %collective-permute-start.17 = (bf16[256,256]{1,0:T(8,128)(2,1)S(1)}, bf16[256,256]{1,0:T(8,128)(2,1)S(1)}, u32[]{:S(2)}, u32[]{:S(2)}) collective-permute-start(bf16[256,256]{1,0:T(8,128)(2,1)S(1)} %get-tuple-element.64), channel_id=1, source_target_pairs={{0,4},{2,6},{4,0},{6,2},{8,12},{10,14},{12,8},{14,10},{16,20},{18,... | collective-permute-start | bytes 393224 | tf_op jit(solution)/shard_map/ppermute | solution.py:192
  63.6 4.8 %collective-permute-start.16 = (bf16[256,256]{1,0:T(8,128)(2,1)S(1)}, bf16[256,256]{1,0:T(8,128)(2,1)S(1)}, u32[]{:S(2)}, u32[]{:S(2)}) collective-permute-start(bf16[256,256]{1,0:T(8,128)(2,1)S(1)} %get-tuple-element.65), channel_id=1, source_target_pairs={{0,2},{2,0},{4,6},{6,4},{8,10},{10,8},{12,14},{14,12},{16,18},{18,... | collective-permute-start | bytes 393224 | tf_op jit(solution)/shard_map/ppermute | solution.py:192
  68.4 8.8 %collective-permute-start.23 = (f16[272,256]{1,0:T(8,128)(2,1)S(1)}, f16[272,256]{1,0:T(8,128)(2,1)S(1)}, u32[]{:S(2)}, u32[]{:S(2)}) collective-permute-start(f16[272,256]{1,0:T(8,128)(2,1)S(1)} %pad_maximum_fusion.5), channel_id=1, source_target_pairs={{0,16},{2,18},{4,20},{6,22},{8,24},{10,26},{12,28},{14,30},{16,0},... | collective-permute-start | bytes 417800 | tf_op jit(solution)/shard_map/ppermute | solution.py:192
  70.5 6.9 %collective-permute-start.21 = (bf16[256,256]{1,0:T(8,128)(2,1)S(1)}, bf16[256,256]{1,0:T(8,128)(2,1)S(1)}, u32[]{:S(2)}, u32[]{:S(2)}) collective-permute-start(bf16[256,256]{1,0:T(8,128)(2,1)S(1)} %bitcast.64), channel_id=1, source_target_pairs={{0,6},{2,4},{4,2},{6,0},{8,14},{10,12},{12,10},{14,8},{16,22},{18,... | collective-permute-start | bytes 393224 | tf_op jit(solution)/shard_map/ppermute | solution.py:192
  77.4 5.1 %collective-permute-start.24 = (f16[272,256]{1,0:T(8,128)(2,1)S(1)}, f16[272,256]{1,0:T(8,128)(2,1)S(1)}, u32[]{:S(2)}, u32[]{:S(2)}) collective-permute-start(f16[272,256]{1,0:T(8,128)(2,1)S(1)} %pad_maximum_fusion.6), channel_id=1, source_target_pairs={{0,4},{2,6},{4,0},{6,2},{8,12},{10,14},{12,8},{14,10},{16,20},{18,... | collective-permute-start | bytes 417800 | tf_op jit(solution)/shard_map/ppermute | solution.py:192
  79.4 5.1 %copy-start.1 = (f32[4,256,256]{2,1,0:T(8,128)S(1)}, f32[4,256,256]{2,1,0:T(8,128)}, u32[]{:S(2)}) copy-start(f32[4,256,256]{2,1,0:T(8,128)} %param.7) | copy-start | bytes 3145732
  82.7 1.6 %collective-permute-start.25 = (f16[2,272,256]{2,1,0:T(8,128)(2,1)S(1)}, f16[2,272,256]{2,1,0:T(8,128)(2,1)S(1)}, u32[]{:S(2)}, u32[]{:S(2)}) collective-permute-start(f16[2,272,256]{2,1,0:T(8,128)(2,1)S(1)} %pad_maximum_fusion.2), channel_id=1, source_target_pairs={{0,2},{2,0},{4,6},{6,4},{8,10},{10,8},{12,14},{14,12},{16,18},{18,... | collective-permute-start | bytes 835592 | tf_op jit(solution)/shard_map/ppermute | solution.py:192

commit v5 on v4

--- a/solution.py
+++ b/solution.py
@@ -211,22 +211,22 @@
     pair_rows = choose(own_rows, first_pair)
     part_a = jnp.stack([choose(pair_rows, first_core), swap(choose(pair_rows, ~first_core), 1)])
     inverse = anc_inverse.reshape(rows, half_w, all_blocks).transpose(2, 0, 1)
-    two_a, one_a = swap(after(part_a, inverse), 8), swap(after(part_a, inverse), 4)
+    two_a, one_a = swap(part_a, 8), swap(after(part_a, inverse), 4)
     give_b = choose(from_pair, ~first_core)
     part_b = jnp.stack([choose(from_pair, first_core), swap(give_b, 1)])
     x_all, y_all = across(inverse), swap(after(inverse, from_pair), 2)
     own = jnp.concatenate([part_a, part_b])
-    n_first = 6 * all_blocks // 16
+    n_first = 7 * all_blocks // 16
     c_first = swap(after(inverse[:n_first], two_a, one_a), 1)
     first = together((part_b, inverse[n_first:]), c_first)
     two_b, one_b, c_rest = swap(first[0], 8), swap(first[0], 4), swap(first[1], 1)
     c_own = jnp.concatenate([c_first, c_rest])
     two, one = jnp.concatenate([two_a, two_b]), jnp.concatenate([one_a, one_b])
-    n_low = 9 * all_blocks // 16
-    second = together((two, own, y_all[:n_low], x_all[n_low:], x_all, y_all), one, c_rest)
-    out, three = outward(second[0]), middle(second[1])
+    n_low = 7 * all_blocks // 16
+    second = together((x_all, y_all, y_all[:n_low], x_all[n_low:], two, own), c_rest, one)
+    out, three = outward(second[4]), middle(second[5])
     xy_low, xy_high = across(second[2]), swap(second[3], 2)
-    c_x, c_y = swap(second[4], 1), swap(second[5], 1)
+    c_x, c_y = swap(second[0], 1), swap(second[1], 1)
 
     def product(scalars, level, groups, sums=None, before=None, ends=True):
         packs = before is not None
@@ -248,10 +248,10 @@
     rows_0, rows_1 = (inverse, x_all), (c_own, c_x)
     first_groups = [(0, early, rows_0), (1, early, rows_1)]
     sums, kept = product((place, structure), [own, one, two], first_groups, ends=False)
-    last = together((three, out, xy_high, xy_low), sums)
-    cxy_low, cxy_high = swap(last[3], 1), swap(last[2], 1)
+    last = together((three, out, xy_low, xy_high), sums)
+    cxy_low, cxy_high = swap(last[2], 1), swap(last[3], 1)
     level = [own, one, two, last[0], last[1]]
-    groups = [(0, late, rows_0), (1, late, rows_1), (2, steps, (y_all, last[3], last[2]))]
+    groups = [(0, late, rows_0), (1, late, rows_1), (2, steps, (y_all, last[2], last[3]))]
     sel, diag = product((kept,), level, groups, sums=sums)
     s_core, s_pair = swap(sel[1], 1), swap(sel[2], 2)
     sel_cross, diag = product((kept,), level, [(3, steps, (c_y, cxy_low, cxy_high))], before=diag)

time: 86 us -> 84.9 us (0.987)
  waiting for transfers between devices: 48.2 us -> 45 us
  starting transfers between devices: 23.4 us -> 25.5 us
    ppermute x22, waiting for transfers between devices: 38.2 us -> 27.2 us  [swap(): return lax.ppermute(x, 'col', [(c, c ^ flip) for c in range(n_col)])]
    ppermute x2, waiting for transfers between devices: 7.54 us -> 15.6 us  [across(): return lax.ppermute(x, 'row', [(0, 1), (1, 0)])]
    ppermute x22, starting transfers between devices: 18.4 us -> 20.4 us  [swap(): return lax.ppermute(x, 'col', [(c, c ^ flip) for c in range(n_col)])]
  transfers between devices with their start and end apart: 26 -> 26, of which waited for: 12 -> 13; matrix products, arithmetic and copies ran while one was open for 3% -> 3% of each run, Pallas kernels for 7% -> 7%
where the time goes in v5:
time: 84.9 us; the launch traced here: 84.7 us
  waiting for transfers between devices  45 us (53%)
  starting transfers between devices  25.5 us (30%)
  Pallas kernels  7.43 us (9%)
  local copies, waits for them, and re-layouts  3.53 us (4%)
  other arithmetic  2.21 us (3%)
  between operations  1.03 us (1%)
    ppermute x22, waiting for transfers between devices, swap(): return lax.ppermute(x, 'col', [(c, c ^ flip) for c in range(n_col)])  27.2 us
    ppermute x22, starting transfers between devices, swap(): return lax.ppermute(x, 'col', [(c, c ^ flip) for c in range(n_col)])  20.4 us
    ppermute x2, waiting for transfers between devices, across(): return lax.ppermute(x, 'row', [(0, 1), (1, 0)])  15.6 us
    pallas_call x3, Pallas kernels, product(): pl.pallas_call(functools.partial(product_kernel, what, len(level), ends,...  6.03 us
    ppermute x2, starting transfers between devices, across(): return lax.ppermute(x, 'row', [(0, 1), (1, 0)])  3.1 us
    ppermute x1, waiting for transfers between devices, outward(): lax.ppermute(x, 'col', [(c, c ^ 4) for c in range(n_col) if c // 4 in (1,...  2.14 us
  transfers between devices with their start and end apart: 26, of which 13 were waited for; matrix products, arithmetic and copies ran while one was open for 3% of the time, Pallas kernels for 7%

profile of v5, /device:TPU:0, one launch (start us, length us, event | category | flops | bytes accessed | tf_op | source)
XLA Modules:
  0.0 84.7 jit_solution(392338014776438790)
XLA Ops:
  0.7 0.1 pad_add_fusion.refs_0_.place
  0.8 1.1 %broadcast_select_fusion.3 = (bf16[256,512]{1,0:T(8,128)(2,1)S(1)}, bf16[256,512]{1,0:T(8,128)(2,1)S(1)}) fusion(pred[]{:T(512)S(6)} %eq.10, bf16[256,1024]{1,0:T(8,128)(2,1)} %bitcast.68, pred[]{:T(512)S(6)} %not.8), kind=kLoop, calls=%fused_computation.16 | loop fusion | flops 262144 | bytes 1048578 | tf_op jit(solution)/shard_map/jit(_where)/select_n | solution.py:207
  1.9 0.5 collective-permute-start
  2.4 2.6 %collective-permute-start.1 = (bf16[256,512]{1,0:T(8,128)(2,1)S(1)}, bf16[256,512]{1,0:T(8,128)(2,1)S(1)}, u32[]{:S(2)}, u32[]{:S(2)}) collective-permute-start(bf16[256,512]{1,0:T(8,128)(2,1)S(1)} %get-tuple-element.63), channel_id=1, source_target_pairs={{0,4},{2,6},{4,0},{6,2},{8,12},{10,14},{12,8},{14,10},{16,20},{18,... | collective-permute-start | bytes 786440 | tf_op jit(solution)/shard_map/ppermute | solution.py:192
  5.0 0.5 copy.6
  5.6 1.0 %copy.7 = bf16[256,128,16]{1,0,2:T(8,128)(2,1)S(1)} copy(bf16[256,128,16]{0,2,1:T(8,128)(2,1)S(1)} %bitcast.65) | data formatting | bytes 2097152 | tf_op jit(solution)/shard_map/reshape | solution.py:213
  6.6 2.7 %collective-permute-start.4 = (bf16[2,256,256]{2,1,0:T(8,128)(2,1)S(1)}, bf16[2,256,256]{2,1,0:T(8,128)(2,1)S(1)}, u32[]{:S(2)}, u32[]{:S(2)}) collective-permute-start(bf16[2,256,256]{2,1,0:T(8,128)(2,1)S(1)} %pad_maximum_fusion.3), channel_id=1, source_target_pairs={{0,16},{2,18},{4,20},{6,22},{8,24},{10,26},{12,28},{14,30},{16,0},... | collective-permute-start | bytes 786440 | tf_op jit(solution)/shard_map/ppermute | solution.py:192
  9.3 1.6 %collective-permute-start.3 = (bf16[2,256,256]{2,1,0:T(8,128)(2,1)S(1)}, bf16[2,256,256]{2,1,0:T(8,128)(2,1)S(1)}, u32[]{:S(2)}, u32[]{:S(2)}) collective-permute-start(bf16[2,256,256]{2,1,0:T(8,128)(2,1)S(1)} %pad_maximum_fusion.3), channel_id=1, source_target_pairs={{0,8},{2,10},{4,12},{6,14},{8,0},{10,2},{12,4},{14,6},{16,24},{18,... | collective-permute-start | bytes 786440 | tf_op jit(solution)/shard_map/ppermute | solution.py:192
  10.8 1.5 %collective-permute-start.8 = (bf16[16,256,128]{2,1,0:T(8,128)(2,1)S(1)}, bf16[16,256,128]{2,1,0:T(8,128)(2,1)S(1)}, u32[]{:S(2)}, u32[]{:S(2)}) collective-permute-start(bf16[16,256,128]{2,1,0:T(8,128)(2,1)S(1)} %bitcast.58), channel_id=1, source_target_pairs={{0,1},{1,0},{2,3},{3,2},{4,5},{5,4},{6,7},{7,6},{8,9},{9,8},{10,11... | collective-permute-start | bytes 3145736 | tf_op jit(solution)/shard_map/ppermute | solution.py:201
  12.4 0.0 collective-permute-done.1
  12.4 1.3 %collective-permute-start.10 = (bf16[16,256,128]{2,1,0:T(8,128)(2,1)S(1)}, bf16[16,256,128]{2,1,0:T(8,128)(2,1)S(1)}, u32[]{:S(2)}, u32[]{:S(2)}) collective-permute-start(bf16[16,256,128]{2,1,0:T(8,128)(2,1)S(1)} %bitcast.60), channel_id=1, source_target_pairs={{0,4},{2,6},{4,0},{6,2},{8,12},{10,14},{12,8},{14,10},{16,20},{18,... | collective-permute-start | bytes 3145736 | tf_op jit(solution)/shard_map/ppermute | solution.py:192
  13.7 8.0 %collective-permute-done.4 = bf16[2,256,256]{2,1,0:T(8,128)(2,1)S(1)} collective-permute-done((bf16[2,256,256]{2,1,0:T(8,128)(2,1)S(1)}, bf16[2,256,256]{2,1,0:T(8,128)(2,1)S(1)}, u32[]{:S(2)}, u32[]{:S(2)}) %collective-permute-start.4) | collective-permute-done | bytes 262176 | tf_op jit(solution)/shard_map/ppermute | solution.py:192
  21.7 0.2 collective-permute-done.3
  21.9 0.6 collective-permute-start.2
  22.5 1.4 %collective-permute-done.2 = bf16[256,256]{1,0:T(8,128)(2,1)S(1)} collective-permute-done((bf16[256,256]{1,0:T(8,128)(2,1)S(1)}, bf16[256,256]{1,0:T(8,128)(2,1)S(1)}, u32[]{:S(2)}, u32[]{:S(2)}) %collective-permute-start.2) | collective-permute-done | bytes 131104 | tf_op jit(solution)/shard_map/ppermute | solution.py:192
  23.9 0.0 collective-permute-done.5
  23.9 1.4 %collective-permute-start.7 = (bf16[2,256,256]{2,1,0:T(8,128)(2,1)S(1)}, bf16[2,256,256]{2,1,0:T(8,128)(2,1)S(1)}, u32[]{:S(2)}, u32[]{:S(2)}) collective-permute-start(bf16[2,256,256]{2,1,0:T(8,128)(2,1)S(1)} %pad_maximum_fusion.4), channel_id=1, source_target_pairs={{0,16},{2,18},{4,20},{6,22},{8,24},{10,26},{12,28},{14,30},{16,0},... | collective-permute-start | bytes 786440 | tf_op jit(solution)/shard_map/ppermute | solution.py:192
  25.3 0.0 collective-permute-start.9
  25.3 2.5 %collective-permute-start.6 = (bf16[2,256,256]{2,1,0:T(8,128)(2,1)S(1)}, bf16[2,256,256]{2,1,0:T(8,128)(2,1)S(1)}, u32[]{:S(2)}, u32[]{:S(2)}) collective-permute-start(bf16[2,256,256]{2,1,0:T(8,128)(2,1)S(1)} %pad_maximum_fusion.4), channel_id=1, source_target_pairs={{0,8},{2,10},{4,12},{6,14},{8,0},{10,2},{12,4},{14,6},{16,24},{18,... | collective-permute-start | bytes 786440 | tf_op jit(solution)/shard_map/ppermute | solution.py:192
  27.8 0.1 pad_maximum_fusion.1.refs_2_.refs_1_
  27.9 7.6 %collective-permute-done.8.refs_6_.refs_7_ = bf16[16,256,128]{2,1,0:T(8,128)(2,1)S(1)} collective-permute-done((bf16[16,256,128]{2,1,0:T(8,128)(2,1)S(1)}, bf16[16,256,128]{2,1,0:T(8,128)(2,1)S(1)}, u32[]{:S(2)}, u32[]{:S(2)}) %collective-permute-start.8) | collective-permute-done | bytes 1048608 | tf_op jit(solution)/shard_map/ppermute | solution.py:201
  35.6 3.4 %collective-permute-done.7 = bf16[2,256,256]{2,1,0:T(8,128)(2,1)S(1)} collective-permute-done((bf16[2,256,256]{2,1,0:T(8,128)(2,1)S(1)}, bf16[2,256,256]{2,1,0:T(8,128)(2,1)S(1)}, u32[]{:S(2)}, u32[]{:S(2)}) %collective-permute-start.7) | collective-permute-done | bytes 262176 | tf_op jit(solution)/shard_map/ppermute | solution.py:192
  39.0 0.5 collective-permute-done.6
  39.5 0.0 collective-permute-done.10.refs_10_
  39.5 0.0 collective-permute-done.9
  39.5 0.1 collective-permute-start.11
  39.6 0.5 collective-permute-start.15
  40.1 0.7 collective-permute-start.12
  40.8 1.3 %collective-permute-start.13 = (bf16[4,256,256]{2,1,0:T(8,128)(2,1)S(1)}, bf16[4,256,256]{2,1,0:T(8,128)(2,1)S(1)}, u32[]{:S(2)}, u32[]{:S(2)}) collective-permute-start(bf16[4,256,256]{2,1,0:T(8,128)(2,1)S(1)} %constant_dynamic-update-slice_fusion.2.refs_4_.refs_3_), channel_id=1, source_target_pairs={{8,0},{10,2},{12,4},{14,6},{16,24},{18,26},{20,28},{22,30},{9,1},{... | collective-permute-start | bytes 1572872 | tf_op jit(solution)/shard_map/ppermute | solution.py:198
  42.1 1.6 %collective-permute-start.14 = (bf16[7,256,128]{2,1,0:T(8,128)(2,1)S(1)}, bf16[7,256,128]{2,1,0:T(8,128)(2,1)S(1)}, u32[]{:S(2)}, u32[]{:S(2)}) collective-permute-start(bf16[7,256,128]{2,1,0:T(8,128)(2,1)S(1)} %slice.121), channel_id=1, source_target_pairs={{0,1},{1,0},{2,3},{3,2},{4,5},{5,4},{6,7},{7,6},{8,9},{9,8},{10,11... | collective-permute-start | bytes 1376264 | tf_op jit(solution)/shard_map/ppermute | solution.py:201
  43.8 0.0 copy-start
  43.8 0.1 constant_dynamic-update-slice_fusion.4.refs_7_.refs_8_
  43.9 0.6 copy-done
  44.5 2.3 %shard_map.59 = (f32[2,256,256]{2,1,0:T(8,128)S(1)}, s32[18]{0:T(128)S(1)}) custom-call(s32[2]{0:T(128)S(1)} %pad_add_fusion.refs_0_.place, s32[8,12]{1,0:T(8,128)S(1)} %copy-done, bf16[4,256,256]{2,1,0:T(8,128)(2,1)S(1)} %pad_maximum_fusion.1.refs_2_.refs_1_, bf16[4,256,256]{2,1,0:T(8,128)(2,1)S(1)} %constant_dynamic-update-slice_fusion.refs_3_.refs_2_, ...), custom_call_target="tpu_custom_call" | custom-call | tf_op jit(solution)/shard_map/pallas_call | solution.py:239
  46.7 8.0 %collective-permute-done.14.refs_11_ = bf16[7,256,128]{2,1,0:T(8,128)(2,1)S(1)} collective-permute-done((bf16[7,256,128]{2,1,0:T(8,128)(2,1)S(1)}, bf16[7,256,128]{2,1,0:T(8,128)(2,1)S(1)}, u32[]{:S(2)}, u32[]{:S(2)}) %collective-permute-start.14) | collective-permute-done | bytes 458784 | tf_op jit(solution)/shard_map/ppermute | solution.py:201
  54.8 2.1 %collective-permute-done.13.refs_5_ = bf16[4,256,256]{2,1,0:T(8,128)(2,1)S(1)} collective-permute-done((bf16[4,256,256]{2,1,0:T(8,128)(2,1)S(1)}, bf16[4,256,256]{2,1,0:T(8,128)(2,1)S(1)}, u32[]{:S(2)}, u32[]{:S(2)}) %collective-permute-start.13) | collective-permute-done | bytes 524320 | tf_op jit(solution)/shard_map/ppermute | solution.py:198
  56.9 0.0 collective-permute-done.15.refs_12_
  56.9 0.0 collective-permute-start.20
  56.9 0.5 collective-permute-start.19
  57.4 2.1 %shard_map.60 = (bf16[3,256,256]{2,1,0:T(8,128)(2,1)S(1)}, f32[256,256]{1,0:T(8,128)S(1)}) custom-call(s32[18]{0:T(128)S(1)} %get-tuple-element.36.refs_0_, bf16[4,256,256]{2,1,0:T(8,128)(2,1)S(1)} %pad_maximum_fusion.1.refs_2_.refs_1_, bf16[4,256,256]{2,1,0:T(8,128)(2,1)S(1)} %constant_dynamic-update-slice_fusion.refs_3_.refs_2_, ...), custom_call_target="tpu_custom_call" | custom-call | tf_op jit(solution)/shard_map/pallas_call | solution.py:239
  59.5 0.0 collective-permute-done.18.refs_6_
  59.5 0.1 collective-permute-done.19.refs_7_
  59.6 1.7 %shard_map.61 = (bf16[1,256,256]{2,1,0:T(8,128)(2,1)S(1)}, f32[272,256]{1,0:T(8,128)S(1)}) custom-call(s32[18]{0:T(128)S(1)} %get-tuple-element.36.refs_0_, bf16[4,256,256]{2,1,0:T(8,128)(2,1)S(1)} %pad_maximum_fusion.1.refs_2_.refs_1_, bf16[4,256,256]{2,1,0:T(8,128)(2,1)S(1)} %constant_dynamic-update-slice_fusion.refs_3_.refs_2_, ...), custom_call_target="tpu_custom_call" | custom-call | tf_op jit(solution)/shard_map/pallas_call | solution.py:239
  61.3 0.6 collective-permute-start.22
  61.9 1.4 %collective-permute-start.17 = (bf16[256,256]{1,0:T(8,128)(2,1)S(1)}, bf16[256,256]{1,0:T(8,128)(2,1)S(1)}, u32[]{:S(2)}, u32[]{:S(2)}) collective-permute-start(bf16[256,256]{1,0:T(8,128)(2,1)S(1)} %get-tuple-element.64), channel_id=1, source_target_pairs={{0,4},{2,6},{4,0},{6,2},{8,12},{10,14},{12,8},{14,10},{16,20},{18,... | collective-permute-start | bytes 393224 | tf_op jit(solution)/shard_map/ppermute | solution.py:192
  63.4 0.0 collective-permute-start.16
  63.4 3.7 %collective-permute-done.22 = f16[272,256]{1,0:T(8,128)(2,1)S(1)} collective-permute-done((f16[272,256]{1,0:T(8,128)(2,1)S(1)}, f16[272,256]{1,0:T(8,128)(2,1)S(1)}, u32[]{:S(2)}, u32[]{:S(2)}) %collective-permute-start.22) | collective-permute-done | bytes 139296 | tf_op jit(solution)/shard_map/ppermute | solution.py:192
  67.1 0.1 multiply_convert_fusion.1
  67.3 0.0 collective-permute-done.16.core_ref
  67.3 2.6 %collective-permute-start.23 = (f16[272,256]{1,0:T(8,128)(2,1)S(1)}, f16[272,256]{1,0:T(8,128)(2,1)S(1)}, u32[]{:S(2)}, u32[]{:S(2)}) collective-permute-start(f16[272,256]{1,0:T(8,128)(2,1)S(1)} %pad_maximum_fusion.5), channel_id=1, source_target_pairs={{0,16},{2,18},{4,20},{6,22},{8,24},{10,26},{12,28},{14,30},{16,0},... | collective-permute-start | bytes 417800 | tf_op jit(solution)/shard_map/ppermute | solution.py:192
  69.9 0.0 collective-permute-start.21
  69.9 6.2 %collective-permute-done.23 = f16[272,256]{1,0:T(8,128)(2,1)S(1)} collective-permute-done((f16[272,256]{1,0:T(8,128)(2,1)S(1)}, f16[272,256]{1,0:T(8,128)(2,1)S(1)}, u32[]{:S(2)}, u32[]{:S(2)}) %collective-permute-start.23) | collective-permute-done | bytes 139296 | tf_op jit(solution)/shard_map/ppermute | solution.py:192
  76.1 0.1 multiply_convert_fusion
  76.3 1.5 %collective-permute-start.24 = (f16[272,256]{1,0:T(8,128)(2,1)S(1)}, f16[272,256]{1,0:T(8,128)(2,1)S(1)}, u32[]{:S(2)}, u32[]{:S(2)}) collective-permute-start(f16[272,256]{1,0:T(8,128)(2,1)S(1)} %pad_maximum_fusion.6), channel_id=1, source_target_pairs={{0,4},{2,6},{4,0},{6,2},{8,12},{10,14},{12,8},{14,10},{16,20},{18,... | collective-permute-start | bytes 417800 | tf_op jit(solution)/shard_map/ppermute | solution.py:192
  77.7 1.4 %shard_map.62 = bf16[256,1024]{1,0:T(8,128)(2,1)} custom-call(s32[2]{0:T(128)S(1)} %pad_add_fusion.refs_0_.place, bf16[256,256]{1,0:T(8,128)(2,1)S(1)} %get-tuple-element.66.own_ref, bf16[256,256]{1,0:T(8,128)(2,1)S(1)} %collective-permute-done.16.core_ref, bf16[256,256]{1,0:T(8,128)(2,1)S(1)} %collective-permute-done.17.pair_ref, ...), custom_call_target="tpu_custom_call" | custom-call | tf_op jit(solution)/shard_map/pallas_call | solution.py:263
  79.1 2.3 %collective-permute-done.24 = f16[272,256]{1,0:T(8,128)(2,1)S(1)} collective-permute-done((f16[272,256]{1,0:T(8,128)(2,1)S(1)}, f16[272,256]{1,0:T(8,128)(2,1)S(1)}, u32[]{:S(2)}, u32[]{:S(2)}) %collective-permute-start.24) | collective-permute-done | bytes 139296 | tf_op jit(solution)/shard_map/ppermute | solution.py:192
  81.4 0.1 select_bitcast_fusion.1
  81.5 0.1 pad_maximum_fusion.2
  81.6 0.1 collective-permute-start.25
  81.6 1.5 %collective-permute-done.25 = f16[2,272,256]{2,1,0:T(8,128)(2,1)S(1)} collective-permute-done((f16[2,272,256]{2,1,0:T(8,128)(2,1)S(1)}, f16[2,272,256]{2,1,0:T(8,128)(2,1)S(1)}, u32[]{:S(2)}, u32[]{:S(2)}) %collective-permute-start.25) | collective-permute-done | bytes 278560 | tf_op jit(solution)/shard_map/ppermute | solution.py:192
  83.2 0.2 broadcast_select_fusion.1
  83.4 0.1 fusion.3
  83.5 0.1 pad_maximum_fusion
  83.6 1.0 %copy.10 = f32[2,2,256,256]{3,2,1,0:T(8,128)} copy(f32[2,2,256,256]{3,2,0,1:T(8,128)S(1)} %pad_maximum_fusion) | data formatting | bytes 2097152 | tf_op jit(solution)/shard_map/stack | solution.py:275
  (39 shorter events, 0.6 us)
Async XLA Ops:
  0.6 4.4 %copy-start.2 = (bf16[256,2048]{1,0:T(8,128)(2,1)S(1)}, bf16[256,2048]{1,0:T(8,128)(2,1)}, u32[]{:S(2)}) copy-start(bf16[256,2048]{1,0:T(8,128)(2,1)} %param.4) | copy-start | bytes 3145732
  1.9 4.6 %collective-permute-start = (bf16[256,256]{1,0:T(8,128)(2,1)S(1)}, bf16[256,256]{1,0:T(8,128)(2,1)S(1)}, u32[]{:S(2)}, u32[]{:S(2)}) collective-permute-start(bf16[256,256]{1,0:T(8,128)(2,1)S(1)} %get-tuple-element.70), channel_id=1, source_target_pairs={{0,2},{2,0},{4,6},{6,4},{8,10},{10,8},{12,14},{14,12},{16,18},{18,... | collective-permute-start | bytes 393224 | tf_op jit(solution)/shard_map/ppermute | solution.py:192
  2.4 9.9 %collective-permute-start.1 = (bf16[256,512]{1,0:T(8,128)(2,1)S(1)}, bf16[256,512]{1,0:T(8,128)(2,1)S(1)}, u32[]{:S(2)}, u32[]{:S(2)}) collective-permute-start(bf16[256,512]{1,0:T(8,128)(2,1)S(1)} %get-tuple-element.63), channel_id=1, source_target_pairs={{0,4},{2,6},{4,0},{6,2},{8,12},{10,14},{12,8},{14,10},{16,20},{18,... | collective-permute-start | bytes 786440 | tf_op jit(solution)/shard_map/ppermute | solution.py:192
  6.6 15.1 %collective-permute-start.4 = (bf16[2,256,256]{2,1,0:T(8,128)(2,1)S(1)}, bf16[2,256,256]{2,1,0:T(8,128)(2,1)S(1)}, u32[]{:S(2)}, u32[]{:S(2)}) collective-permute-start(bf16[2,256,256]{2,1,0:T(8,128)(2,1)S(1)} %pad_maximum_fusion.3), channel_id=1, source_target_pairs={{0,16},{2,18},{4,20},{6,22},{8,24},{10,26},{12,28},{14,30},{16,0},... | collective-permute-start | bytes 786440 | tf_op jit(solution)/shard_map/ppermute | solution.py:192
  9.3 12.6 %collective-permute-start.3 = (bf16[2,256,256]{2,1,0:T(8,128)(2,1)S(1)}, bf16[2,256,256]{2,1,0:T(8,128)(2,1)S(1)}, u32[]{:S(2)}, u32[]{:S(2)}) collective-permute-start(bf16[2,256,256]{2,1,0:T(8,128)(2,1)S(1)} %pad_maximum_fusion.3), channel_id=1, source_target_pairs={{0,8},{2,10},{4,12},{6,14},{8,0},{10,2},{12,4},{14,6},{16,24},{18,... | collective-permute-start | bytes 786440 | tf_op jit(solution)/shard_map/ppermute | solution.py:192
  10.8 24.7 %collective-permute-start.8 = (bf16[16,256,128]{2,1,0:T(8,128)(2,1)S(1)}, bf16[16,256,128]{2,1,0:T(8,128)(2,1)S(1)}, u32[]{:S(2)}, u32[]{:S(2)}) collective-permute-start(bf16[16,256,128]{2,1,0:T(8,128)(2,1)S(1)} %bitcast.58), channel_id=1, source_target_pairs={{0,1},{1,0},{2,3},{3,2},{4,5},{5,4},{6,7},{7,6},{8,9},{9,8},{10,11... | collective-permute-start | bytes 3145736 | tf_op jit(solution)/shard_map/ppermute | solution.py:201
  12.4 27.1 %collective-permute-start.10 = (bf16[16,256,128]{2,1,0:T(8,128)(2,1)S(1)}, bf16[16,256,128]{2,1,0:T(8,128)(2,1)S(1)}, u32[]{:S(2)}, u32[]{:S(2)}) collective-permute-start(bf16[16,256,128]{2,1,0:T(8,128)(2,1)S(1)} %bitcast.60), channel_id=1, source_target_pairs={{0,4},{2,6},{4,0},{6,2},{8,12},{10,14},{12,8},{14,10},{16,20},{18,... | collective-permute-start | bytes 3145736 | tf_op jit(solution)/shard_map/ppermute | solution.py:192
  21.9 2.0 %collective-permute-start.5 = (bf16[7,256,128]{2,1,0:T(8,128)(2,1)S(1)}, bf16[7,256,128]{2,1,0:T(8,128)(2,1)S(1)}, u32[]{:S(2)}, u32[]{:S(2)}) collective-permute-start(bf16[7,256,128]{2,1,0:T(8,128)(2,1)S(1)} %slice.120), channel_id=1, source_target_pairs={{0,2},{2,0},{4,6},{6,4},{8,10},{10,8},{12,14},{14,12},{16,18},{18,... | collective-permute-start | bytes 1376264 | tf_op jit(solution)/shard_map/ppermute | solution.py:192
  21.9 2.0 %collective-permute-start.2 = (bf16[256,256]{1,0:T(8,128)(2,1)S(1)}, bf16[256,256]{1,0:T(8,128)(2,1)S(1)}, u32[]{:S(2)}, u32[]{:S(2)}) collective-permute-start(bf16[256,256]{1,0:T(8,128)(2,1)S(1)} %get-tuple-element.72), channel_id=1, source_target_pairs={{0,2},{2,0},{4,6},{6,4},{8,10},{10,8},{12,14},{14,12},{16,18},{18,... | collective-permute-start | bytes 393224 | tf_op jit(solution)/shard_map/ppermute | solution.py:192
  23.9 15.0 %collective-permute-start.7 = (bf16[2,256,256]{2,1,0:T(8,128)(2,1)S(1)}, bf16[2,256,256]{2,1,0:T(8,128)(2,1)S(1)}, u32[]{:S(2)}, u32[]{:S(2)}) collective-permute-start(bf16[2,256,256]{2,1,0:T(8,128)(2,1)S(1)} %pad_maximum_fusion.4), channel_id=1, source_target_pairs={{0,16},{2,18},{4,20},{6,22},{8,24},{10,26},{12,28},{14,30},{16,0},... | collective-permute-start | bytes 786440 | tf_op jit(solution)/shard_map/ppermute | solution.py:192
  25.3 14.2 %collective-permute-start.9 = (bf16[9,256,128]{2,1,0:T(8,128)(2,1)S(1)}, bf16[9,256,128]{2,1,0:T(8,128)(2,1)S(1)}, u32[]{:S(2)}, u32[]{:S(2)}) collective-permute-start(bf16[9,256,128]{2,1,0:T(8,128)(2,1)S(1)} %slice.119), channel_id=1, source_target_pairs={{0,2},{2,0},{4,6},{6,4},{8,10},{10,8},{12,14},{14,12},{16,18},{18,... | collective-permute-start | bytes 1769480 | tf_op jit(solution)/shard_map/ppermute | solution.py:192
  25.3 14.1 %collective-permute-start.6 = (bf16[2,256,256]{2,1,0:T(8,128)(2,1)S(1)}, bf16[2,256,256]{2,1,0:T(8,128)(2,1)S(1)}, u32[]{:S(2)}, u32[]{:S(2)}) collective-permute-start(bf16[2,256,256]{2,1,0:T(8,128)(2,1)S(1)} %pad_maximum_fusion.4), channel_id=1, source_target_pairs={{0,8},{2,10},{4,12},{6,14},{8,0},{10,2},{12,4},{14,6},{16,24},{18,... | collective-permute-start | bytes 786440 | tf_op jit(solution)/shard_map/ppermute | solution.py:192
  39.5 4.2 %collective-permute-start.11 = (bf16[16,256,128]{2,1,0:T(8,128)(2,1)S(1)}, bf16[16,256,128]{2,1,0:T(8,128)(2,1)S(1)}, u32[]{:S(2)}, u32[]{:S(2)}) collective-permute-start(bf16[16,256,128]{2,1,0:T(8,128)(2,1)S(1)} %collective-permute-done.8.refs_6_.refs_7_), channel_id=1, source_target_pairs={{0,2},{2,0},{4,6},{6,4},{8,10},{10,8},{12,14},{14,12},{16,18},{18,... | collective-permute-start | bytes 3145736 | tf_op jit(solution)/shard_map/ppermute | solution.py:192
  39.6 17.3 %collective-permute-start.15 = (bf16[9,256,128]{2,1,0:T(8,128)(2,1)S(1)}, bf16[9,256,128]{2,1,0:T(8,128)(2,1)S(1)}, u32[]{:S(2)}, u32[]{:S(2)}) collective-permute-start(bf16[9,256,128]{2,1,0:T(8,128)(2,1)S(1)} %slice.122), channel_id=1, source_target_pairs={{0,4},{2,6},{4,0},{6,2},{8,12},{10,14},{12,8},{14,10},{16,20},{18,... | collective-permute-start | bytes 1769480 | tf_op jit(solution)/shard_map/ppermute | solution.py:192
  40.1 14.6 %collective-permute-start.12 = (bf16[4,256,256]{2,1,0:T(8,128)(2,1)S(1)}, bf16[4,256,256]{2,1,0:T(8,128)(2,1)S(1)}, u32[]{:S(2)}, u32[]{:S(2)}) collective-permute-start(bf16[4,256,256]{2,1,0:T(8,128)(2,1)S(1)} %pad_maximum_fusion.1.refs_2_.refs_1_), channel_id=1, source_target_pairs={{8,16},{10,18},{12,20},{14,22},{16,8},{18,10},{20,12},{22,14},{9,1... | collective-permute-start | bytes 1572872 | tf_op jit(solution)/shard_map/ppermute | solution.py:195
  40.8 16.1 %collective-permute-start.13 = (bf16[4,256,256]{2,1,0:T(8,128)(2,1)S(1)}, bf16[4,256,256]{2,1,0:T(8,128)(2,1)S(1)}, u32[]{:S(2)}, u32[]{:S(2)}) collective-permute-start(bf16[4,256,256]{2,1,0:T(8,128)(2,1)S(1)} %constant_dynamic-update-slice_fusion.2.refs_4_.refs_3_), channel_id=1, source_target_pairs={{8,0},{10,2},{12,4},{14,6},{16,24},{18,26},{20,28},{22,30},{9,1},{... | collective-permute-start | bytes 1572872 | tf_op jit(solution)/shard_map/ppermute | solution.py:198
  42.1 12.7 %collective-permute-start.14 = (bf16[7,256,128]{2,1,0:T(8,128)(2,1)S(1)}, bf16[7,256,128]{2,1,0:T(8,128)(2,1)S(1)}, u32[]{:S(2)}, u32[]{:S(2)}) collective-permute-start(bf16[7,256,128]{2,1,0:T(8,128)(2,1)S(1)} %slice.121), channel_id=1, source_target_pairs={{0,1},{1,0},{2,3},{3,2},{4,5},{5,4},{6,7},{7,6},{8,9},{9,8},{10,11... | collective-permute-start | bytes 1376264 | tf_op jit(solution)/shard_map/ppermute | solution.py:201
  43.7 15.8 %collective-permute-start.18 = (bf16[16,256,128]{2,1,0:T(8,128)(2,1)S(1)}, bf16[16,256,128]{2,1,0:T(8,128)(2,1)S(1)}, u32[]{:S(2)}, u32[]{:S(2)}) collective-permute-start(bf16[16,256,128]{2,1,0:T(8,128)(2,1)S(1)} %collective-permute-done.10.refs_10_), channel_id=1, source_target_pairs={{0,2},{2,0},{4,6},{6,4},{8,10},{10,8},{12,14},{14,12},{16,18},{18,... | collective-permute-start | bytes 3145736 | tf_op jit(solution)/shard_map/ppermute | solution.py:192
  43.8 0.7 copy-start
  56.9 2.7 %collective-permute-start.20 = (bf16[9,256,128]{2,1,0:T(8,128)(2,1)S(1)}, bf16[9,256,128]{2,1,0:T(8,128)(2,1)S(1)}, u32[]{:S(2)}, u32[]{:S(2)}) collective-permute-start(bf16[9,256,128]{2,1,0:T(8,128)(2,1)S(1)} %collective-permute-done.15.refs_12_), channel_id=1, source_target_pairs={{0,2},{2,0},{4,6},{6,4},{8,10},{10,8},{12,14},{14,12},{16,18},{18,... | collective-permute-start | bytes 1769480 | tf_op jit(solution)/shard_map/ppermute | solution.py:192
  56.9 2.7 %collective-permute-start.19 = (bf16[7,256,128]{2,1,0:T(8,128)(2,1)S(1)}, bf16[7,256,128]{2,1,0:T(8,128)(2,1)S(1)}, u32[]{:S(2)}, u32[]{:S(2)}) collective-permute-start(bf16[7,256,128]{2,1,0:T(8,128)(2,1)S(1)} %collective-permute-done.14.refs_11_), channel_id=1, source_target_pairs={{0,2},{2,0},{4,6},{6,4},{8,10},{10,8},{12,14},{14,12},{16,18},{18,... | collective-permute-start | bytes 1376264 | tf_op jit(solution)/shard_map/ppermute | solution.py:192
  61.3 5.8 %collective-permute-start.22 = (f16[272,256]{1,0:T(8,128)(2,1)S(1)}, f16[272,256]{1,0:T(8,128)(2,1)S(1)}, u32[]{:S(2)}, u32[]{:S(2)}) collective-permute-start(f16[272,256]{1,0:T(8,128)(2,1)S(1)} %convert_element_type.41), channel_id=1, source_target_pairs={{0,8},{2,10},{4,12},{6,14},{8,0},{10,2},{12,4},{14,6},{16,24},{18,... | collective-permute-start | bytes 417800 | tf_op jit(solution)/shard_map/ppermute | solution.py:192
  61.9 5.3 %collective-permute-start.17 = (bf16[256,256]{1,0:T(8,128)(2,1)S(1)}, bf16[256,256]{1,0:T(8,128)(2,1)S(1)}, u32[]{:S(2)}, u32[]{:S(2)}) collective-permute-start(bf16[256,256]{1,0:T(8,128)(2,1)S(1)} %get-tuple-element.64), channel_id=1, source_target_pairs={{0,4},{2,6},{4,0},{6,2},{8,12},{10,14},{12,8},{14,10},{16,20},{18,... | collective-permute-start | bytes 393224 | tf_op jit(solution)/shard_map/ppermute | solution.py:192
  63.4 3.9 %collective-permute-start.16 = (bf16[256,256]{1,0:T(8,128)(2,1)S(1)}, bf16[256,256]{1,0:T(8,128)(2,1)S(1)}, u32[]{:S(2)}, u32[]{:S(2)}) collective-permute-start(bf16[256,256]{1,0:T(8,128)(2,1)S(1)} %get-tuple-element.65), channel_id=1, source_target_pairs={{0,2},{2,0},{4,6},{6,4},{8,10},{10,8},{12,14},{14,12},{16,18},{18,... | collective-permute-start | bytes 393224 | tf_op jit(solution)/shard_map/ppermute | solution.py:192
  67.3 8.8 %collective-permute-start.23 = (f16[272,256]{1,0:T(8,128)(2,1)S(1)}, f16[272,256]{1,0:T(8,128)(2,1)S(1)}, u32[]{:S(2)}, u32[]{:S(2)}) collective-permute-start(f16[272,256]{1,0:T(8,128)(2,1)S(1)} %pad_maximum_fusion.5), channel_id=1, source_target_pairs={{0,16},{2,18},{4,20},{6,22},{8,24},{10,26},{12,28},{14,30},{16,0},... | collective-permute-start | bytes 417800 | tf_op jit(solution)/shard_map/ppermute | solution.py:192
  69.9 6.4 %collective-permute-start.21 = (bf16[256,256]{1,0:T(8,128)(2,1)S(1)}, bf16[256,256]{1,0:T(8,128)(2,1)S(1)}, u32[]{:S(2)}, u32[]{:S(2)}) collective-permute-start(bf16[256,256]{1,0:T(8,128)(2,1)S(1)} %bitcast.64), channel_id=1, source_target_pairs={{0,6},{2,4},{4,2},{6,0},{8,14},{10,12},{12,10},{14,8},{16,22},{18,... | collective-permute-start | bytes 393224 | tf_op jit(solution)/shard_map/ppermute | solution.py:192
  76.3 5.1 %collective-permute-start.24 = (f16[272,256]{1,0:T(8,128)(2,1)S(1)}, f16[272,256]{1,0:T(8,128)(2,1)S(1)}, u32[]{:S(2)}, u32[]{:S(2)}) collective-permute-start(f16[272,256]{1,0:T(8,128)(2,1)S(1)} %pad_maximum_fusion.6), channel_id=1, source_target_pairs={{0,4},{2,6},{4,0},{6,2},{8,12},{10,14},{12,8},{14,10},{16,20},{18,... | collective-permute-start | bytes 417800 | tf_op jit(solution)/shard_map/ppermute | solution.py:192
  79.1 4.3 %copy-start.1 = (f32[4,256,256]{2,1,0:T(8,128)S(1)}, f32[4,256,256]{2,1,0:T(8,128)}, u32[]{:S(2)}) copy-start(f32[4,256,256]{2,1,0:T(8,128)} %param.7) | copy-start | bytes 3145732
  81.6 1.6 %collective-permute-start.25 = (f16[2,272,256]{2,1,0:T(8,128)(2,1)S(1)}, f16[2,272,256]{2,1,0:T(8,128)(2,1)S(1)}, u32[]{:S(2)}, u32[]{:S(2)}) collective-permute-start(f16[2,272,256]{2,1,0:T(8,128)(2,1)S(1)} %pad_maximum_fusion.2), channel_id=1, source_target_pairs={{0,2},{2,0},{4,6},{6,4},{8,10},{10,8},{12,14},{14,12},{16,18},{18,... | collective-permute-start | bytes 835592 | tf_op jit(solution)/shard_map/ppermute | solution.py:192
